TPU v7x, 32 devices: a whole 2x2x4 slice. The times are simulated.
32 devices in a mesh: fsdp: 4 (over y, x), ctx: 4 (over z), tp: 2 (over core).
Axes of the slice: x: 2, y: 2, z: 4, core: 2. Of those that a mesh axis runs over, the one named last changes fastest.
Arguments:
- hidden: bfloat16 [4, 2048, 1024], P('fsdp', 'ctx'), may hold values from -6 to 6
- teacher: bfloat16 [4, 2048, 1024], P('fsdp', 'ctx'), may hold values from -6 to 6
- positions: int32 [4, 2048], P('fsdp', 'ctx'), may hold values from 0 to 2047, as said below
- valid_mask: int32 [4, 2048], P('fsdp', 'ctx'), may hold values from 0 to 1, as said below
- norm_gain: bfloat16 [1024], P(('fsdp', 'ctx')), may hold values from 0.5 to 1.5
- w_query: bfloat16 [1024, 512], P(('fsdp', 'ctx'), 'tp'), may hold values from -0.1875 to 0.1875
- key_value_weight: bfloat16 [1024, 2, 128], P(('fsdp', 'ctx'), None, 'tp'), may hold values from -0.1875 to 0.1875
- w_gatein: bfloat16 [1024, 2, 1536], P(('fsdp', 'ctx'), None, 'tp'), may hold values from -0.1875 to 0.1875
- w_bc: bfloat16 [1024, 256], P(('fsdp', 'ctx')), may hold values from -0.1875 to 0.1875
- w_step: bfloat16 [1024, 24], P(('fsdp', 'ctx'), 'tp'), may hold values from -0.1875 to 0.1875
- ssm_gain: bfloat16 [1536], P(('tp', 'fsdp', 'ctx')), may hold values from 0.5 to 1.5
- mlp_gain: bfloat16 [1024], P(('fsdp', 'ctx')), may hold values from 0.5 to 1.5
- w_gateup: bfloat16 [1024, 2, 2048], P(('fsdp', 'ctx'), None, 'tp'), may hold values from -0.1875 to 0.1875
- w_out_attn: bfloat16 [512, 1024], P('tp', ('fsdp', 'ctx')), may hold values from -1 to 1
- w_out_ssm: bfloat16 [1536, 1024], P('tp', ('fsdp', 'ctx')), may hold values from -0.15625 to 0.15625
- w_down: bfloat16 [2048, 1024], P('tp', ('fsdp', 'ctx')), may hold values from -0.125 to 0.125
- conv_inner: bfloat16 [4, 1536], P(None, ('tp', 'fsdp', 'ctx')), may hold values from -3 to 3
- conv_bc: bfloat16 [4, 256], P(None, ('fsdp', 'ctx')), may hold values from -3 to 3
- head_params: float32 [3, 24], P(None, 'tp'), may hold values from -5.3 to 1.5, as said below
Outputs:
- out: bfloat16 [4, 2048, 1024], P('fsdp', 'ctx')
- loss: float32 [], replicated
- grad_hidden: float32 [4, 2048, 1024], P('fsdp', 'ctx')
- grad_norm_gain: float32 [1024], P(('fsdp', 'ctx'))
- grad_w_query: float32 [1024, 512], P(('fsdp', 'ctx'), 'tp')
- grad_w_keyval: float32 [1024, 2, 128], P(('fsdp', 'ctx'), None, 'tp')
- grad_w_gatein: float32 [1024, 2, 1536], P(('fsdp', 'ctx'), None, 'tp')
- grad_w_bc: float32 [1024, 256], P(('fsdp', 'ctx'))
- grad_w_step: float32 [1024, 24], P(('fsdp', 'ctx'), 'tp')
- grad_ssm_gain: float32 [1536], P(('tp', 'fsdp', 'ctx'))
- grad_mlp_gain: float32 [1024], P(('fsdp', 'ctx'))
- grad_w_gateup: float32 [1024, 2, 2048], P(('fsdp', 'ctx'), None, 'tp')
- grad_w_out_attn: float32 [512, 1024], P('tp', ('fsdp', 'ctx'))
- grad_w_out_ssm: float32 [1536, 1024], P('tp', ('fsdp', 'ctx'))
- grad_w_down: float32 [2048, 1024], P('tp', ('fsdp', 'ctx'))
- grad_conv_inner: float32 [4, 1536], P(None, ('tp', 'fsdp', 'ctx'))
- grad_conv_bc: float32 [4, 256], P(None, ('fsdp', 'ctx'))
- grad_head_params: float32 [3, 24], P(None, 'tp')
Inputs may be any that keep to these rules, and one draw needn't show every extreme that they name: `positions`: each row is a run of documents, padding (if any) being its last one; a position is a token's offset in its document, 0 at a document's first token and one more than the token before elsewhere; row 0 is one document of 2048 tokens. `valid_mask`: 1 before a row's padding and 0 on it; row 0 has no padding, the last row has some. `head_params`: row 0 holds a head's step bias, row 1 the logarithm of its decay rate, row 2 its skip weight.
All inputs are finite; a program needn't handle non-finite values.
Results may differ from a plain program's by a relative error of at most 0.012.
Values may be sent and summed in bfloat16 or wider, within the bound.
No kernel may reach another device: no remote copies, remote signals or barrier semaphores. Data moves between devices by JAX's collectives and lax.ppermute only.
A program may use at most 192 MiB of HBM per device.

v0:
```python
import functools

import jax
import jax.numpy as jnp
from jax import lax
from jax.experimental import pallas as pl
from jax.experimental.pallas import tpu as pltpu
from jax.sharding import PartitionSpec as P

MODEL_WIDTH = 1024
HEAD_SIZE = 64
HS = 24
DS = 128
KC = 4

eps = 1e-05
rope_base = 100000000000.0
masked_score = -1e30
f32 = jnp.float32
bf16 = jnp.bfloat16
CHUNK = 128
HALO = 128
VMEM_LIMIT = 40 * 2**20


def dot(left, right, left_dim, right_dim, precision=None):
    return lax.dot_general(
        left, right, (((left_dim,), (right_dim,)), ((), ())), precision=precision, preferred_element_type=f32
    )


def exact(left, right, left_dim, right_dim):
    return dot(left, right, left_dim, right_dim, lax.Precision.HIGHEST)


def low(value):
    return value.astype(bf16)


def factors():
    fsdp = lax.axis_size("fsdp")
    side = int(round(fsdp**0.5))
    if side * side != fsdp:
        side = 1
    return (
        ("fsdp", fsdp // side, side),
        ("fsdp", side, 1),
        ("ctx", lax.axis_size("ctx"), 1),
    )


def coordinate(dim):
    axis, size, stride = dim
    return lax.rem(lax.axis_index(axis) // stride, size)


def shifted(value, dim, step):
    axis, size, stride = dim
    pairs = []
    for source in range(lax.axis_size(axis)):
        at = source // stride % size
        pairs.append((source, source + ((at + step) % size - at) * stride))
    return lax.ppermute(value, axis, pairs)


def passed_along(value, axis, steps):
    count = lax.axis_size(axis)
    pairs = [(s, s + steps) for s in range(count) if 0 <= s + steps < count]
    return lax.ppermute(value, axis, pairs)


def swapped(value):
    return lax.ppermute(value, "tp", [(0, 1), (1, 0)])


def gathered_along(value, dim):
    size = dim[1]
    if size == 1:
        return value[None]
    at = coordinate(dim)
    if size == 2:
        other = shifted(value, dim, 1)
        return jnp.where(at == 0, jnp.stack([value, other]), jnp.stack([other, value]))
    pieces = [value] + [shifted(value, dim, s) for s in range(1, size)]
    ring = jnp.stack((pieces[::-1]) * 2)
    return lax.dynamic_slice_in_dim(ring, size - 1 - at, size, 0)


def tied(*values):
    return lax.optimization_barrier(values)


def gathered_line(shard, doubling=True):
    zdim = factors()[2]
    size = zdim[1]
    if not doubling or size & (size - 1):
        return gathered_along(shard, zdim)
    at = coordinate(zdim)
    value = shard[None]
    step = 1
    while step < size:
        other = lax.ppermute(value, zdim[0], [(i, i ^ step) for i in range(size)])
        pair = (jnp.concatenate([value, other]), jnp.concatenate([other, value]))
        value = jnp.where(at // step % 2 == 0, *pair)
        step *= 2
    return value


def gathered_plane(line):
    ydim, xdim, _ = factors()
    columns = line.shape[-1]
    half = columns // 256 * 128
    one = gathered_along(line[..., :half], ydim)
    two = gathered_along(line[..., half:], xdim)
    one = jnp.swapaxes(gathered_along(one, xdim), 0, 1)
    two = gathered_along(two, ydim)
    return jnp.concatenate([one, two], axis=-1).reshape(-1, columns)


def in_pair(value, kept):
    body, tail = value[..., :-128], value[..., -128:]
    whole = tail + jnp.roll(tail, 64, axis=-1)
    high = lax.reduce_precision(whole, 8, 7)
    rest = (whole - high).astype(bf16)
    high = high.astype(bf16)
    column = lax.broadcasted_iota(jnp.int32, tail.shape, tail.ndim - 1)
    tail = jnp.where(column < kept, tail.astype(bf16), jnp.where(column < 64, high, rest))
    return jnp.concatenate([body.astype(bf16), tail], axis=-1)


def reduced_along(value, dim, front, kept=None):
    size = dim[1]
    if size == 1:
        return lax.index_in_dim(value, 0, front, False)
    at = coordinate(dim)
    total = lax.dynamic_index_in_dim(value, at, front, False).astype(f32)
    for step in range(1, size):
        piece = lax.dynamic_index_in_dim(value, lax.rem(at + step, size), front, False)
        total = total + shifted(piece, dim, step).astype(f32)
    return total.astype(bf16) if kept is None else in_pair(total, kept)


def scatter_first(partial, kept=None):
    ydim, xdim, zdim = factors()
    columns = partial.shape[1]
    blocks = partial.reshape(ydim[1], xdim[1], zdim[1], -1, columns)
    half = columns // 256 * 128
    return reduced_along(blocks[..., :half], xdim, 1), reduced_along(blocks[..., half:], ydim, 0, kept)


def scatter_second(parts, kept=None):
    ydim, xdim, _ = factors()
    return reduced_along(parts[0], ydim, 0), reduced_along(parts[1], xdim, 0, kept)


def exchanged(blocks, step):
    zdim = factors()[2]
    upper = coordinate(zdim) // step % 2 == 1
    halves = blocks.reshape(2, step, *blocks.shape[1:])
    kept = jnp.where(upper, halves[1], halves[0])
    sent = jnp.where(upper, halves[0], halves[1])
    return kept, lax.ppermute(sent, zdim[0], [(i, i ^ step) for i in range(zdim[1])])


def halved(parts):
    blocks = jnp.concatenate(parts, axis=-1)
    return exchanged(blocks, blocks.shape[0] // 2)


def halved_on(kept, other):
    while True:
        total = kept.astype(f32) + other.astype(f32)
        if total.shape[0] == 1:
            return total[0]
        kept, other = exchanged(total.astype(bf16), total.shape[0] // 2)


def scatter_third(parts):
    zdim = factors()[2]
    blocks = jnp.concatenate(parts, axis=-1)
    at = coordinate(zdim)
    total = lax.dynamic_index_in_dim(blocks, at, 0, False).astype(f32)
    for step in range(1, zdim[1]):
        piece = lax.dynamic_index_in_dim(blocks, lax.rem(at + step, zdim[1]), 0, False)
        total = total + shifted(piece, zdim, step).astype(f32)
    return total


def call(body, outs, scratch, *args):
    return pl.pallas_call(
        body,
        out_shape=[jax.ShapeDtypeStruct(s, d) for s, d in outs],
        in_specs=[pl.BlockSpec(memory_space=pltpu.VMEM)] * len(args),
        out_specs=[pl.BlockSpec(memory_space=pltpu.VMEM)] * len(outs),
        scratch_shapes=[pltpu.VMEM(s, d) for s, d in scratch],
        compiler_params=pltpu.CompilerParams(vmem_limit_bytes=VMEM_LIMIT),
        cost_estimate=pl.CostEstimate(flops=1000, bytes_accessed=1000, transcendentals=0),
    )(*args)


def rotated(block, cosine, sine):
    half = block.shape[0] // 2
    one, two = block[:half], block[half:]
    return jnp.concatenate([one * cosine - two * sine, two * cosine + one * sine], axis=0)


def flipped(block):
    return jnp.transpose(block.astype(f32)).astype(block.dtype)


def block_scores(keys, query, low, at, back, width):
    scores = dot(keys, query, 1, 0)
    place = lax.broadcasted_iota(jnp.int32, scores.shape, 0) - back
    allowed = place >= low
    if back == 0:
        token = at + lax.broadcasted_iota(jnp.int32, scores.shape, 1)
        allowed = allowed & (place <= token)
    return jnp.where(allowed, scores, masked_score)


def attend_body(blocks, heads, q_ref, low_ref, *refs):
    kv = refs[:blocks]
    out_ref, log_ref, key_ref, score_ref = refs[blocks:]
    length = q_ref.shape[1]
    width = min(256, length)
    for j in range(blocks):
        key_ref[j] = flipped(kv[j][:HEAD_SIZE, :])

    @pl.loop(0, heads)
    def _(h):
        rows = pl.ds(pl.multiple_of(h * HEAD_SIZE, HEAD_SIZE), HEAD_SIZE)
        for at in range(0, length, width):
            lanes = slice(at, at + width)
            query = q_ref[rows, lanes]
            low = low_ref[0:1, lanes]
            top = jnp.full((1, width), masked_score, f32)
            for j in range(blocks):
                scores = block_scores(key_ref[j], query, low, at, j * length, width)
                score_ref[j] = scores
                top = jnp.maximum(top, jnp.max(scores, axis=0, keepdims=True))
            total = jnp.zeros((1, width), f32)
            mixed = jnp.zeros((HEAD_SIZE, width), f32)
            for j in range(blocks):
                weight = jnp.exp(score_ref[j] - top)
                total = total + jnp.sum(weight, axis=0, keepdims=True)
                mixed = mixed + dot(kv[j][HEAD_SIZE:, :], weight.astype(bf16), 1, 0)
            out_ref[rows, lanes] = (mixed / total).astype(bf16)
            log_ref[h, :, lanes] = jnp.broadcast_to(top + jnp.log(total), (8, width))


def attend(query, low, kv):
    heads, length = query.shape[0] // HEAD_SIZE, query.shape[1]
    width = min(256, length)
    return call(
        functools.partial(attend_body, len(kv), heads),
        [(query.shape, bf16), ((heads, 8, length), f32)],
        [((len(kv), length, HEAD_SIZE), bf16), ((len(kv), length, width), f32)],
        query, low, *kv,
    )


def attend_back_body(blocks, heads, q_ref, low_ref, out_ref, log_ref, g_ref, cos_ref, sin_ref, *refs):
    kv = refs[:blocks]
    gq_ref = refs[blocks]
    gkv = refs[blocks + 1 : 2 * blocks + 1]
    key_ref, value_ref, sum_ref = refs[2 * blocks + 1 :]
    length = q_ref.shape[1]
    width = min(256, length)
    for j in range(blocks):
        key_ref[j] = flipped(kv[j][:HEAD_SIZE, :])
        value_ref[j] = flipped(kv[j][HEAD_SIZE:, :])
    sum_ref[...] = jnp.zeros_like(sum_ref)

    @pl.loop(0, heads)
    def _(h):
        rows = pl.ds(pl.multiple_of(h * HEAD_SIZE, HEAD_SIZE), HEAD_SIZE)
        for at in range(0, length, width):
            lanes = slice(at, at + width)
            query = q_ref[rows, lanes]
            grad = g_ref[rows, lanes]
            low = low_ref[0:1, lanes]
            log_total = log_ref[h, 0:1, lanes]
            inner = jnp.sum(grad.astype(f32) * out_ref[rows, lanes].astype(f32), axis=0, keepdims=True)
            gq = jnp.zeros((HEAD_SIZE, width), f32)
            for j in range(blocks):
                scores = block_scores(key_ref[j], query, low, at, j * length, width)
                probs = jnp.exp(scores - log_total)
                grad_probs = dot(value_ref[j], grad, 1, 0)
                grad_scores = (probs * (grad_probs - inner)).astype(bf16)
                gq = gq + dot(kv[j][:HEAD_SIZE, :], grad_scores, 1, 0)
                sum_ref[j, :HEAD_SIZE, :] += dot(query, grad_scores, 1, 1)
                sum_ref[j, HEAD_SIZE:, :] += dot(grad, probs.astype(bf16), 1, 1)
            gq = rotated(gq * HEAD_SIZE**-0.5, cos_ref[:, lanes], -sin_ref[:, lanes])
            gq_ref[rows, lanes] = gq.astype(bf16)

    for j in range(blocks):
        gkv[j][...] = sum_ref[j].astype(gkv[j].dtype)


def attend_back(query, low, out, log_total, grad, cosine, sine, kv):
    heads, length = query.shape[0] // HEAD_SIZE, query.shape[1]
    blocks = len(kv)
    return call(
        functools.partial(attend_back_body, blocks, heads),
        [(query.shape, bf16)] + [((2 * HEAD_SIZE, length), bf16)] * blocks,
        [((blocks, length, HEAD_SIZE), bf16)] * 2 + [((blocks, 2 * HEAD_SIZE, length), f32)],
        query, low, out, log_total, grad, cosine, sine, *kv,
    )


def pack_body(q_ref, kv_ref, bc_ref, step_ref, gains_ref, ssm_ref, inner_ref, basis_ref, valid_ref, out_ref, small_ref):
    rows, heads = step_ref.shape
    small_ref[...] = jnp.zeros_like(small_ref)
    small_ref[heads : heads + 2, :rows] = gains_ref[...].astype(f32)
    small_ref[heads + 2 : heads + 3, : ssm_ref.shape[1]] = ssm_ref[...].astype(f32)
    small_ref[heads + 3 : heads + 3 + KC, : inner_ref.shape[1]] = inner_ref[...].astype(f32)
    small_ref[heads + 3 + KC : heads + 3 + 2 * KC, : basis_ref.shape[1]] = basis_ref[...].astype(f32)
    count = jnp.sum(valid_ref[...].astype(f32), axis=1, keepdims=True)
    high = jnp.floor(count * (1.0 / 16.0))
    small_ref[heads + 3 + 2 * KC : heads + 4 + 2 * KC, 0:1] = high
    small_ref[heads + 4 + 2 * KC : heads + 5 + 2 * KC, 0:1] = count - 16.0 * high
    tail = jnp.transpose(small_ref[...])[:rows, :]
    step = jnp.concatenate([step_ref[...].astype(f32), jnp.zeros((rows, 128 - heads), f32)], axis=1)
    at = 0
    for ref in (q_ref, kv_ref, bc_ref):
        out_ref[:, at : at + ref.shape[1]] = ref[...]
        at += ref.shape[1]
    out_ref[:, at:] = (tail + step).astype(bf16)


def packed(*args):
    columns = sum(a.shape[1] for a in args[:3]) + 128
    return call(pack_body, [((args[0].shape[0], columns), bf16)], [((128, 128), f32)], *args)[0]


def prep_body(x_ref, before_ref, xt_ref, scale_ref):
    length = x_ref.shape[0]
    for at in range(-HALO, length, HALO):
        if at < 0:
            first = HALO - before_ref.shape[0]
            block = jnp.concatenate([jnp.zeros((first, x_ref.shape[1]), f32), before_ref[...].astype(f32)], axis=0)
        else:
            block = x_ref[at : at + HALO, :].astype(f32)
        block = jnp.transpose(block)
        lanes = slice(at + HALO, at + 2 * HALO)
        xt_ref[:, lanes] = block.astype(bf16)
        mean = jnp.mean(block * block, axis=0, keepdims=True)
        scale_ref[:, lanes] = jnp.broadcast_to(lax.rsqrt(mean + eps), (8, HALO))


def prepared(x, before):
    length, features = x.shape
    return call(prep_body, [((features, length + HALO), bf16), ((8, length + HALO), f32)], [], x, before)


def params_body(shape, w_ref, xt_ref, scale_ref, inner_ref, basis_ref, gains_ref, n1_ref):
    ways, rows, inner_rows, bc_rows, heads, step_at = shape
    tail = w_ref[:, step_at:].astype(f32)
    for s in range(ways):
        inner_ref[s * inner_rows : (s + 1) * inner_rows, :] = tail[s * rows : s * rows + inner_rows, :]
        basis_ref[s * bc_rows : (s + 1) * bc_rows, :] = tail[s * rows : s * rows + bc_rows, :]
    gains_ref[...] = jnp.transpose(tail)
    for at in range(0, xt_ref.shape[1], HALO):
        lanes = slice(at, at + HALO)
        normed = xt_ref[:, lanes].astype(f32) * scale_ref[0:1, lanes] * tail[:, heads : heads + 1]
        n1_ref[:, lanes] = normed.astype(bf16)


def unpacked(shape, first_w, xt, scale):
    ways, rows, inner_rows, bc_rows, heads, step_at = shape
    return call(
        functools.partial(params_body, shape),
        [((ways * inner_rows, 128), f32), ((ways * bc_rows, 128), f32), ((128, ways * rows), f32), (xt.shape, bf16)],
        [],
        first_w, xt, scale,
    )


def rope_body(attn_width, lin_ref, cos_ref, sin_ref, q_ref, kv_ref):
    cosine, sine = cos_ref[...], sin_ref[...]
    for at in range(0, attn_width, HEAD_SIZE):
        query = rotated(lin_ref[at : at + HEAD_SIZE, HALO:], cosine, sine)
        q_ref[at : at + HEAD_SIZE, :] = query.astype(bf16) * bf16(HEAD_SIZE**-0.5)
    keys = lin_ref[attn_width : attn_width + HEAD_SIZE, HALO:]
    kv_ref[:HEAD_SIZE, :] = rotated(keys, cosine, sine).astype(bf16)
    kv_ref[HEAD_SIZE:, :] = lin_ref[attn_width + HEAD_SIZE : attn_width + 2 * HEAD_SIZE, HALO:].astype(bf16)


def roped(attn_width, first_lin, cosine, sine):
    length = cosine.shape[1]
    return call(
        functools.partial(rope_body, attn_width),
        [((attn_width, length), bf16), ((2 * HEAD_SIZE, length), bf16)],
        [],
        first_lin, cosine, sine,
    )


def conv_pre(block, taps, places):
    total = None
    for lag in range(KC):
        back = KC - 1 - lag
        moved = pltpu.roll(block, back, 1) if back else block
        term = taps[:, lag : lag + 1] * moved[:, HALO:]
        if back:
            term = jnp.where(places >= back, term, 0.0)
        total = term if total is None else total + term
    return total


def sigmoid(value):
    return 1.0 / (1.0 + jnp.exp(-value))


def running_sum(value, reverse=False):
    width = value.shape[1]
    lane = lax.broadcasted_iota(jnp.int32, value.shape, 1)
    step = 1
    while step < width:
        if reverse:
            value = value + jnp.where(lane < width - step, pltpu.roll(value, width - step, 1), 0.0)
        else:
            value = value + jnp.where(lane >= step, pltpu.roll(value, step, 1), 0.0)
        step *= 2
    return value


def widened(rows):
    return jnp.transpose(jnp.concatenate([rows, jnp.zeros((112, rows.shape[1]), f32)], axis=0))


def pack_decay(ref, decay, first):
    wide = jnp.broadcast_to(decay, (16, DS))
    high = wide.astype(bf16)
    ref[first : first + 16, :] = high
    ref[first + 16 : first + 32, :] = (wide - high.astype(f32)).astype(bf16)


def chain(packs, heads, state_ref):
    width = heads * HEAD_SIZE
    for h in range(heads):
        rows = slice(h * HEAD_SIZE, (h + 1) * HEAD_SIZE)
        state = jnp.zeros((HEAD_SIZE, DS), f32)
        for pack in packs[::-1]:
            decay = pack[width : width + 16, :].astype(f32) + pack[width + 16 : width + 32, :].astype(f32)
            state = pack[rows, :].astype(f32) + decay[h : h + 1, :] * state
        state_ref[rows, :] = state


def conv_body(heads, bc_at, u_ref, lin_ref, inner_ref, basis_ref, hp_ref, place_ref, xs_ref, b_ref, c_ref, bt_ref, ct_ref, dt_ref, cum_ref, cumt_ref, pack_ref, end_ref):
    places = place_ref[0:1, :]
    length = places.shape[1]
    width = heads * HEAD_SIZE
    for at, flat, side in ((0, b_ref, bt_ref), (DS, c_ref, ct_ref)):
        taps = basis_ref[at : at + DS, heads + 3 + KC : heads + 3 + 2 * KC]
        pre = conv_pre(lin_ref[bc_at + at : bc_at + at + DS, :], taps, places)
        basis = pre * sigmoid(pre)
        side[...] = basis
        flat[...] = jnp.transpose(basis)
    raw = lin_ref[bc_at + 2 * DS : bc_at + 2 * DS + 16, HALO:] + hp_ref[:, 0:1]
    dt = jnp.maximum(raw, 0.0) + jnp.log1p(jnp.exp(-jnp.abs(raw)))
    cum = running_sum(dt * -jnp.exp(hp_ref[:, 1:2]))
    dt_ref[...] = dt
    cum_ref[...] = cum
    cumt_ref[...] = widened(cum)
    last = cum[:, length - 1 :]
    lane = lax.broadcasted_iota(jnp.int32, (1, length), 1)
    last_place = places[:, length - 1 :]
    reach = lane >= length - 1 - last_place
    to_end = jnp.where(reach, jnp.exp(jnp.minimum(last - cum, 0.0)) * dt, 0.0)
    end_ref[...] = to_end

    def one(h, _):
        rows = pl.ds(pl.multiple_of(h * HEAD_SIZE, HEAD_SIZE), HEAD_SIZE)
        pre = conv_pre(u_ref[rows, :], inner_ref[rows, :][:, heads + 3 : heads + 3 + KC], places)
        values = pre * sigmoid(pre)
        xs_ref[rows, :] = values
        summary = dot((values * end_ref[pl.ds(h, 1), :]).astype(bf16), low(b_ref[...]), 1, 0)
        pack_ref[rows, :] = summary.astype(bf16)
        return 0

    lax.fori_loop(0, heads, one, 0)
    keep = (last_place > length - 1).astype(f32)
    pack_decay(pack_ref, jnp.exp(last) * keep, width)


def conv_forward(heads, bc_at, u, lin, inner, basis, hp, places):
    length = places.shape[1]
    width = heads * HEAD_SIZE
    return call(
        functools.partial(conv_body, heads, bc_at),
        [
            ((width, length), f32),
            ((length, DS), f32),
            ((length, DS), f32),
            ((DS, length), f32),
            ((DS, length), f32),
            ((16, length), f32),
            ((16, length), f32),
            ((length, 128), f32),
            ((width + 32, DS), bf16),
        ],
        [((16, length), f32)],
        u, lin, inner, basis, hp, places,
    )


def chunk_rows(k, cum_ref, place_ref):
    lanes = slice(k * CHUNK, (k + 1) * CHUNK)
    cum = cum_ref[:, lanes]
    places = place_ref[0:1, lanes]
    base = cum_ref[:, k * CHUNK - 1 : k * CHUNK] if k else jnp.zeros((16, 1), f32)
    last = cum[:, CHUNK - 1 :]
    last_place = places[:, CHUNK - 1 :]
    lane = lax.broadcasted_iota(jnp.int32, (1, CHUNK), 1)
    entry = jnp.where(places > lane, jnp.exp(jnp.minimum(cum - base, 0.0)), 0.0)
    to_end = jnp.where(lane >= CHUNK - 1 - last_place, jnp.exp(jnp.minimum(last - cum, 0.0)), 0.0)
    over = jnp.where(last_place > CHUNK - 1, jnp.exp(jnp.minimum(last - base, 0.0)), 0.0)
    source = lax.broadcasted_iota(jnp.int32, (CHUNK, CHUNK), 0)
    target = lax.broadcasted_iota(jnp.int32, (CHUNK, CHUNK), 1)
    allowed = (source <= target) & (source >= target - places)
    return cum, entry, to_end, over, allowed


def mix_body(heads, packs, xs_ref, b_ref, ct_ref, dt_ref, cum_ref, cumt_ref, hp_ref, place_ref, z_ref, *refs):
    pack_refs = refs[:packs]
    y_ref, states_ref, squares_ref, state_ref, inter_ref, w_ref = refs[packs:]
    length = place_ref.shape[1]
    chain(pack_refs, heads, state_ref)
    for k in range(length // CHUNK):
        lanes = slice(k * CHUNK, (k + 1) * CHUNK)
        cum, entry, to_end, over, allowed = chunk_rows(k, cum_ref, place_ref)
        low_state = state_ref[...].astype(bf16)
        states_ref[k] = low_state
        side = ct_ref[:, lanes]
        match = jnp.where(allowed, exact(b_ref[lanes, :], side, 1, 0), 0.0)
        inter_ref[...] = dot(low_state, low(side), 1, 0)
        squares = jnp.zeros((1, CHUNK), f32)
        for h in range(heads):
            rows = slice(h * HEAD_SIZE, (h + 1) * HEAD_SIZE)
            spread = cum[h : h + 1, :] - cumt_ref[lanes, h : h + 1]
            mixing = (jnp.exp(jnp.minimum(spread, 0.0)) * match).astype(bf16)
            values = xs_ref[rows, lanes]
            stepped = values * dt_ref[h : h + 1, lanes]
            result = dot(stepped.astype(bf16), mixing, 1, 0)
            result = result + inter_ref[rows, :] * entry[h : h + 1, :] + hp_ref[h : h + 1, 2:3] * values
            y_ref[rows, lanes] = result
            w_ref[rows, :] = (stepped * to_end[h : h + 1, :]).astype(bf16)
            gate = z_ref[rows, lanes]
            gated = result * gate * sigmoid(gate)
            squares = squares + jnp.sum(gated * gated, axis=0, keepdims=True)
        squares_ref[:, lanes] = jnp.broadcast_to(squares, (8, CHUNK))
        if k + 1 < length // CHUNK:
            added = dot(w_ref[...], low(b_ref[lanes, :]), 1, 0)
            for h in range(heads):
                rows = slice(h * HEAD_SIZE, (h + 1) * HEAD_SIZE)
                state_ref[rows, :] = over[h : h + 1, :] * state_ref[rows, :] + added[rows, :]


def mix_forward(heads, xs, b, ct, dt, cum, cumt, hp, places, z, packs):
    length = places.shape[1]
    width = heads * HEAD_SIZE
    return call(
        functools.partial(mix_body, heads, len(packs)),
        [
            ((width, length), f32),
            ((length // CHUNK, width, DS), bf16),
            ((8, length), f32),
        ],
        [((width, DS), f32), ((width, CHUNK), f32), ((width, CHUNK), bf16)],
        xs, b, ct, dt, cum, cumt, hp, places, z, *packs,
    )


def gate_body(heads, g_ref, y_ref, z_ref, gain_ref, inv_ref, dot_ref, c_ref, cum_ref, place_ref, gy_ref, gz_ref, ggain_ref, pack_ref, entry_ref):
    length = place_ref.shape[1]
    width = heads * HEAD_SIZE
    first = g_ref.shape[0] - width
    places = place_ref[0:1, :]
    inv = inv_ref[0:1, :]
    shrink = inv * inv * inv * dot_ref[0:1, :] * (1.0 / (HS * HEAD_SIZE))
    lane = lax.broadcasted_iota(jnp.int32, (1, length), 1)
    entry_ref[...] = jnp.where(places > lane, jnp.exp(jnp.minimum(cum_ref[...], 0.0)), 0.0)

    def one(h, _):
        start = pl.multiple_of(h * HEAD_SIZE, HEAD_SIZE)
        rows = pl.ds(start, HEAD_SIZE)
        grad = g_ref[pl.ds(start + first, HEAD_SIZE), :] * inv
        values = y_ref[rows, :]
        gate = z_ref[rows, :]
        sig = sigmoid(gate)
        silu = gate * sig
        gated = values * silu
        column = lax.broadcasted_iota(jnp.int32, (HEAD_SIZE, 128), 1)
        ggain_ref[rows, :] = jnp.where(column == heads + 2, jnp.sum(grad * gated, axis=1, keepdims=True), 0.0)
        grad_gated = grad * gain_ref[rows, :][:, heads + 2 : heads + 3] - shrink * gated
        grad_values = grad_gated * silu
        gy_ref[rows, :] = grad_values
        gz_ref[rows, :] = (grad_gated * values * sig * (1.0 + gate * (1.0 - sig))).astype(bf16)
        entered = (grad_values * entry_ref[pl.ds(h, 1), :]).astype(bf16)
        pack_ref[rows, :] = dot(entered, low(c_ref[...]), 1, 0).astype(bf16)
        return 0

    lax.fori_loop(0, heads, one, 0)
    last = length - 1
    keep = (places[:, last:] > last).astype(f32)
    pack_decay(pack_ref, jnp.exp(cum_ref[:, last:]) * keep, width)


def gate_back(heads, grads, y, z, gain, inv, inner, c, cum, places):
    length = places.shape[1]
    width = heads * HEAD_SIZE
    return call(
        functools.partial(gate_body, heads),
        [
            ((width, length), f32),
            ((width, length), bf16),
            ((width, 128), f32),
            ((width + 32, DS), bf16),
        ],
        [((16, length), f32)],
        grads, y, z, gain, inv, inner, c, cum, places,
    )


def mix_back_body(heads, packs, step_at, gy_ref, xs_ref, b_ref, c_ref, bt_ref, ct_ref, dt_ref, cum_ref, cumt_ref, lin_ref, hp_ref, place_ref, states_ref, *refs):
    pack_refs = refs[:packs]
    gxs_ref, gbc_ref, gstep_ref, grow_ref, ghead_ref, grad_ref, reach_ref, inter_ref, gye_ref, w_ref, col_ref, cumg_ref, dtg_ref = refs[packs:]
    length = place_ref.shape[1]
    chain(pack_refs, heads, grad_ref)
    col_ref[...] = jnp.zeros_like(col_ref)
    cumg_ref[...] = jnp.zeros_like(cumg_ref)
    dtg_ref[...] = jnp.zeros_like(dtg_ref)
    rate = -jnp.exp(hp_ref[:, 1:2])
    bias_sum = jnp.zeros((16, CHUNK), f32)
    rate_sum = jnp.zeros((16, CHUNK), f32)
    ghead_ref[...] = jnp.zeros_like(ghead_ref)
    at_last = lax.broadcasted_iota(jnp.int32, (1, CHUNK), 1) == CHUNK - 1
    for k in reversed(range(length // CHUNK)):
        lanes = slice(k * CHUNK, (k + 1) * CHUNK)
        cum, entry, to_end, over, allowed = chunk_rows(k, cum_ref, place_ref)
        b_side, c_side = bt_ref[:, lanes], ct_ref[:, lanes]
        b_flat, c_flat = b_ref[lanes, :], c_ref[lanes, :]
        match = jnp.where(allowed, exact(b_flat, c_side, 1, 0), 0.0)
        low_grad = grad_ref[...].astype(bf16)
        reach_ref[...] = dot(low_grad, low(b_side), 1, 0)
        inter_ref[...] = dot(states_ref[k], low(c_side), 1, 0)
        grad_match = jnp.zeros((CHUNK, CHUNK), f32)
        for h in range(heads):
            rows = slice(h * HEAD_SIZE, (h + 1) * HEAD_SIZE)
            head = slice(h, h + 1)
            grad = gy_ref[rows, lanes]
            values = xs_ref[rows, lanes]
            dt = dt_ref[head, lanes]
            stepped = values * dt
            decay = jnp.exp(jnp.minimum(cum[head, :] - cumt_ref[lanes, head], 0.0))
            mixing = decay * match
            low_y = grad.astype(bf16)
            grad_mixing = dot(stepped.astype(bf16), low_y, 0, 0)
            grad_match = grad_match + grad_mixing * decay
            spread = grad_mixing * mixing
            to = to_end[head, :]
            reached = reach_ref[rows, :] * to
            grad_stepped = dot(low_y, mixing.astype(bf16), 1, 1) + reached
            ended = jnp.sum(reached * stepped, axis=0, keepdims=True)
            entered = grad * entry[head, :]
            entry_sum = jnp.sum(entered * inter_ref[rows, :], axis=0, keepdims=True)
            kept = over[head, :] * jnp.sum(
                jnp.sum(grad_ref[rows, :] * states_ref[k, rows, :].astype(f32), axis=0, keepdims=True),
                axis=1, keepdims=True,
            )
            at_end = jnp.sum(ended, axis=1, keepdims=True) + kept
            cumg_ref[head, :] = (
                jnp.sum(spread, axis=0, keepdims=True) + entry_sum - ended + jnp.where(at_last, at_end, 0.0)
            )
            col_ref[:, head] = jnp.sum(spread, axis=1, keepdims=True)
            dtg_ref[head, :] = jnp.sum(grad_stepped * values, axis=0, keepdims=True)
            gxs_ref[rows, lanes] = grad_stepped * dt + hp_ref[head, 2:3] * grad
            ghead_ref[head, 2:3] += jnp.sum(
                jnp.sum(grad * values, axis=0, keepdims=True), axis=1, keepdims=True
            )
            gye_ref[rows, :] = entered.astype(bf16)
            w_ref[rows, :] = (stepped * to).astype(bf16)
        low_match = jnp.where(allowed, grad_match, 0.0)
        gbc_ref[:DS, lanes] = exact(c_side, low_match, 1, 1) + dot(low_grad, w_ref[...], 0, 0)
        gbc_ref[DS:, lanes] = exact(b_side, low_match, 1, 0) + dot(states_ref[k], gye_ref[...], 0, 0)
        if k:
            added = dot(gye_ref[...], low(c_flat), 1, 0)
            for h in range(heads):
                rows = slice(h * HEAD_SIZE, (h + 1) * HEAD_SIZE)
                grad_ref[rows, :] = over[h : h + 1, :] * grad_ref[rows, :] + added[rows, :]
        grad_log = running_sum(cumg_ref[...] - jnp.transpose(col_ref[...])[:16, :], reverse=True)
        dt = dt_ref[:, lanes]
        rate_sum = rate_sum + grad_log * dt
        grad_step = (dtg_ref[...] + grad_log * rate) * sigmoid(lin_ref[step_at : step_at + 16, HALO:][:, lanes] + hp_ref[:, 0:1])
        gstep_ref[:, lanes] = grad_step
        bias_sum = bias_sum + grad_step
    ghead_ref[:, 0:1] = jnp.sum(bias_sum, axis=1, keepdims=True)
    ghead_ref[:, 1:2] = jnp.sum(rate_sum, axis=1, keepdims=True) * rate
    side = jnp.transpose(jnp.concatenate([ghead_ref[...], jnp.zeros((112, 128), f32)], axis=0))
    lane = lax.broadcasted_iota(jnp.int32, (8, 128), 1)
    row = jnp.zeros((8, 128), f32)
    for j in range(3):
        own = jnp.where(lane < heads, jnp.broadcast_to(side[j : j + 1, :], (8, 128)), 0.0)
        row = row + pltpu.roll(own, heads + 3 + 2 * KC + j * heads, 1)
    grow_ref[...] = row


def mix_back(heads, step_at, gy, xs, b, c, bt, ct, dt, cum, cumt, lin, hp, places, states, packs):
    length = places.shape[1]
    width = heads * HEAD_SIZE
    return call(
        functools.partial(mix_back_body, heads, len(packs), step_at),
        [
            ((width, length), f32),
            ((2 * DS, length), f32),
            ((16, length), f32),
            ((8, 128), f32),
        ],
        [
            ((16, 128), f32),
            ((width, DS), f32),
            ((width, CHUNK), f32),
            ((width, CHUNK), f32),
            ((width, CHUNK), bf16),
            ((width, CHUNK), bf16),
            ((CHUNK, 128), f32),
            ((16, CHUNK), f32),
            ((16, CHUNK), f32),
        ],
        gy, xs, b, c, bt, ct, dt, cum, cumt, lin, hp, places, states, *packs,
    )


def conv_back_body(heads, bc_at, u_ref, lin_ref, gxs_ref, gbc_ref, inner_ref, basis_ref, place_ref, g_ref, halo_ref, ginner_ref, gbasis_ref):
    places = place_ref[0:1, :]
    length = places.shape[1]
    width = u_ref.shape[0]

    def one(block, grads, taps, first, sums_ref, at):
        pre = conv_pre(block, taps, places)
        sig = sigmoid(pre)
        grad_pre = grads * sig * (1.0 + pre * (1.0 - sig))
        total = None
        for lag in range(KC):
            back = KC - 1 - lag
            counted = jnp.where(places >= back, grad_pre, 0.0) if back else grad_pre
            moved = pltpu.roll(block, back, 1) if back else block
            sums_ref[at, first + lag : first + lag + 1] = jnp.sum(counted * moved[:, HALO:], axis=1, keepdims=True)
            wide = jnp.concatenate([jnp.zeros((counted.shape[0], HALO), f32), counted * taps[:, lag : lag + 1]], axis=1)
            wide = pltpu.roll(wide, length + HALO - back, 1) if back else wide
            total = wide if total is None else total + wide
        return total[:, HALO:], jnp.transpose(total[:, :HALO])[HALO - 8 :, :]

    ginner_ref[...] = jnp.zeros_like(ginner_ref)
    gbasis_ref[...] = jnp.zeros_like(gbasis_ref)

    def inner(i, _):
        start = pl.multiple_of(i * 128, 128)
        rows = pl.ds(start, 128)
        taps = inner_ref[rows, :][:, heads + 3 : heads + 3 + KC]
        own, halo = one(u_ref[rows, :], gxs_ref[rows, :], taps, heads + 3, ginner_ref, rows)
        g_ref[rows, :] = own
        halo_ref[:, pl.ds(start, 128)] = halo
        return 0

    lax.fori_loop(0, width // 128, inner, 0)
    for i in range(0, 2 * DS, 128):
        rows = slice(i, i + 128)
        first = heads + 3 + KC
        block = lin_ref[bc_at + i : bc_at + i + 128, :]
        own, halo = one(block, gbc_ref[rows, :], basis_ref[rows, first : first + KC], first, gbasis_ref, rows)
        g_ref[width + i : width + i + 128, :] = own
        halo_ref[:, width + i : width + i + 128] = halo


def conv_back(heads, bc_at, u, lin, gxs, gbc, inner, basis, places):
    length = places.shape[1]
    width = u.shape[0]
    return call(
        functools.partial(conv_back_body, heads, bc_at),
        [((width + 2 * DS, length), f32), ((8, width + 2 * DS), f32), ((width, 128), f32), ((2 * DS, 128), f32)],
        [],
        u, lin, gxs, gbc, inner, basis, places,
    )


def early_body(pieces, n1_ref, gq_ref, gz_ref, cos_ref, sin_ref, first_ref, z_ref, *refs):
    kv_refs = refs[:pieces]
    gw_ref, gn_ref = refs[pieces:]
    n1 = n1_ref[:, HALO:]
    gkv = kv_refs[0][...].astype(f32)
    for ref in kv_refs[1:]:
        gkv = gkv + ref[...].astype(f32)
    gkv = jnp.concatenate([rotated(gkv[:HEAD_SIZE], cos_ref[...], -sin_ref[...]), gkv[HEAD_SIZE:]], axis=0).astype(bf16)
    at = 0
    total = None
    for grad, weights in ((gz_ref[...], z_ref[...]), (gq_ref[...], first_ref), (gkv, first_ref)):
        rows = grad.shape[0]
        gw_ref[:, at : at + rows] = dot(n1, grad, 1, 1).astype(bf16)
        if weights is first_ref:
            first = at - gz_ref.shape[0]
            weights = first_ref[:, first : first + rows]
        term = dot(weights, grad, 1, 0)
        total = term if total is None else total + term
        at += rows
    gn_ref[...] = total


def rows_call(body, outs, cuts, *args):
    blocks = 4

    def spec(shape, cut=0):
        if cut is None:
            return pl.BlockSpec(shape, lambda i: (0,) * len(shape))
        if cut == 1:
            return pl.BlockSpec((shape[0], shape[1] // blocks), lambda i: (0, i))
        return pl.BlockSpec((shape[0] // blocks, cut or shape[1]), lambda i: (i, 0))

    return pl.pallas_call(
        body,
        grid=(blocks,),
        out_shape=[jax.ShapeDtypeStruct(s, d) for s, d in outs],
        in_specs=[spec(a.shape, cut) for a, cut in zip(args, cuts, strict=True)],
        out_specs=[spec(s) for s, _ in outs],
        compiler_params=pltpu.CompilerParams(vmem_limit_bytes=VMEM_LIMIT),
        cost_estimate=pl.CostEstimate(flops=1000, bytes_accessed=1000, transcendentals=0),
    )(*args)


def early_products(n1, gq, gz, cosine, sine, first_w, last_w, gkv):
    features, length = n1.shape[0], gq.shape[1]
    columns = gq.shape[0] + gkv[0].shape[0] + gz.shape[0]
    return rows_call(
        functools.partial(early_body, len(gkv)),
        [((features, columns), bf16), ((features, length), f32)],
        (0, None, None, None, None, 0, gz.shape[0]) + (None,) * len(gkv),
        n1, gq, gz, cosine, sine, first_w, last_w, *gkv,
    )


def join_body(width, heads, g_ref, behind_ref, step_ref, low_ref):
    length = g_ref.shape[1]
    if length > 128:
        low_ref[: g_ref.shape[0], : length - 128] = g_ref[:, : length - 128].astype(bf16)
    behind = jnp.concatenate([jnp.zeros((120, behind_ref.shape[1]), f32), behind_ref[...]], axis=0)
    low_ref[: g_ref.shape[0], length - 128 :] = (g_ref[:, length - 128 :] + jnp.transpose(behind)).astype(bf16)
    row = lax.broadcasted_iota(jnp.int32, (16, length), 0)
    step = jnp.where(row < heads, step_ref[...], 0.0)
    low_ref[g_ref.shape[0] :, :] = jnp.concatenate([step, jnp.zeros((112, length), f32)], axis=0).astype(bf16)


def joined(heads, grads, behind, step):
    rows, length = grads.shape
    return call(functools.partial(join_body, rows, heads), [((rows + 128, length), bf16)], [], grads, behind, step)[0]


def late_body(shape, width, rest_at, n1_ref, xt_ref, scale_ref, g_ref, first_ref, u_ref, gn_ref, two_ref, inner_a_ref, inner_b_ref, basis_ref, head_ref, loss_ref, gw_ref, total_ref, low_ref, tail_ref):
    rows, inner_rows, bc_rows, heads = shape
    grad = g_ref[...]
    columns = grad.shape[0]
    made = dot(n1_ref[:, HALO:], grad, 1, 1)
    gw_ref[:, : columns - 128] = made[:, : columns - 128].astype(bf16)
    total = gn_ref[...] + dot(u_ref[...], grad[:width], 1, 0) + dot(first_ref[:, rest_at:], grad[width:], 1, 0)
    total_ref[...] = total
    low_ref[...] = total.astype(bf16)
    scaled = xt_ref[:, HALO:].astype(f32) * scale_ref[0:1, HALO:]
    column = lax.broadcasted_iota(jnp.int32, tail_ref.shape, 1)
    one = jnp.sum(total * scaled, axis=1, keepdims=True)
    two = jnp.concatenate([two_ref[...], jnp.zeros((120, two_ref.shape[1]), f32)], axis=0)
    two = jnp.transpose(two)[:, 0:1]
    tail_ref[...] = made[:, columns - 128 :] + jnp.where(column == heads, one, jnp.where(column == heads + 1, two, 0.0))
    for s in range(tail_ref.shape[0] // rows):
        inner = slice(s * inner_rows, (s + 1) * inner_rows)
        tail_ref[s * rows : s * rows + inner_rows, :] += inner_a_ref[inner, :] + inner_b_ref[inner, :]
        tail_ref[s * rows : s * rows + bc_rows, :] += basis_ref[s * bc_rows : (s + 1) * bc_rows, :]
        tail_ref[s * rows : s * rows + 1, :] += head_ref[0:1, :] + loss_ref[0:1, :]
    value = tail_ref[...]
    high = value.astype(bf16).astype(f32)
    rest = pltpu.roll(value - high, 64, 1)
    gw_ref[:, columns - 128 :] = jnp.where(column < 64, high, jnp.where(column < 64 + heads, 0.0, rest)).astype(bf16)


def late_products(shape, width, rest_at, n1, xt, scale, grads, first_w, u_w, gn, two, inner_a, inner_b, basis, head, loss):
    features, length = gn.shape
    return rows_call(
        functools.partial(late_body, shape, width, rest_at),
        [((features, grads.shape[0]), bf16), ((features, length), f32), ((features, length), bf16), ((features, 128), f32)],
        (0, 0, None, None, 0, 0, 0, 1, 0, 0, 0, None, None),
        n1, xt, scale, grads, first_w, u_w, gn, two, inner_a, inner_b, basis, head, loss,
    )[:3]


def finish_body(shape, total_ref, other_ref, count_ref, bc_ref, norm_ref, step_ref, ssm_ref, two_ref, inner_ref, basis_ref, head_ref, loss_ref):
    rows, inner_rows, bc_rows, heads, bc_at = shape
    bc_width = bc_ref.shape[1]
    bc_ref[...] = total_ref[:, bc_at : bc_at + bc_width] + other_ref[:, :bc_width]
    tail = total_ref[:, bc_at + bc_width :]
    own = jnp.where(lax.broadcasted_iota(jnp.int32, tail.shape, 1) < heads, tail, tail + pltpu.roll(tail, 64, 1))
    step_ref[...] = own[:, :heads]
    other = other_ref[:, bc_width:]
    both = own + other + pltpu.roll(other, 64, 1)
    own = jnp.concatenate([own, jnp.zeros((128 - rows, 128), f32)], axis=0) if rows < 128 else own
    both = jnp.concatenate([both, jnp.zeros((128 - rows, 128), f32)], axis=0) if rows < 128 else both
    side, side_both = jnp.transpose(own), jnp.transpose(both)
    norm_ref[...] = side_both[heads : heads + 1, :rows]
    two_ref[...] = side[heads + 1 : heads + 2, :rows]
    ssm_ref[...] = side[heads + 2 : heads + 3, :inner_rows]
    inner_ref[...] = side[heads + 3 : heads + 3 + KC, :inner_rows]
    basis_ref[...] = side_both[heads + 3 + KC : heads + 3 + 2 * KC, :bc_rows]
    at = heads + 3 + 2 * KC
    for j in range(3):
        head_ref[j : j + 1, :] = own[0:1, at + j * heads : at + (j + 1) * heads]
    loss_ref[...] = own[0:1, at + 3 * heads : at + 3 * heads + 1] / (count_ref[0:1, 0:1] * MODEL_WIDTH)


def finished(shape, total, other, count):
    rows, inner_rows, bc_rows, heads, _ = shape
    return call(
        functools.partial(finish_body, shape),
        [
            ((rows, 2 * DS), f32),
            ((1, rows), f32),
            ((rows, heads), f32),
            ((1, inner_rows), f32),
            ((1, rows), f32),
            ((KC, inner_rows), f32),
            ((KC, bc_rows), f32),
            ((3, heads), f32),
            ((1, 1), f32),
        ],
        [],
        total, other, count,
    )


def input_body(own_ref, low_ref, x_ref, res_ref, gain_ref, out_ref):
    length = x_ref.shape[0]
    for at in range(0, length, HALO):
        rows = slice(at, at + HALO)
        grad = jnp.transpose(own_ref[:, rows] + low_ref[:, rows].astype(f32)) * gain_ref[0:1, :]
        x = x_ref[rows, :].astype(f32)
        scale = lax.rsqrt(jnp.mean(x * x, axis=1, keepdims=True) + eps)
        inner = jnp.mean(grad * x, axis=1, keepdims=True)
        out_ref[rows, :] = res_ref[rows, :] + scale * grad - scale * scale * scale * x * inner


def input_grad(own, low, x, res, gain):
    return call(input_body, [(x.shape, f32)], [], own, low, x, res, gain)[0]


def mlp_grads_body(n2_ref, e_ref, ggu_ref, m_ref, out_ref):
    both = ggu_ref.shape[1]
    out_ref[:, :both] = dot(n2_ref[...], ggu_ref[...], 0, 0).astype(bf16)
    out_ref[:, both:] = dot(e_ref[...], m_ref[...], 0, 0).astype(bf16)


def mlp_weight_grads(n2, e, ggu, m):
    length, features = n2.shape
    blocks = 4
    columns = ggu.shape[1] + m.shape[1]
    cut = pl.BlockSpec((length, features // blocks), lambda i: (0, i))
    return pl.pallas_call(
        mlp_grads_body,
        grid=(blocks,),
        out_shape=jax.ShapeDtypeStruct((features, columns), bf16),
        in_specs=[cut, cut, pl.BlockSpec(ggu.shape, lambda i: (0, 0)), pl.BlockSpec(m.shape, lambda i: (0, 0))],
        out_specs=pl.BlockSpec((features // blocks, columns), lambda i: (i, 0)),
        compiler_params=pltpu.CompilerParams(vmem_limit_bytes=VMEM_LIMIT),
        cost_estimate=pl.CostEstimate(flops=1000, bytes_accessed=1000, transcendentals=0),
    )(n2, e, ggu, m)


def residual_body(own_ref, low_ref, res_ref, gf_ref, gain_ref, out_ref, ea_ref, ggain_ref):
    total = jnp.zeros((1, res_ref.shape[1]), f32)
    for at in range(0, res_ref.shape[0], HALO):
        rows = slice(at, at + HALO)
        grad = own_ref[rows, :] + low_ref[rows, :].astype(f32)
        res = res_ref[rows, :]
        scale = lax.rsqrt(jnp.mean(res * res, axis=1, keepdims=True) + eps)
        total = total + jnp.sum(grad * (res * scale), axis=0, keepdims=True)
        grad = grad * gain_ref[0:1, :]
        inner = jnp.mean(grad * res, axis=1, keepdims=True)
        grad = gf_ref[rows, :] + scale * grad - scale * scale * scale * res * inner
        out_ref[rows, :] = grad
        ea_ref[rows, :] = grad.astype(bf16)
    ggain_ref[...] = jnp.broadcast_to(total, ggain_ref.shape)


def residual_back(own, low, res, gf, gain):
    return call(
        residual_body, [(res.shape, f32), (res.shape, bf16), ((8, res.shape[1]), f32)], [], own, low, res, gf, gain
    )


def rms_scale(values):
    return lax.rsqrt(jnp.mean(values * values, axis=-1, keepdims=True) + eps)


def norm_back(inputs, inv_rms, grad_normed):
    inner_mean = jnp.mean(grad_normed * inputs, axis=-1, keepdims=True)
    return inv_rms * grad_normed - inv_rms * inv_rms * inv_rms * inputs * inner_mean


def padded_rows(block, rows):
    return jnp.pad(block, ((0, rows - block.shape[0]), (0, 0)))


def shards(
    hidden,
    teacher,
    positions,
    valid_mask,
    norm_gain,
    w_query,
    key_value_weight,
    w_gatein,
    w_bc,
    w_step,
    ssm_gain,
    mlp_gain,
    w_gateup,
    w_out_attn,
    w_out_ssm,
    w_down,
    conv_inner,
    conv_bc,
    head_params,
):
    ways = lax.axis_size(("fsdp", "ctx"))
    blocks = lax.axis_size("ctx")
    rows = norm_gain.shape[0]
    length = hidden.shape[1]
    heads = w_step.shape[1]
    width = heads * HEAD_SIZE
    attn_width = w_query.shape[1]
    kv_width = key_value_weight.shape[2]
    ff_local = w_down.shape[0]
    inner_rows = ssm_gain.shape[0]
    bc_rows = conv_bc.shape[1]
    qkv_width = attn_width + 2 * kv_width
    step_at = qkv_width + 2 * DS

    live_rows = valid_mask.reshape(length, 1).astype(f32)
    count_at = heads + 3 + 2 * KC
    first_shard = packed(
        w_query,
        key_value_weight.reshape(rows, 2 * kv_width),
        w_bc,
        w_step,
        jnp.stack([norm_gain, mlp_gain]),
        ssm_gain[None],
        conv_inner,
        conv_bc,
        valid_mask,
    )
    mlp_shard = jnp.concatenate([w_gateup.reshape(rows, 2 * ff_local), w_down.T], axis=1)
    u_shard = w_gatein[:, 1]
    last_shard = jnp.concatenate([w_gatein[:, 0], jnp.concatenate([w_out_attn, w_out_ssm], axis=0).T], axis=1)

    flat_in = hidden.reshape(length, MODEL_WIDTH)
    first_line = gathered_line(first_shard, False)
    before = passed_along(flat_in[length - 16 :], "ctx", 1)
    u_shard, first_line = tied(u_shard, first_line)
    u_line = gathered_line(u_shard)
    first_w = gathered_plane(first_line)
    mlp_w = lax.all_gather(mlp_shard, ("fsdp", "ctx"), axis=0, tiled=True)

    places = positions.reshape(1, length)
    place_rows = jnp.broadcast_to(places, (8, length))
    low_rows = jnp.broadcast_to(jnp.arange(length, dtype=jnp.int32)[None] - places, (8, length))
    half = HEAD_SIZE // 2
    frequency = rope_base ** (-2.0 * jnp.arange(half, dtype=f32) / HEAD_SIZE)
    angle = frequency[:, None] * places.astype(f32)
    cosine, sine = jnp.cos(angle), jnp.sin(angle)
    hp = jnp.pad(head_params.T, ((0, 16 - heads), (0, 125)))
    xt, scale_one = prepared(flat_in, before)
    xt, scale_one, cosine, sine, hp, first_w = lax.optimization_barrier((xt, scale_one, cosine, sine, hp, first_w))

    shape = (ways, rows, inner_rows, bc_rows, heads, step_at)
    par_inner, par_basis, param_rows, n1 = unpacked(shape, first_w, xt, scale_one)
    total_count = jnp.sum(param_rows[count_at]) * 16.0 + jnp.sum(param_rows[count_at + 1])
    gain_ssm = par_inner[:, heads + 2 : heads + 3]
    gain_two = param_rows[heads + 1 : heads + 2]
    gain_two_rows = jnp.broadcast_to(gain_two, (8, MODEL_WIDTH))

    first_lin = dot(first_w, n1, 0, 0)
    query, kv_own = roped(attn_width, first_lin, cosine, sine)
    last_shard, kv_own = tied(last_shard, kv_own)
    last_line = gathered_line(last_shard)
    kv = [kv_own] + [passed_along(kv_own, "ctx", s) for s in range(1, blocks)]
    u_w = gathered_plane(u_line)
    attn, log_total = attend(query, low_rows, kv)
    u_w, attn = tied(u_w, attn)
    u_in = dot(u_w, n1, 0, 0)

    xs, b_flat, c_flat, b_side, c_side, dt, cum, cumt, pack = conv_forward(
        heads, qkv_width, u_in, first_lin, par_inner, par_basis, hp, place_rows
    )
    packs = [passed_along(pack, "ctx", s) for s in range(1, blocks)]
    last_w = gathered_plane(last_line)
    last_w, packs = tied(last_w, packs)
    z_w, out_w = last_w[:, :width], last_w[:, width:]
    gateup_w, down_w = mlp_w[:, : 2 * ff_local], mlp_w[:, 2 * ff_local :]
    gate_z = dot(z_w, n1[:, HALO:], 0, 0)
    ssm, states, squares = mix_forward(heads, xs, b_flat, c_side, dt, cum, cumt, hp, place_rows, gate_z, packs)
    inv_ssm = lax.rsqrt((squares + swapped(squares)) / (HS * HEAD_SIZE) + eps)
    gated = ssm * jax.nn.silu(gate_z)
    branches = jnp.concatenate([attn, (gated * gain_ssm * inv_ssm[0:1]).astype(bf16)], axis=0)
    part = dot(branches, out_w, 0, 1)
    residual = flat_in.astype(f32) + (part + swapped(part.astype(bf16)).astype(f32))

    scale_two = rms_scale(residual)
    normed_two = (residual * scale_two * gain_two).astype(bf16)
    gateup = dot(normed_two, gateup_w, 1, 0)
    gate_part, up_part = gateup[:, :ff_local], gateup[:, ff_local:]
    hidden_mlp = (jax.nn.silu(gate_part) * up_part).astype(bf16)
    part = dot(hidden_mlp, down_w, 1, 1)
    final_rows = residual + (part + swapped(part.astype(bf16)).astype(f32))
    difference = (final_rows - teacher.reshape(length, MODEL_WIDTH).astype(f32)) * live_rows
    local_sq = jnp.sum(difference * difference)

    all_tokens = length * ways
    grad_final = difference * (all_tokens / total_count)
    grad_low = grad_final.astype(bf16)
    grad_hidden_mlp = dot(grad_low, down_w, 1, 0)
    sigma = jax.nn.sigmoid(gate_part)
    grad_gate = grad_hidden_mlp * up_part * sigma * (1.0 + gate_part * (1.0 - sigma))
    grad_up = grad_hidden_mlp * gate_part * sigma
    grad_gateup = jnp.concatenate([grad_gate, grad_up], axis=-1).astype(bf16)
    part = dot(grad_gateup, gateup_w, 1, 1)
    low_part, grad_gateup = tied(part.astype(bf16), grad_gateup)
    loss_lane = heads + 3 + 2 * KC + 3 * heads
    loss_row = jnp.where(lax.broadcasted_iota(jnp.int32, (8, 128), 1) == loss_lane, local_sq, 0.0)
    mlp_grads = mlp_weight_grads(normed_two, grad_low, grad_gateup, hidden_mlp)
    mlp_out = lax.psum_scatter(mlp_grads, "fsdp", scatter_dimension=0, tiled=True)
    grad_residual, grad_out, grad_gain_two = residual_back(part, swapped(low_part), residual, grad_final, gain_two_rows)

    grad_branches = dot(out_w, grad_out, 0, 1)
    grad_attn = grad_branches[:attn_width].astype(bf16)
    inner = jnp.sum(grad_branches[attn_width:] * gated * gain_ssm, axis=0, keepdims=True)
    inner = jnp.broadcast_to(inner, (8, length))
    inner = inner + swapped(inner)
    gy, grad_z, grad_gain_ssm, back_pack = gate_back(
        heads, grad_branches, ssm, gate_z, par_inner, inv_ssm, inner, c_flat, cum, place_rows
    )
    out_partial = dot(grad_out, branches, 0, 1).astype(bf16)
    grad_attn, out_partial, back_pack = tied(grad_attn, out_partial, back_pack)
    back_packs = [passed_along(back_pack, "ctx", -s) for s in range(1, blocks)]
    out_parts = scatter_first(out_partial)
    grad_query, *grad_kv = attend_back(query, low_rows, attn, log_total, grad_attn, cosine, sine, kv)
    back_packs, out_parts, grad_kv = lax.optimization_barrier((back_packs, out_parts, grad_kv))
    returned = [passed_along(grad_kv[s], "ctx", -s) for s in range(1, blocks)]
    out_parts = scatter_second(out_parts)
    grad_xs, grad_basis, grad_step, grad_head = mix_back(
        heads, step_at, gy, xs, b_flat, c_flat, b_side, c_side, dt, cum, cumt, first_lin, hp, place_rows, states, back_packs
    )
    *grad_kv, grad_xs = tied(grad_kv[0], *returned, grad_xs)
    early_w, grad_first = early_products(n1, grad_query, grad_z, cosine, sine, first_w, last_w, grad_kv)
    grad_xs, early_w = tied(grad_xs, early_w)
    early_parts = scatter_first(early_w)
    grad_conv, halo, grad_inner, grad_bc_taps = conv_back(
        heads, qkv_width, u_in, first_lin, grad_xs, grad_basis, par_inner, par_basis, place_rows
    )
    halo, mlp_out = tied(halo, mlp_out)
    mlp_out = lax.psum_scatter(mlp_out, "ctx", scatter_dimension=0, tiled=True)
    behind = passed_along(halo, "ctx", -1)
    behind, early_parts, out_parts = tied(behind, early_parts, out_parts)
    early_parts = scatter_second(early_parts)
    grad_late = joined(heads, grad_conv, behind, grad_step)
    late_w, grad_normed, low_normed = late_products(
        shape[1:-1], width, qkv_width, n1, xt, scale_one, grad_late, first_w, u_w, grad_first,
        grad_gain_two, grad_gain_ssm, grad_inner, grad_bc_taps, grad_head, loss_row,
    )
    gain_one = jnp.broadcast_to(param_rows[heads : heads + 1], (8, MODEL_WIDTH))
    late_w, low_normed, early_parts, out_parts = tied(late_w, low_normed, early_parts, out_parts)
    late_parts = scatter_first(late_w, heads)
    inner_kept, inner_other = halved([*early_parts, *out_parts])
    grad_input = input_grad(grad_normed, swapped(low_normed), flat_in, grad_residual, gain_one)
    gateup_out = mlp_out[:, : 2 * ff_local].astype(f32).reshape(rows, 2, ff_local)
    down_out = mlp_out[:, 2 * ff_local :].astype(f32).T
    late_parts, grad_input, gateup_out, down_out = tied(late_parts, grad_input, gateup_out, down_out)
    late_parts = scatter_second(late_parts, heads)
    late_parts, inner_other = tied(late_parts, inner_other)
    inner_parts = halved_on(inner_kept, inner_other)
    out_at = width + attn_width + 2 * kv_width
    query_out = inner_parts[:, width : width + attn_width]
    kv_out = inner_parts[:, width + attn_width : out_at].reshape(rows, 2, kv_width)
    attn_out = inner_parts[:, out_at : out_at + attn_width].T
    ssm_out = inner_parts[:, out_at + attn_width :].T
    late_out = scatter_third(late_parts)
    count_row = jnp.full((8, 128), total_count, f32)
    bc_out, norm_out, step_out, ssm_gain_out, mlp_gain_out, inner_out, basis_out, head_out, loss_value = finished(
        (rows, inner_rows, bc_rows, heads, width), late_out, swapped(late_out[:, width:]), count_row
    )
    return (
        final_rows.astype(bf16).reshape(1, length, MODEL_WIDTH),
        loss_value.reshape(()),
        grad_input.reshape(1, length, MODEL_WIDTH),
        norm_out.reshape(rows),
        query_out,
        kv_out,
        jnp.stack([inner_parts[:, :width], late_out[:, :width]], axis=1),
        bc_out,
        step_out,
        ssm_gain_out.reshape(inner_rows),
        mlp_gain_out.reshape(rows),
        gateup_out,
        attn_out,
        ssm_out,
        down_out,
        inner_out,
        basis_out,
        head_out,
    )


def solution(mesh):
    placed = (
        P("fsdp", "ctx", None),
        P("fsdp", "ctx", None),
        P("fsdp", "ctx"),
        P("fsdp", "ctx"),
        P(("fsdp", "ctx")),
        P(("fsdp", "ctx"), "tp"),
        P(("fsdp", "ctx"), None, "tp"),
        P(("fsdp", "ctx"), None, "tp"),
        P(("fsdp", "ctx"), None),
        P(("fsdp", "ctx"), "tp"),
        P(("tp", "fsdp", "ctx")),
        P(("fsdp", "ctx")),
        P(("fsdp", "ctx"), None, "tp"),
        P("tp", ("fsdp", "ctx")),
        P("tp", ("fsdp", "ctx")),
        P("tp", ("fsdp", "ctx")),
        P(None, ("tp", "fsdp", "ctx")),
        P(None, ("fsdp", "ctx")),
        P(None, "tp"),
    )
    return jax.shard_map(
        shards,
        mesh=mesh,
        in_specs=placed,
        out_specs=(
            P("fsdp", "ctx", None),
            P(),
            P("fsdp", "ctx", None),
            P(("fsdp", "ctx")),
            P(("fsdp", "ctx"), "tp"),
            P(("fsdp", "ctx"), None, "tp"),
            P(("fsdp", "ctx"), None, "tp"),
            P(("fsdp", "ctx"), None),
            P(("fsdp", "ctx"), "tp"),
            P(("tp", "fsdp", "ctx")),
            P(("fsdp", "ctx")),
            P(("fsdp", "ctx"), None, "tp"),
            P("tp", ("fsdp", "ctx")),
            P("tp", ("fsdp", "ctx")),
            P("tp", ("fsdp", "ctx")),
            P(None, ("tp", "fsdp", "ctx")),
            P(None, ("fsdp", "ctx")),
            P(None, "tp"),
        ),
        check_vma=False,
    )
```

profile of v0, /device:TPU:0, one launch (start us, length us, event | category | flops | bytes accessed | tf_op | source)
XLA Modules:
  0.0 427.5 jit_solution(15129251975483153661)
XLA Ops:
  14.0 5.1 %collective-permute-start = (bf16[64,768]{1,0:T(8,128)(2,1)S(1)}, bf16[64,768]{1,0:T(8,128)(2,1)S(1)}, u32[]{:S(2)}, u32[]{:S(2)}) collective-permute-start(bf16[64,768]{1,0:T(8,128)(2,1)S(1)} %shard_map.322), channel_id=1, source_target_pairs={{0,6},{2,0},{4,2},{6,4},{1,7},{3,1},{5,3},{7,5},{8,14},{10,8},{12,... | collective-permute-start | bytes 294920 | tf_op jit(solution)/shard_map/ppermute | solution.py:63
  20.8 4.4 %collective-permute-start.9 = (bf16[16,1024]{1,0:T(8,128)(2,1)S(1)}, bf16[16,1024]{1,0:T(8,128)(2,1)S(1)}, u32[]{:S(2)}, u32[]{:S(2)}) collective-permute-start(bf16[16,1024]{1,0:T(8,128)(2,1)S(1)} %slice_bitcast_fusion.4), channel_id=1, source_target_pairs={{0,2},{2,4},{4,6},{1,3},{3,5},{5,7},{8,10},{10,12},{12,14},{9,11},... | collective-permute-start | bytes 98312 | tf_op jit(solution)/shard_map/ppermute | solution.py:69
  45.2 6.0 %collective-permute-done.11 = bf16[2,4,64,384]{3,2,1,0:T(8,128)(2,1)S(1)} collective-permute-done((bf16[2,4,64,384]{3,2,1,0:T(8,128)(2,1)S(1)}, bf16[2,4,64,384]{3,2,1,0:T(8,128)(2,1)S(1)}, u32[]{:S(2)}, u32[]{:S(2)}) %collective-permute-start.11) | collective-permute-done | bytes 393248 | tf_op jit(solution)/shard_map/ppermute | solution.py:63
  56.6 2.0 collective-permute-start.17
  59.9 8.5 %collective-permute-done.17 = bf16[1,64,1792]{2,1,0:T(8,128)(2,1)} collective-permute-done((bf16[1,64,1792]{2,1,0:T(8,128)(2,1)}, bf16[1,64,1792]{2,1,0:T(8,128)(2,1)}, u32[]{:S(2)}, u32[]{:S(2)}) %collective-permute-start.17) | collective-permute-done | bytes 229408 | tf_op jit(solution)/shard_map/ppermute | solution.py:102
  71.4 6.2 %collective-permute-done.7 = bf16[4,64,384]{2,1,0:T(8,128)(2,1)S(1)} collective-permute-done((bf16[4,64,384]{2,1,0:T(8,128)(2,1)S(1)}, bf16[4,64,384]{2,1,0:T(8,128)(2,1)S(1)}, u32[]{:S(2)}, u32[]{:S(2)}) %collective-permute-start.7) | collective-permute-done | bytes 196640 | tf_op jit(solution)/shard_map/ppermute | solution.py:63
  78.9 3.6 collective-permute-start.14
  82.5 4.3 %collective-permute-start.15 = (bf16[128,512]{1,0:T(8,128)(2,1)S(1)}, bf16[128,512]{1,0:T(8,128)(2,1)S(1)}, u32[]{:S(2)}, u32[]{:S(2)}) collective-permute-start(bf16[128,512]{1,0:T(8,128)(2,1)S(1)} %copy-done.61), channel_id=1, source_target_pairs={{0,4},{2,6},{1,5},{3,7},{8,12},{10,14},{9,13},{11,15},{16,20},{18,... | collective-permute-start | bytes 393224 | tf_op jit(solution)/shard_map/ppermute | solution.py:69
  86.9 12.7 %collective-permute-done.18 = bf16[2,64,1792]{2,1,0:T(8,128)(2,1)S(1)} collective-permute-done((bf16[2,64,1792]{2,1,0:T(8,128)(2,1)S(1)}, bf16[2,64,1792]{2,1,0:T(8,128)(2,1)S(1)}, u32[]{:S(2)}, u32[]{:S(2)}) %collective-permute-start.18) | collective-permute-done | bytes 458784 | tf_op jit(solution)/shard_map/ppermute | solution.py:102
  102.2 7.3 %collective-permute-start.16 = (bf16[128,512]{1,0:T(8,128)(2,1)S(1)}, bf16[128,512]{1,0:T(8,128)(2,1)S(1)}, u32[]{:S(2)}, u32[]{:S(2)}) collective-permute-start(bf16[128,512]{1,0:T(8,128)(2,1)S(1)} %copy-done.61), channel_id=1, source_target_pairs={{0,6},{1,7},{8,14},{9,15},{16,22},{17,23},{24,30},{25,31}} | collective-permute-start | bytes 393224 | tf_op jit(solution)/shard_map/ppermute | solution.py:69
  111.0 3.8 collective-permute-done.16.refs_3_
  114.9 8.9 %shard_map.326 = (bf16[256,512]{1,0:T(8,128)(2,1)S(1)}, f32[4,8,512]{2,1,0:T(8,128)S(1)}) custom-call(bf16[256,512]{1,0:T(8,128)(2,1)S(1)} %copy-done.51, s32[8,512]{1,0:T(8,128)S(1)} %broadcast_in_dim.58.low_ref, bf16[128,512]{1,0:T(8,128)(2,1)S(1)} %copy-done.61, bf16[128,512]{1,0:T(8,128)(2,1)S(1)} %collective-permute-done.14.refs_1_, ...), custom_call_target="tpu_custom_call" | custom-call | flops 1000 | bytes 1000 | tf_op jit(solution)/shard_map/pallas_call | solution.py:190
  125.7 12.0 %collective-permute-done.6 = bf16[2,4,64,384]{3,2,1,0:T(8,128)(2,1)S(1)} collective-permute-done((bf16[2,4,64,384]{3,2,1,0:T(8,128)(2,1)S(1)}, bf16[2,4,64,384]{3,2,1,0:T(8,128)(2,1)S(1)}, u32[]{:S(2)}, u32[]{:S(2)}) %collective-permute-start.6) | collective-permute-done | bytes 393248 | tf_op jit(solution)/shard_map/ppermute | solution.py:63
  138.1 2.5 collective-permute-start.20
  144.2 6.7 %shard_map.327 = (f32[768,512]{1,0:T(8,128)S(1)}, f32[512,128]{1,0:T(8,128)S(1)}, f32[512,128]{1,0:T(8,128)S(1)}, f32[128,512]{1,0:T(8,128)S(1)}, f32[128,512]{1...) custom-call(f32[768,640]{1,0:T(8,128)S(1)} %fusion.54.u_ref, ...), custom_call_target="tpu_custom_call" | custom-call | flops 1000 | bytes 1000 | tf_op jit(solution)/shard_map/pallas_call | solution.py:190
  150.9 4.6 %collective-permute-start.23 = (bf16[800,128]{1,0:T(8,128)(2,1)S(1)}, bf16[800,128]{1,0:T(8,128)(2,1)S(1)}, u32[]{:S(2)}, u32[]{:S(2)}) collective-permute-start(bf16[800,128]{1,0:T(8,128)(2,1)S(1)} %get-tuple-element.158), channel_id=1, source_target_pairs={{0,2},{2,4},{4,6},{1,3},{3,5},{5,7},{8,10},{10,12},{12,14},{9,11},... | collective-permute-start | bytes 614408 | tf_op jit(solution)/shard_map/ppermute | solution.py:69
  155.5 5.4 %collective-permute-start.24 = (bf16[800,128]{1,0:T(8,128)(2,1)S(1)}, bf16[800,128]{1,0:T(8,128)(2,1)S(1)}, u32[]{:S(2)}, u32[]{:S(2)}) collective-permute-start(bf16[800,128]{1,0:T(8,128)(2,1)S(1)} %get-tuple-element.158), channel_id=1, source_target_pairs={{0,4},{2,6},{1,5},{3,7},{8,12},{10,14},{9,13},{11,15},{16,20},{18,... | collective-permute-start | bytes 614408 | tf_op jit(solution)/shard_map/ppermute | solution.py:69
  165.3 3.2 collective-permute-done.24.refs_1_
  168.4 2.2 collective-permute-done.25.refs_2_
  171.7 2.4 shard_map.328
  177.6 2.0 slice_reduce_fusion.1
  181.8 4.9 %fusion.2 = f32[512,2048]{1,0:T(8,128)S(1)} fusion(bf16[512,1024]{1,0:T(8,128)(2,1)} %multiply_convert_fusion.3.n2_ref, bf16[1024,3072]{1,0:T(8,128)(2,1)} %all-gather.2.cloned.1.call-done), kind=kOutput, calls=%fused_computation.2 | convolution fusion | flops 2147483648 | bytes 9437184 | tf_op jit(solution)/shard_map/dot_general | solution.py:27
  188.8 4.9 %fusion.51 = (bf16[512,1024]{1,0:T(8,128)(2,1)}, f32[512,1024]{1,0:T(8,128)}) fusion(bf16[512,1024]{1,0:T(8,128)(2,1)S(1)} %multiply_convert_fusion.2.m_ref, bf16[1024,3072]{1,0:T(8,128)(2,1)} %all-gather.2.cloned.1.call-done), kind=kOutput, calls=%fused_computation.196 | convolution fusion | flops 1074266112 | bytes 6291456 | tf_op jit(solution)/shard_map/dot_general | solution.py:27
  196.7 3.8 multiply_reduce_fusion
  200.5 2.1 fusion.44
  203.9 3.7 multiply_convert_fusion.1
  207.8 4.1 fusion.52
  211.9 4.4 %shard_map.335 = bf16[1024,3072]{1,0:T(8,128)(2,1)S(1)} custom-call(bf16[512,1024]{1,0:T(8,128)(2,1)S(1)} %copy-done.28, bf16[512,1024]{1,0:T(8,128)(2,1)S(1)} %get-tuple-element.286.e_ref, bf16[512,2048]{1,0:T(8,128)(2,1)S(1)} %pad_maximum_fusion.1.ggu_ref, bf16[512,1024]{1,0:T(8,128)(2,1)S(1)} %copy-done.27), custom_call_target="tpu_custom_call" | custom-call | flops 1000 | bytes 1000 | tf_op jit(solution)/shard_map/pallas_call | solution.py:963
  216.3 2.6 copy-done.4
  219.2 2.8 collective-permute-done.29.low_ref
  225.9 2.6 shard_map.329
  234.8 3.2 shard_map.330
  250.0 13.7 %shard_map.331 = (bf16[256,512]{1,0:T(8,128)(2,1)S(1)}, bf16[128,512]{1,0:T(8,128)(2,1)S(1)}, bf16[128,512]{1,0:T(8,128)(2,1)S(1)}, bf16[128,512]{1,0:T(8,128)(2,1)S(1)}, bf16[128,512]{1,0:T(8,128)(2,1)S(1)}) custom-call(bf16[256,512]{1,0:T(8,128)(2,1)S(1)} %copy-done.52, s32[8,512]{1,0:T(8,128)S(1)} %copy-done.79, bf16[256,512]{1,0:T(8,128)(2,1)S(1)} %copy-done.77, ...), custom_call_target="tpu_custom_call" | custom-call | flops 1000 | bytes 1000 | tf_op jit(solution)/shard_map/pallas_call | solution.py:190
  263.7 3.9 collective-permute-done.34
  282.9 13.5 %shard_map.332 = (f32[768,512]{1,0:T(8,128)S(1)}, f32[256,512]{1,0:T(8,128)S(1)}, f32[16,512]{1,0:T(8,128)S(1)}, f32[8,128]{1,0:T(8,128)S(1)}) custom-call(f32[768,512]{1,0:T(8,128)S(1)} %copy-done.37, f32[768,512]{1,0:T(8,128)S(1)} %copy-done.19, f32[512,128]{1,0:T(8,128)S(1)} %copy-done.43, f32[512,128]{1,0:T(8,128)S(1)} %copy-done.45, ...), custom_call_target="tpu_custom_call" | custom-call | flops 1000 | bytes 1000 | tf_op jit(solution)/shard_map/pallas_call | solution.py:190
  296.5 4.0 shard_map.333
  305.7 8.1 %shard_map.334 = (f32[1024,512]{1,0:T(8,128)S(1)}, f32[8,1024]{1,0:T(8,128)S(1)}, f32[768,128]{1,0:T(8,128)S(1)}, f32[256,128]{1,0:T(8,128)S(1)}) custom-call(f32[768,640]{1,0:T(8,128)S(1)} %copy-done.15, f32[768,640]{1,0:T(8,128)S(1)} %copy-done.1, f32[768,512]{1,0:T(8,128)S(1)} %get-tuple-element.197.gxs_ref, f32[256,512]{1,0:T(8,128)S(1)} %get-tuple-element.198.gbc_ref, ...), custom_call_target="tpu_custom_call" | custom-call | flops 1000 | bytes 1000 | tf_op jit(solution)/shard_map/pallas_call | solution.py:190
  322.6 2.3 fusion.19
  324.9 4.7 %collective-permute-done.39.behind_ref = f32[8,1024]{1,0:T(8,128)S(1)} collective-permute-done((f32[8,1024]{1,0:T(8,128)S(1)}, f32[8,1024]{1,0:T(8,128)S(1)}, u32[]{:S(2)}, u32[]{:S(2)}) %collective-permute-start.39) | collective-permute-done | bytes 32800 | tf_op jit(solution)/shard_map/ppermute | solution.py:69
  343.7 5.3 %shard_map.337 = (bf16[1024,1152]{1,0:T(8,128)(2,1)}, f32[1024,512]{1,0:T(8,128)S(1)}, bf16[1024,512]{1,0:T(8,128)(2,1)S(1)}, f32[1024,128]{1,0:T(8,128)}) custom-call(bf16[1024,640]{1,0:T(8,128)(2,1)S(1)} %copy-done.23, bf16[1024,640]{1,0:T(8,128)(2,1)S(1)} %copy-done.25, f32[8,640]{1,0:T(8,128)S(1)} %copy-done.87, bf16[1152,512]{1,0:T(8,128)(2,1)S(1)} %shard_map.336.g_ref, ...), custom_call_target="tpu_custom_call" | custom-call | flops 1000 | bytes 1000 | tf_op jit(solution)/shard_map/pallas_call | solution.py:820
  352.9 9.0 %collective-permute-done.46 = bf16[2,4,64,512]{3,2,1,0:T(8,128)(2,1)S(1)} collective-permute-done((bf16[2,4,64,512]{3,2,1,0:T(8,128)(2,1)S(1)}, bf16[2,4,64,512]{3,2,1,0:T(8,128)(2,1)S(1)}, u32[]{:S(2)}, u32[]{:S(2)}) %collective-permute-start.46) | collective-permute-done | bytes 524320 | tf_op jit(solution)/shard_map/ppermute | solution.py:63
  362.1 3.2 collective-permute-done.47
  367.1 2.5 shard_map.338
  375.5 3.3 collective-permute-start.51
  381.3 16.7 %collective-permute-done.51 = bf16[2,64,2176]{2,1,0:T(8,128)(2,1)S(1)} collective-permute-done((bf16[2,64,2176]{2,1,0:T(8,128)(2,1)S(1)}, bf16[2,64,2176]{2,1,0:T(8,128)(2,1)S(1)}, u32[]{:S(2)}, u32[]{:S(2)}) %collective-permute-start.51) | collective-permute-done | bytes 557088 | tf_op jit(solution)/shard_map/ppermute | solution.py:162
  398.2 3.6 collective-permute-start.54
  402.7 2.9 collective-permute-start.56
  406.1 8.0 %collective-permute-done.53 = bf16[64,1152]{1,0:T(8,128)(2,1)S(1)} collective-permute-done((bf16[64,1152]{1,0:T(8,128)(2,1)S(1)}, bf16[64,1152]{1,0:T(8,128)(2,1)S(1)}, u32[]{:S(2)}, u32[]{:S(2)}) %collective-permute-start.53) | collective-permute-done | bytes 147488 | tf_op jit(solution)/shard_map/ppermute | solution.py:63
  (530 shorter events, 151.7 us)
Async XLA Ops:
  7.2 174.6 %all-gather.2.cloned.1.call-start = ((), (), s32[]{:S(2)}) async-start(), calls=%async_computation.2 | async-start | bytes 6684672 | tf_op jit(solution)/shard_map/all_gather | solution.py:1067
  14.0 15.7 %collective-permute-start = (bf16[64,768]{1,0:T(8,128)(2,1)S(1)}, bf16[64,768]{1,0:T(8,128)(2,1)S(1)}, u32[]{:S(2)}, u32[]{:S(2)}) collective-permute-start(bf16[64,768]{1,0:T(8,128)(2,1)S(1)} %shard_map.322), channel_id=1, source_target_pairs={{0,6},{2,0},{4,2},{6,4},{1,7},{3,1},{5,3},{7,5},{8,14},{10,8},{12,... | collective-permute-start | bytes 294920 | tf_op jit(solution)/shard_map/ppermute | solution.py:63
  19.1 10.6 %collective-permute-start.1 = (bf16[64,768]{1,0:T(8,128)(2,1)S(1)}, bf16[64,768]{1,0:T(8,128)(2,1)S(1)}, u32[]{:S(2)}, u32[]{:S(2)}) collective-permute-start(bf16[64,768]{1,0:T(8,128)(2,1)S(1)} %shard_map.322), channel_id=1, source_target_pairs={{0,4},{2,6},{4,0},{6,2},{1,5},{3,7},{5,1},{7,3},{8,12},{10,14},{12... | collective-permute-start | bytes 294920 | tf_op jit(solution)/shard_map/ppermute | solution.py:63
  19.1 10.7 %collective-permute-start.2 = (bf16[64,768]{1,0:T(8,128)(2,1)S(1)}, bf16[64,768]{1,0:T(8,128)(2,1)S(1)}, u32[]{:S(2)}, u32[]{:S(2)}) collective-permute-start(bf16[64,768]{1,0:T(8,128)(2,1)S(1)} %shard_map.322), channel_id=1, source_target_pairs={{0,2},{2,4},{4,6},{6,0},{1,3},{3,5},{5,7},{7,1},{8,10},{10,12},{12... | collective-permute-start | bytes 294920 | tf_op jit(solution)/shard_map/ppermute | solution.py:63
  20.8 12.5 %collective-permute-start.9 = (bf16[16,1024]{1,0:T(8,128)(2,1)S(1)}, bf16[16,1024]{1,0:T(8,128)(2,1)S(1)}, u32[]{:S(2)}, u32[]{:S(2)}) collective-permute-start(bf16[16,1024]{1,0:T(8,128)(2,1)S(1)} %slice_bitcast_fusion.4), channel_id=1, source_target_pairs={{0,2},{2,4},{4,6},{1,3},{3,5},{5,7},{8,10},{10,12},{12,14},{9,11},... | collective-permute-start | bytes 98312 | tf_op jit(solution)/shard_map/ppermute | solution.py:69
  27.9 292.0 %reduce-scatter.3.cloned.1.call-start = ((), (), s32[]{:S(2)}) async-start(), calls=%async_computation.3 | async-start | bytes 7864320 | tf_op jit(solution)/shard_map/reduce_scatter | solution.py:1136
  30.7 8.8 %collective-permute-start.10 = (bf16[4,64,384]{2,1,0:T(8,128)(2,1)}, bf16[4,64,384]{2,1,0:T(8,128)(2,1)}, u32[]{:S(2)}, u32[]{:S(2)}) collective-permute-start(bf16[4,64,384]{2,1,0:T(8,128)(2,1)} %get-tuple-element.325), channel_id=1, source_target_pairs={{0,16},{8,24},{16,0},{24,8},{1,17},{9,25},{17,1},{25,9},{2,18},{10... | collective-permute-start | bytes 589832 | tf_op jit(solution)/shard_map/ppermute | solution.py:63
  34.0 9.8 %collective-permute-start.12 = (bf16[4,64,384]{2,1,0:T(8,128)(2,1)}, bf16[4,64,384]{2,1,0:T(8,128)(2,1)S(1)}, u32[]{:S(2)}, u32[]{:S(2)}) collective-permute-start(bf16[4,64,384]{2,1,0:T(8,128)(2,1)} %get-tuple-element.324), channel_id=1, source_target_pairs={{0,8},{8,0},{16,24},{24,16},{1,9},{9,1},{17,25},{25,17},{2,10},{10... | collective-permute-start | bytes 589832 | tf_op jit(solution)/shard_map/ppermute | solution.py:63
  38.7 20.0 %collective-permute-start.4 = (bf16[2,64,768]{2,1,0:T(8,128)(2,1)}, bf16[2,64,768]{2,1,0:T(8,128)(2,1)}, u32[]{:S(2)}, u32[]{:S(2)}) collective-permute-start(bf16[2,64,768]{2,1,0:T(8,128)(2,1)} %maximum_select_fusion.18), channel_id=1, source_target_pairs={{0,4},{2,6},{4,0},{6,2},{1,5},{3,7},{5,1},{7,3},{8,12},{10,14},{12... | collective-permute-start | bytes 589832 | tf_op jit(solution)/shard_map/ppermute | solution.py:102
  40.7 10.5 %collective-permute-start.11 = (bf16[2,4,64,384]{3,2,1,0:T(8,128)(2,1)S(1)}, bf16[2,4,64,384]{3,2,1,0:T(8,128)(2,1)S(1)}, u32[]{:S(2)}, u32[]{:S(2)}) collective-permute-start(bf16[2,4,64,384]{3,2,1,0:T(8,128)(2,1)S(1)} %maximum_select_fusion.15), channel_id=1, source_target_pairs={{0,8},{8,0},{16,24},{24,16},{1,9},{9,1},{17,25},{25,17},{2,10},{10... | collective-permute-start | bytes 1179656 | tf_op jit(solution)/shard_map/ppermute | solution.py:63
  56.6 11.8 %collective-permute-start.17 = (bf16[1,64,1792]{2,1,0:T(8,128)(2,1)}, bf16[1,64,1792]{2,1,0:T(8,128)(2,1)}, u32[]{:S(2)}, u32[]{:S(2)}) collective-permute-start(bf16[1,64,1792]{2,1,0:T(8,128)(2,1)} %bitcast.48), channel_id=1, source_target_pairs={{0,2},{2,0},{4,6},{6,4},{1,3},{3,1},{5,7},{7,5},{8,10},{10,8},{12,... | collective-permute-start | bytes 688136 | tf_op jit(solution)/shard_map/ppermute | solution.py:102
  69.8 29.7 %collective-permute-start.18 = (bf16[2,64,1792]{2,1,0:T(8,128)(2,1)S(1)}, bf16[2,64,1792]{2,1,0:T(8,128)(2,1)S(1)}, u32[]{:S(2)}, u32[]{:S(2)}) collective-permute-start(bf16[2,64,1792]{2,1,0:T(8,128)(2,1)S(1)} %maximum_select_fusion.10), channel_id=1, source_target_pairs={{0,4},{2,6},{4,0},{6,2},{1,5},{3,7},{5,1},{7,3},{8,12},{10,14},{12... | collective-permute-start | bytes 1376264 | tf_op jit(solution)/shard_map/ppermute | solution.py:102
  71.4 30.2 %collective-permute-start.5 = (bf16[4,64,384]{2,1,0:T(8,128)(2,1)S(1)}, bf16[4,64,384]{2,1,0:T(8,128)(2,1)S(1)}, u32[]{:S(2)}, u32[]{:S(2)}) collective-permute-start(bf16[4,64,384]{2,1,0:T(8,128)(2,1)S(1)} %get-tuple-element.319), channel_id=1, source_target_pairs={{0,16},{8,24},{16,0},{24,8},{1,17},{9,25},{17,1},{25,9},{2,18},{10... | collective-permute-start | bytes 589832 | tf_op jit(solution)/shard_map/ppermute | solution.py:63
  77.6 46.2 %collective-permute-start.8 = (bf16[2,4,64,384]{3,2,1,0:T(8,128)(2,1)S(1)}, bf16[2,4,64,384]{3,2,1,0:T(8,128)(2,1)S(1)}, u32[]{:S(2)}, u32[]{:S(2)}) collective-permute-start(bf16[2,4,64,384]{3,2,1,0:T(8,128)(2,1)S(1)} %maximum_select_fusion.14), channel_id=1, source_target_pairs={{0,16},{8,24},{16,0},{24,8},{1,17},{9,25},{17,1},{25,9},{2,18},{10... | collective-permute-start | bytes 1179656 | tf_op jit(solution)/shard_map/ppermute | solution.py:63
  78.9 23.3 %collective-permute-start.14 = (bf16[128,512]{1,0:T(8,128)(2,1)S(1)}, bf16[128,512]{1,0:T(8,128)(2,1)S(1)}, u32[]{:S(2)}, u32[]{:S(2)}) collective-permute-start(bf16[128,512]{1,0:T(8,128)(2,1)S(1)} %copy-done.61), channel_id=1, source_target_pairs={{0,2},{2,4},{4,6},{1,3},{3,5},{5,7},{8,10},{10,12},{12,14},{9,11},... | collective-permute-start | bytes 393224 | tf_op jit(solution)/shard_map/ppermute | solution.py:69
  82.5 27.1 %collective-permute-start.15 = (bf16[128,512]{1,0:T(8,128)(2,1)S(1)}, bf16[128,512]{1,0:T(8,128)(2,1)S(1)}, u32[]{:S(2)}, u32[]{:S(2)}) collective-permute-start(bf16[128,512]{1,0:T(8,128)(2,1)S(1)} %copy-done.61), channel_id=1, source_target_pairs={{0,4},{2,6},{1,5},{3,7},{8,12},{10,14},{9,13},{11,15},{16,20},{18,... | collective-permute-start | bytes 393224 | tf_op jit(solution)/shard_map/ppermute | solution.py:69
  100.0 23.9 %collective-permute-start.21 = (bf16[4,64,896]{2,1,0:T(8,128)(2,1)S(1)}, bf16[4,64,896]{2,1,0:T(8,128)(2,1)S(1)}, u32[]{:S(2)}, u32[]{:S(2)}) collective-permute-start(bf16[4,64,896]{2,1,0:T(8,128)(2,1)S(1)} %get-tuple-element.301), channel_id=1, source_target_pairs={{0,8},{8,0},{16,24},{24,16},{1,9},{9,1},{17,25},{25,17},{2,10},{10... | collective-permute-start | bytes 1376264 | tf_op jit(solution)/shard_map/ppermute | solution.py:63
  101.6 36.1 %collective-permute-start.6 = (bf16[2,4,64,384]{3,2,1,0:T(8,128)(2,1)S(1)}, bf16[2,4,64,384]{3,2,1,0:T(8,128)(2,1)S(1)}, u32[]{:S(2)}, u32[]{:S(2)}) collective-permute-start(bf16[2,4,64,384]{3,2,1,0:T(8,128)(2,1)S(1)} %maximum_select_fusion.13), channel_id=1, source_target_pairs={{0,8},{8,0},{16,24},{24,16},{1,9},{9,1},{17,25},{25,17},{2,10},{10... | collective-permute-start | bytes 1179656 | tf_op jit(solution)/shard_map/ppermute | solution.py:63
  102.2 12.6 %collective-permute-start.16 = (bf16[128,512]{1,0:T(8,128)(2,1)S(1)}, bf16[128,512]{1,0:T(8,128)(2,1)S(1)}, u32[]{:S(2)}, u32[]{:S(2)}) collective-permute-start(bf16[128,512]{1,0:T(8,128)(2,1)S(1)} %copy-done.61), channel_id=1, source_target_pairs={{0,6},{1,7},{8,14},{9,15},{16,22},{17,23},{24,30},{25,31}} | collective-permute-start | bytes 393224 | tf_op jit(solution)/shard_map/ppermute | solution.py:69
  109.7 28.2 %collective-permute-start.19 = (bf16[4,64,896]{2,1,0:T(8,128)(2,1)S(1)}, bf16[4,64,896]{2,1,0:T(8,128)(2,1)S(1)}, u32[]{:S(2)}, u32[]{:S(2)}) collective-permute-start(bf16[4,64,896]{2,1,0:T(8,128)(2,1)S(1)} %get-tuple-element.302), channel_id=1, source_target_pairs={{0,16},{8,24},{16,0},{24,8},{1,17},{9,25},{17,1},{25,9},{2,18},{10... | collective-permute-start | bytes 1376264 | tf_op jit(solution)/shard_map/ppermute | solution.py:63
  124.2 38.9 %collective-permute-start.22 = (bf16[2,4,64,896]{3,2,1,0:T(8,128)(2,1)S(1)}, bf16[2,4,64,896]{3,2,1,0:T(8,128)(2,1)S(1)}, u32[]{:S(2)}, u32[]{:S(2)}) collective-permute-start(bf16[2,4,64,896]{3,2,1,0:T(8,128)(2,1)S(1)} %maximum_select_fusion.5), channel_id=1, source_target_pairs={{0,16},{8,24},{16,0},{24,8},{1,17},{9,25},{17,1},{25,9},{2,18},{10... | collective-permute-start | bytes 2752520 | tf_op jit(solution)/shard_map/ppermute | solution.py:63
  138.1 25.4 %collective-permute-start.20 = (bf16[2,4,64,896]{3,2,1,0:T(8,128)(2,1)S(1)}, bf16[2,4,64,896]{3,2,1,0:T(8,128)(2,1)S(1)}, u32[]{:S(2)}, u32[]{:S(2)}) collective-permute-start(bf16[2,4,64,896]{3,2,1,0:T(8,128)(2,1)S(1)} %maximum_select_fusion.3), channel_id=1, source_target_pairs={{0,8},{8,0},{16,24},{24,16},{1,9},{9,1},{17,25},{25,17},{2,10},{10... | collective-permute-start | bytes 2752520 | tf_op jit(solution)/shard_map/ppermute | solution.py:63
  150.9 14.3 %collective-permute-start.23 = (bf16[800,128]{1,0:T(8,128)(2,1)S(1)}, bf16[800,128]{1,0:T(8,128)(2,1)S(1)}, u32[]{:S(2)}, u32[]{:S(2)}) collective-permute-start(bf16[800,128]{1,0:T(8,128)(2,1)S(1)} %get-tuple-element.158), channel_id=1, source_target_pairs={{0,2},{2,4},{4,6},{1,3},{3,5},{5,7},{8,10},{10,12},{12,14},{9,11},... | collective-permute-start | bytes 614408 | tf_op jit(solution)/shard_map/ppermute | solution.py:69
  155.5 12.9 %collective-permute-start.24 = (bf16[800,128]{1,0:T(8,128)(2,1)S(1)}, bf16[800,128]{1,0:T(8,128)(2,1)S(1)}, u32[]{:S(2)}, u32[]{:S(2)}) collective-permute-start(bf16[800,128]{1,0:T(8,128)(2,1)S(1)} %get-tuple-element.158), channel_id=1, source_target_pairs={{0,4},{2,6},{1,5},{3,7},{8,12},{10,14},{9,13},{11,15},{16,20},{18,... | collective-permute-start | bytes 614408 | tf_op jit(solution)/shard_map/ppermute | solution.py:69
  161.0 9.7 %collective-permute-start.25 = (bf16[800,128]{1,0:T(8,128)(2,1)S(1)}, bf16[800,128]{1,0:T(8,128)(2,1)S(1)}, u32[]{:S(2)}, u32[]{:S(2)}) collective-permute-start(bf16[800,128]{1,0:T(8,128)(2,1)S(1)} %get-tuple-element.158), channel_id=1, source_target_pairs={{0,6},{1,7},{8,14},{9,15},{16,22},{17,23},{24,30},{25,31}} | collective-permute-start | bytes 614408 | tf_op jit(solution)/shard_map/ppermute | solution.py:69
  218.9 150.7 %reduce-scatter.5.cloned.1.call-start = ((), (), s32[]{:S(2)}) async-start(), calls=%async_computation.4 | async-start | bytes 1966080 | tf_op jit(solution)/shard_map/reduce_scatter | solution.py:1166
  241.7 26.0 %collective-permute-start.34 = (bf16[2,4,64,512]{3,2,1,0:T(8,128)(2,1)}, bf16[2,4,64,512]{3,2,1,0:T(8,128)(2,1)}, u32[]{:S(2)}, u32[]{:S(2)}) collective-permute-start(bf16[2,4,64,512]{3,2,1,0:T(8,128)(2,1)} %dynamic-slice_bitcast_fusion.5), channel_id=1, source_target_pairs={{0,8},{8,0},{16,24},{24,16},{1,9},{9,1},{17,25},{25,17},{2,10},{10... | collective-permute-start | bytes 1572872 | tf_op jit(solution)/shard_map/ppermute | solution.py:63
  244.1 25.9 %collective-permute-start.35 = (bf16[2,4,64,512]{3,2,1,0:T(8,128)(2,1)}, bf16[2,4,64,512]{3,2,1,0:T(8,128)(2,1)}, u32[]{:S(2)}, u32[]{:S(2)}) collective-permute-start(bf16[2,4,64,512]{3,2,1,0:T(8,128)(2,1)} %dynamic-slice_bitcast_fusion.4), channel_id=1, source_target_pairs={{0,16},{8,24},{16,0},{24,8},{1,17},{9,25},{17,1},{25,9},{2,18},{10... | collective-permute-start | bytes 1572872 | tf_op jit(solution)/shard_map/ppermute | solution.py:63
  245.8 25.6 %collective-permute-start.31 = (bf16[800,128]{1,0:T(8,128)(2,1)S(1)}, bf16[800,128]{1,0:T(8,128)(2,1)S(1)}, u32[]{:S(2)}, u32[]{:S(2)}) collective-permute-start(bf16[800,128]{1,0:T(8,128)(2,1)S(1)} %get-tuple-element.170), channel_id=1, source_target_pairs={{2,0},{4,2},{6,4},{3,1},{5,3},{7,5},{10,8},{12,10},{14,12},{11,9},... | collective-permute-start | bytes 614408 | tf_op jit(solution)/shard_map/ppermute | solution.py:69
  247.1 25.4 %collective-permute-start.32 = (bf16[800,128]{1,0:T(8,128)(2,1)S(1)}, bf16[800,128]{1,0:T(8,128)(2,1)S(1)}, u32[]{:S(2)}, u32[]{:S(2)}) collective-permute-start(bf16[800,128]{1,0:T(8,128)(2,1)S(1)} %get-tuple-element.170), channel_id=1, source_target_pairs={{4,0},{6,2},{5,1},{7,3},{12,8},{14,10},{13,9},{15,11},{20,16},{22,... | collective-permute-start | bytes 614408 | tf_op jit(solution)/shard_map/ppermute | solution.py:69
  248.4 24.1 %collective-permute-start.33 = (bf16[800,128]{1,0:T(8,128)(2,1)S(1)}, bf16[800,128]{1,0:T(8,128)(2,1)S(1)}, u32[]{:S(2)}, u32[]{:S(2)}) collective-permute-start(bf16[800,128]{1,0:T(8,128)(2,1)S(1)} %get-tuple-element.170), channel_id=1, source_target_pairs={{6,0},{7,1},{14,8},{15,9},{22,16},{23,17},{30,24},{31,25}} | collective-permute-start | bytes 614408 | tf_op jit(solution)/shard_map/ppermute | solution.py:69
  272.4 24.0 %collective-permute-start.36 = (bf16[128,512]{1,0:T(8,128)(2,1)S(1)}, bf16[128,512]{1,0:T(8,128)(2,1)S(1)}, u32[]{:S(2)}, u32[]{:S(2)}) collective-permute-start(bf16[128,512]{1,0:T(8,128)(2,1)S(1)} %get-tuple-element.179), channel_id=1, source_target_pairs={{2,0},{4,2},{6,4},{3,1},{5,3},{7,5},{10,8},{12,10},{14,12},{11,9},... | collective-permute-start | bytes 393224 | tf_op jit(solution)/shard_map/ppermute | solution.py:69
  273.7 22.7 %collective-permute-start.37 = (bf16[128,512]{1,0:T(8,128)(2,1)S(1)}, bf16[128,512]{1,0:T(8,128)(2,1)S(1)}, u32[]{:S(2)}, u32[]{:S(2)}) collective-permute-start(bf16[128,512]{1,0:T(8,128)(2,1)S(1)} %get-tuple-element.180), channel_id=1, source_target_pairs={{4,0},{6,2},{5,1},{7,3},{12,8},{14,10},{13,9},{15,11},{20,16},{22,... | collective-permute-start | bytes 393224 | tf_op jit(solution)/shard_map/ppermute | solution.py:69
  275.0 21.4 %collective-permute-start.38 = (bf16[128,512]{1,0:T(8,128)(2,1)S(1)}, bf16[128,512]{1,0:T(8,128)(2,1)S(1)}, u32[]{:S(2)}, u32[]{:S(2)}) collective-permute-start(bf16[128,512]{1,0:T(8,128)(2,1)S(1)} %get-tuple-element.181), channel_id=1, source_target_pairs={{6,0},{7,1},{14,8},{15,9},{22,16},{23,17},{30,24},{31,25}} | collective-permute-start | bytes 393224 | tf_op jit(solution)/shard_map/ppermute | solution.py:69
  277.1 39.4 %collective-permute-start.42 = (bf16[4,64,512]{2,1,0:T(8,128)(2,1)}, bf16[4,64,512]{2,1,0:T(8,128)(2,1)}, u32[]{:S(2)}, u32[]{:S(2)}) collective-permute-start(bf16[4,64,512]{2,1,0:T(8,128)(2,1)} %dynamic-slice_bitcast_fusion.11), channel_id=1, source_target_pairs={{0,16},{8,24},{16,0},{24,8},{1,17},{9,25},{17,1},{25,9},{2,18},{10... | collective-permute-start | bytes 786440 | tf_op jit(solution)/shard_map/ppermute | solution.py:63
  278.5 39.7 %collective-permute-start.43 = (bf16[4,64,512]{2,1,0:T(8,128)(2,1)}, bf16[4,64,512]{2,1,0:T(8,128)(2,1)}, u32[]{:S(2)}, u32[]{:S(2)}) collective-permute-start(bf16[4,64,512]{2,1,0:T(8,128)(2,1)} %dynamic-slice_bitcast_fusion.10), channel_id=1, source_target_pairs={{0,8},{8,0},{16,24},{24,16},{1,9},{9,1},{17,25},{25,17},{2,10},{10... | collective-permute-start | bytes 786440 | tf_op jit(solution)/shard_map/ppermute | solution.py:63
  302.8 17.2 %collective-permute-start.40 = (bf16[2,4,64,512]{3,2,1,0:T(8,128)(2,1)}, bf16[2,4,64,512]{3,2,1,0:T(8,128)(2,1)}, u32[]{:S(2)}, u32[]{:S(2)}) collective-permute-start(bf16[2,4,64,512]{3,2,1,0:T(8,128)(2,1)} %dynamic-slice_bitcast_fusion.3), channel_id=1, source_target_pairs={{0,8},{8,0},{16,24},{24,16},{1,9},{9,1},{17,25},{25,17},{2,10},{10... | collective-permute-start | bytes 1572872 | tf_op jit(solution)/shard_map/ppermute | solution.py:63
  304.4 18.2 %collective-permute-start.41 = (bf16[2,4,64,640]{3,2,1,0:T(8,128)(2,1)}, bf16[2,4,64,640]{3,2,1,0:T(8,128)(2,1)}, u32[]{:S(2)}, u32[]{:S(2)}) collective-permute-start(bf16[2,4,64,640]{3,2,1,0:T(8,128)(2,1)} %dynamic-slice_bitcast_fusion.1), channel_id=1, source_target_pairs={{0,16},{8,24},{16,0},{24,8},{1,17},{9,25},{17,1},{25,9},{2,18},{10... | collective-permute-start | bytes 1966088 | tf_op jit(solution)/shard_map/ppermute | solution.py:63
  321.3 8.3 %collective-permute-start.39 = (f32[8,1024]{1,0:T(8,128)S(1)}, f32[8,1024]{1,0:T(8,128)S(1)}, u32[]{:S(2)}, u32[]{:S(2)}) collective-permute-start(f32[8,1024]{1,0:T(8,128)S(1)} %copy-done.109), channel_id=1, source_target_pairs={{2,0},{4,2},{6,4},{3,1},{5,3},{7,5},{10,8},{12,10},{14,12},{11,9},... | collective-permute-start | bytes 98312 | tf_op jit(solution)/shard_map/ppermute | solution.py:69
  331.0 18.0 %collective-permute-start.44 = (bf16[4,64,512]{2,1,0:T(8,128)(2,1)}, bf16[4,64,512]{2,1,0:T(8,128)(2,1)}, u32[]{:S(2)}, u32[]{:S(2)}) collective-permute-start(bf16[4,64,512]{2,1,0:T(8,128)(2,1)} %dynamic-slice_bitcast_fusion.9), channel_id=1, source_target_pairs={{0,16},{8,24},{16,0},{24,8},{1,17},{9,25},{17,1},{25,9},{2,18},{10... | collective-permute-start | bytes 786440 | tf_op jit(solution)/shard_map/ppermute | solution.py:63
  334.5 15.8 %collective-permute-start.45 = (bf16[4,64,640]{2,1,0:T(8,128)(2,1)S(1)}, bf16[4,64,640]{2,1,0:T(8,128)(2,1)S(1)}, u32[]{:S(2)}, u32[]{:S(2)}) collective-permute-start(bf16[4,64,640]{2,1,0:T(8,128)(2,1)S(1)} %dynamic-slice_bitcast_fusion.7), channel_id=1, source_target_pairs={{0,8},{8,0},{16,24},{24,16},{1,9},{9,1},{17,25},{25,17},{2,10},{10... | collective-permute-start | bytes 983048 | tf_op jit(solution)/shard_map/ppermute | solution.py:63
  351.9 10.0 %collective-permute-start.46 = (bf16[2,4,64,512]{3,2,1,0:T(8,128)(2,1)S(1)}, bf16[2,4,64,512]{3,2,1,0:T(8,128)(2,1)S(1)}, u32[]{:S(2)}, u32[]{:S(2)}) collective-permute-start(bf16[2,4,64,512]{3,2,1,0:T(8,128)(2,1)S(1)} %dynamic-slice_bitcast_fusion.2), channel_id=1, source_target_pairs={{0,8},{8,0},{16,24},{24,16},{1,9},{9,1},{17,25},{25,17},{2,10},{10... | collective-permute-start | bytes 1572872 | tf_op jit(solution)/shard_map/ppermute | solution.py:63
  352.3 13.0 %collective-permute-start.47 = (bf16[2,4,64,640]{3,2,1,0:T(8,128)(2,1)S(1)}, bf16[2,4,64,640]{3,2,1,0:T(8,128)(2,1)S(1)}, u32[]{:S(2)}, u32[]{:S(2)}) collective-permute-start(bf16[2,4,64,640]{3,2,1,0:T(8,128)(2,1)S(1)} %dynamic-slice_bitcast_fusion), channel_id=1, source_target_pairs={{0,16},{8,24},{16,0},{24,8},{1,17},{9,25},{17,1},{25,9},{2,18},{10... | collective-permute-start | bytes 1966088 | tf_op jit(solution)/shard_map/ppermute | solution.py:63
  352.7 13.3 %collective-permute-start.48 = (bf16[1024,512]{1,0:T(8,128)(2,1)S(1)}, bf16[1024,512]{1,0:T(8,128)(2,1)S(1)}, u32[]{:S(2)}, u32[]{:S(2)}) collective-permute-start(bf16[1024,512]{1,0:T(8,128)(2,1)S(1)} %get-tuple-element.222), channel_id=1, source_target_pairs={{0,1},{1,0},{2,3},{3,2},{4,5},{5,4},{6,7},{7,6},{8,9},{9,8},{10,11... | collective-permute-start | bytes 3145736 | tf_op jit(solution)/shard_map/ppermute | solution.py:73
  375.5 22.5 %collective-permute-start.51 = (bf16[2,64,2176]{2,1,0:T(8,128)(2,1)S(1)}, bf16[2,64,2176]{2,1,0:T(8,128)(2,1)S(1)}, u32[]{:S(2)}, u32[]{:S(2)}) collective-permute-start(bf16[2,64,2176]{2,1,0:T(8,128)(2,1)S(1)} %broadcast_select_fusion), channel_id=1, source_target_pairs={{0,4},{2,6},{4,0},{6,2},{1,5},{3,7},{5,1},{7,3},{8,12},{10,14},{12... | collective-permute-start | bytes 1671176 | tf_op jit(solution)/shard_map/ppermute | solution.py:162
  401.8 12.3 %collective-permute-start.53 = (bf16[64,1152]{1,0:T(8,128)(2,1)S(1)}, bf16[64,1152]{1,0:T(8,128)(2,1)S(1)}, u32[]{:S(2)}, u32[]{:S(2)}) collective-permute-start(bf16[64,1152]{1,0:T(8,128)(2,1)S(1)} %get-tuple-element.307), channel_id=1, source_target_pairs={{0,4},{2,6},{4,0},{6,2},{1,5},{3,7},{5,1},{7,3},{8,12},{10,14},{12... | collective-permute-start | bytes 442376 | tf_op jit(solution)/shard_map/ppermute | solution.py:63
  401.8 12.3 %collective-permute-start.52 = (bf16[64,1152]{1,0:T(8,128)(2,1)S(1)}, bf16[64,1152]{1,0:T(8,128)(2,1)S(1)}, u32[]{:S(2)}, u32[]{:S(2)}) collective-permute-start(bf16[64,1152]{1,0:T(8,128)(2,1)S(1)} %get-tuple-element.305), channel_id=1, source_target_pairs={{0,2},{2,4},{4,6},{6,0},{1,3},{3,5},{5,7},{7,1},{8,10},{10,12},{12... | collective-permute-start | bytes 442376 | tf_op jit(solution)/shard_map/ppermute | solution.py:63
  402.7 14.6 %collective-permute-start.56 = (bf16[1,64,2176]{2,1,0:T(8,128)(2,1)S(1)}, bf16[1,64,2176]{2,1,0:T(8,128)(2,1)S(1)}, u32[]{:S(2)}, u32[]{:S(2)}) collective-permute-start(bf16[1,64,2176]{2,1,0:T(8,128)(2,1)S(1)} %broadcast_select_fusion.1), channel_id=1, source_target_pairs={{0,2},{2,0},{4,6},{6,4},{1,3},{3,1},{5,7},{7,5},{8,10},{10,8},{12,... | collective-permute-start | bytes 835592 | tf_op jit(solution)/shard_map/ppermute | solution.py:162
  (155 other events, 1203.7 us)
Sparse Core Ops, SparseCore 0:
  28.1 138.2 all-gather.1
  219.1 87.3 reduce-scatter.2
  320.0 41.4 reduce-scatter.4
where the time goes:
time: 435 us; the launch traced here: 427 us
  waiting for transfers between devices  116 us (27%)
  starting transfers between devices  88.5 us (20%)
  Pallas kernels  77.6 us (18%)
  local copies, waits for them, and re-layouts  60.1 us (14%)
  other arithmetic  42.1 us (10%)
  matrix products  25.4 us (6%)
  between operations  17.9 us (4%)
    pallas_call x15, Pallas kernels, call(): pl.pallas_call(body, out_shape=[jax.ShapeDtypeStruct(s, d) for s, d in ou...  63.9 us
    ppermute x30, waiting for transfers between devices, shifted(): return lax.ppermute(value, axis, pairs)  54 us
    ppermute x14, starting transfers between devices, passed_along(): return lax.ppermute(value, axis, pairs)  40.6 us
    unnamed x302, local copies, waits for them, and re-layouts  40.2 us
    ppermute x30, starting transfers between devices, shifted(): return lax.ppermute(value, axis, pairs)  37.7 us
    dot_general x10, matrix products, dot(): lax.dot_general(left, right, (((left_dim,), (right_dim,)), ((), ())), pre...  25.4 us
    ppermute x4, waiting for transfers between devices, gathered_line(): other = lax.ppermute(value, zdim[0], [(i, i ^ step) for i in range(size)])  22.6 us
    ppermute x2, waiting for transfers between devices, exchanged(): lax.ppermute(sent, zdim[0], [(i, i ^ step) for i in range(zdim[1])])  16.9 us
  transfers between devices with their start and end apart: 60, of which 29 were waited for; matrix products, arithmetic and copies ran while one was open for 13% of the time, Pallas kernels for 17%

commit v1 on v0

--- a/solution.py
+++ b/solution.py
@@ -106,15 +106,22 @@
     return value
 
 
-def gathered_plane(line):
+def plane_first(line):
     ydim, xdim, _ = factors()
-    columns = line.shape[-1]
-    half = columns // 256 * 128
-    one = gathered_along(line[..., :half], ydim)
-    two = gathered_along(line[..., half:], xdim)
+    half = line.shape[-1] // 256 * 128
+    return gathered_along(line[..., :half], ydim), gathered_along(line[..., half:], xdim)
+
+
+def plane_second(one, two):
+    ydim, xdim, _ = factors()
     one = jnp.swapaxes(gathered_along(one, xdim), 0, 1)
     two = gathered_along(two, ydim)
-    return jnp.concatenate([one, two], axis=-1).reshape(-1, columns)
+    whole = jnp.concatenate([one, two], axis=-1)
+    return whole.reshape(-1, whole.shape[-1])
+
+
+def gathered_plane(line):
+    return plane_second(*plane_first(line))
 
 
 def in_pair(value, kept):
@@ -186,7 +193,12 @@
     return total
 
 
+COSTS = {"prep_body": 1, "params_body": 1, "rope_body": 1, "attend_body": 9, "attend_back_body": 14, "conv_body": 7, "mix_body": 3,
+    "gate_body": 3, "mix_back_body": 13, "conv_back_body": 8, "residual_body": 2, "input_body": 2}
+
+
 def call(body, outs, scratch, *args):
+    name = getattr(body, "func", body).__name__
     return pl.pallas_call(
         body,
         out_shape=[jax.ShapeDtypeStruct(s, d) for s, d in outs],
@@ -194,7 +206,7 @@
         out_specs=[pl.BlockSpec(memory_space=pltpu.VMEM)] * len(outs),
         scratch_shapes=[pltpu.VMEM(s, d) for s, d in scratch],
         compiler_params=pltpu.CompilerParams(vmem_limit_bytes=VMEM_LIMIT),
-        cost_estimate=pl.CostEstimate(flops=1000, bytes_accessed=1000, transcendentals=0),
+        cost_estimate=pl.CostEstimate(flops=COSTS.get(name, 1) * 10**9, bytes_accessed=1000, transcendentals=0),
     )(*args)
 
 
@@ -861,7 +873,7 @@
     columns = grad.shape[0]
     made = dot(n1_ref[:, HALO:], grad, 1, 1)
     gw_ref[:, : columns - 128] = made[:, : columns - 128].astype(bf16)
-    total = gn_ref[...] + dot(u_ref[...], grad[:width], 1, 0) + dot(first_ref[:, rest_at:], grad[width:], 1, 0)
+    total = gn_ref[...] + dot(u_ref[:, width:], grad[:width], 1, 0) + dot(first_ref[:, rest_at:], grad[width:], 1, 0)
     total_ref[...] = total
     low_ref[...] = total.astype(bf16)
     scaled = xt_ref[:, HALO:].astype(f32) * scale_ref[0:1, HALO:]
@@ -1055,14 +1067,14 @@
         valid_mask,
     )
     mlp_shard = jnp.concatenate([w_gateup.reshape(rows, 2 * ff_local), w_down.T], axis=1)
-    u_shard = w_gatein[:, 1]
-    last_shard = jnp.concatenate([w_gatein[:, 0], jnp.concatenate([w_out_attn, w_out_ssm], axis=0).T], axis=1)
+    mixer_shard = w_gatein.reshape(rows, 2 * width)
+    out_shard = jnp.concatenate([w_out_attn, w_out_ssm], axis=0).T
 
     flat_in = hidden.reshape(length, MODEL_WIDTH)
     first_line = gathered_line(first_shard, False)
     before = passed_along(flat_in[length - 16 :], "ctx", 1)
-    u_shard, first_line = tied(u_shard, first_line)
-    u_line = gathered_line(u_shard)
+    mixer_shard, first_line = tied(mixer_shard, first_line)
+    mixer_line = gathered_line(mixer_shard)
     first_w = gathered_plane(first_line)
     mlp_w = lax.all_gather(mlp_shard, ("fsdp", "ctx"), axis=0, tiled=True)
 
@@ -1086,23 +1098,25 @@
 
     first_lin = dot(first_w, n1, 0, 0)
     query, kv_own = roped(attn_width, first_lin, cosine, sine)
-    last_shard, kv_own = tied(last_shard, kv_own)
-    last_line = gathered_line(last_shard)
+    mixer_line, kv_own = tied(mixer_line, kv_own)
     kv = [kv_own] + [passed_along(kv_own, "ctx", s) for s in range(1, blocks)]
-    u_w = gathered_plane(u_line)
+    one, two = plane_first(mixer_line)
+    one, two, out_shard, *kv = tied(one, two, out_shard, *kv)
+    mixer_w = plane_second(one, two)
+    out_line = gathered_line(out_shard)
     attn, log_total = attend(query, low_rows, kv)
-    u_w, attn = tied(u_w, attn)
-    u_in = dot(u_w, n1, 0, 0)
+    mixer_w, attn, out_line = tied(mixer_w, attn, out_line)
+    out_halves = plane_first(out_line)
+    mixer_lin = dot(mixer_w, n1, 0, 0)
+    gate_z, u_in = mixer_lin[:width, HALO:], mixer_lin[width:]
 
     xs, b_flat, c_flat, b_side, c_side, dt, cum, cumt, pack = conv_forward(
         heads, qkv_width, u_in, first_lin, par_inner, par_basis, hp, place_rows
     )
     packs = [passed_along(pack, "ctx", s) for s in range(1, blocks)]
-    last_w = gathered_plane(last_line)
-    last_w, packs = tied(last_w, packs)
-    z_w, out_w = last_w[:, :width], last_w[:, width:]
+    xs, *out_halves = tied(xs, *out_halves)
+    out_w = plane_second(*out_halves)
     gateup_w, down_w = mlp_w[:, : 2 * ff_local], mlp_w[:, 2 * ff_local :]
-    gate_z = dot(z_w, n1[:, HALO:], 0, 0)
     ssm, states, squares = mix_forward(heads, xs, b_flat, c_side, dt, cum, cumt, hp, place_rows, gate_z, packs)
     inv_ssm = lax.rsqrt((squares + swapped(squares)) / (HS * HEAD_SIZE) + eps)
     gated = ssm * jax.nn.silu(gate_z)
@@ -1156,7 +1170,7 @@
         heads, step_at, gy, xs, b_flat, c_flat, b_side, c_side, dt, cum, cumt, first_lin, hp, place_rows, states, back_packs
     )
     *grad_kv, grad_xs = tied(grad_kv[0], *returned, grad_xs)
-    early_w, grad_first = early_products(n1, grad_query, grad_z, cosine, sine, first_w, last_w, grad_kv)
+    early_w, grad_first = early_products(n1, grad_query, grad_z, cosine, sine, first_w, mixer_w, grad_kv)
     grad_xs, early_w = tied(grad_xs, early_w)
     early_parts = scatter_first(early_w)
     grad_conv, halo, grad_inner, grad_bc_taps = conv_back(
@@ -1169,7 +1183,7 @@
     early_parts = scatter_second(early_parts)
     grad_late = joined(heads, grad_conv, behind, grad_step)
     late_w, grad_normed, low_normed = late_products(
-        shape[1:-1], width, qkv_width, n1, xt, scale_one, grad_late, first_w, u_w, grad_first,
+        shape[1:-1], width, qkv_width, n1, xt, scale_one, grad_late, first_w, mixer_w, grad_first,
         grad_gain_two, grad_gain_ssm, grad_inner, grad_bc_taps, grad_head, loss_row,
     )
     gain_one = jnp.broadcast_to(param_rows[heads : heads + 1], (8, MODEL_WIDTH))
@@ -1179,9 +1193,8 @@
     grad_input = input_grad(grad_normed, swapped(low_normed), flat_in, grad_residual, gain_one)
     gateup_out = mlp_out[:, : 2 * ff_local].astype(f32).reshape(rows, 2, ff_local)
     down_out = mlp_out[:, 2 * ff_local :].astype(f32).T
-    late_parts, grad_input, gateup_out, down_out = tied(late_parts, grad_input, gateup_out, down_out)
     late_parts = scatter_second(late_parts, heads)
-    late_parts, inner_other = tied(late_parts, inner_other)
+    late_parts, inner_other, grad_input, gateup_out, down_out = tied(late_parts, inner_other, grad_input, gateup_out, down_out)
     inner_parts = halved_on(inner_kept, inner_other)
     out_at = width + attn_width + 2 * kv_width
     query_out = inner_parts[:, width : width + attn_width]

time: 435 us -> 416 us (0.956)
  local copies, waits for them, and re-layouts: 60.1 us -> 39.4 us
  waiting for transfers between devices: 116 us -> 133 us
  other arithmetic: 42.1 us -> 30.6 us
    ppermute x30, waiting for transfers between devices: 54 us -> 68.4 us  [shifted(): return lax.ppermute(value, axis, pairs)]
    ppermute x4, waiting for transfers between devices: 22.6 us -> 35.2 us  [gathered_line(): other = lax.ppermute(value, zdim[0], [(i, i ^ step) for i in range(size)])]
    unnamed x302 -> x269, local copies, waits for them, and re-layouts: 40.2 us -> 29.1 us
    ppermute x14, starting transfers between devices: 40.6 us -> 31.6 us  [passed_along(): return lax.ppermute(value, axis, pairs)]
    ppermute x4, starting transfers between devices: 3 us -> 10.3 us  [gathered_line(): other = lax.ppermute(value, zdim[0], [(i, i ^ step) for i in range(size)])]
    ppermute x14, waiting for transfers between devices: 16 us -> 10.5 us  [passed_along(): return lax.ppermute(value, axis, pairs)]
    convert_element_type x10, other arithmetic: 11.3 us -> 6.4 us  [reduced_along(): return total.astype(bf16) if kept is None else in_pair(total, kept)]
    squeeze x12 -> x11, local copies, waits for them, and re-layouts: 7.91 us -> 3.09 us  [reduced_along(): lax.dynamic_index_in_dim(value, lax.rem(at + step, size), front, False)]
  transfers between devices with their start and end apart: 60 -> 60, of which waited for: 29 -> 29; matrix products, arithmetic and copies ran while one was open for 13% -> 9% of each run, Pallas kernels for 17% -> 18%
where the time goes in v1:
time: 416 us; the launch traced here: 410 us
  waiting for transfers between devices  133 us (32%)
  starting transfers between devices  84.6 us (20%)
  Pallas kernels  78.6 us (19%)
  local copies, waits for them, and re-layouts  39.4 us (9%)
  other arithmetic  30.6 us (7%)
  matrix products  25.8 us (6%)
  between operations  17.6 us (4%)
    ppermute x30, waiting for transfers between devices, shifted(): return lax.ppermute(value, axis, pairs)  68.4 us
    pallas_call x15, Pallas kernels, call(): pl.pallas_call(body, out_shape=[jax.ShapeDtypeStruct(s, d) for s, d in ou...  64 us
    ppermute x30, starting transfers between devices, shifted(): return lax.ppermute(value, axis, pairs)  35.6 us
    ppermute x4, waiting for transfers between devices, gathered_line(): other = lax.ppermute(value, zdim[0], [(i, i ^ step) for i in range(size)])  35.2 us
    ppermute x14, starting transfers between devices, passed_along(): return lax.ppermute(value, axis, pairs)  31.6 us
    unnamed x269, local copies, waits for them, and re-layouts  29.1 us
    dot_general x9, matrix products, dot(): lax.dot_general(left, right, (((left_dim,), (right_dim,)), ((), ())), pre...  25.8 us
    ppermute x2, waiting for transfers between devices, exchanged(): lax.ppermute(sent, zdim[0], [(i, i ^ step) for i in range(zdim[1])])  12.1 us
  transfers between devices with their start and end apart: 60, of which 29 were waited for; matrix products, arithmetic and copies ran while one was open for 9% of the time, Pallas kernels for 18%

profile of v1, /device:TPU:0, one launch (start us, length us, event | category | flops | bytes accessed | tf_op | source)
XLA Modules:
  0.0 409.5 jit_solution(4944499657218146911)
XLA Ops:
  14.0 5.1 %collective-permute-start = (bf16[64,768]{1,0:T(8,128)(2,1)S(1)}, bf16[64,768]{1,0:T(8,128)(2,1)S(1)}, u32[]{:S(2)}, u32[]{:S(2)}) collective-permute-start(bf16[64,768]{1,0:T(8,128)(2,1)S(1)} %shard_map.322), channel_id=1, source_target_pairs={{0,6},{2,0},{4,2},{6,4},{1,7},{3,1},{5,3},{7,5},{8,14},{10,8},{12,... | collective-permute-start | bytes 294920 | tf_op jit(solution)/shard_map/ppermute | solution.py:63
  20.8 4.4 %collective-permute-start.5 = (bf16[16,1024]{1,0:T(8,128)(2,1)S(1)}, bf16[16,1024]{1,0:T(8,128)(2,1)S(1)}, u32[]{:S(2)}, u32[]{:S(2)}) collective-permute-start(bf16[16,1024]{1,0:T(8,128)(2,1)S(1)} %slice_bitcast_fusion.4), channel_id=1, source_target_pairs={{0,2},{2,4},{4,6},{1,3},{3,5},{5,7},{8,10},{10,12},{12,14},{9,11},... | collective-permute-start | bytes 98312 | tf_op jit(solution)/shard_map/ppermute | solution.py:69
  36.2 3.0 collective-permute-done.6
  39.4 5.1 %collective-permute-done.3 = bf16[1,64,1536]{2,1,0:T(8,128)(2,1)S(1)} collective-permute-done((bf16[1,64,1536]{2,1,0:T(8,128)(2,1)S(1)}, bf16[1,64,1536]{2,1,0:T(8,128)(2,1)S(1)}, u32[]{:S(2)}, u32[]{:S(2)}) %collective-permute-start.3) | collective-permute-done | bytes 196640 | tf_op jit(solution)/shard_map/ppermute | solution.py:102
  44.5 2.0 collective-permute-start.4
  50.9 12.0 %collective-permute-done.4 = bf16[2,64,1536]{2,1,0:T(8,128)(2,1)S(1)} collective-permute-done((bf16[2,64,1536]{2,1,0:T(8,128)(2,1)S(1)}, bf16[2,64,1536]{2,1,0:T(8,128)(2,1)S(1)}, u32[]{:S(2)}, u32[]{:S(2)}) %collective-permute-start.4) | collective-permute-done | bytes 393248 | tf_op jit(solution)/shard_map/ppermute | solution.py:102
  67.3 4.4 %collective-permute-start.13 = (bf16[128,512]{1,0:T(8,128)(2,1)S(1)}, bf16[128,512]{1,0:T(8,128)(2,1)S(1)}, u32[]{:S(2)}, u32[]{:S(2)}) collective-permute-start(bf16[128,512]{1,0:T(8,128)(2,1)S(1)} %get-tuple-element.153.refs_0_), channel_id=1, source_target_pairs={{0,4},{2,6},{1,5},{3,7},{8,12},{10,14},{9,13},{11,15},{16,20},{18,... | collective-permute-start | bytes 393224 | tf_op jit(solution)/shard_map/ppermute | solution.py:69
  73.2 5.0 %collective-permute-done.10 = bf16[4,64,768]{2,1,0:T(8,128)(2,1)S(1)} collective-permute-done((bf16[4,64,768]{2,1,0:T(8,128)(2,1)S(1)}, bf16[4,64,768]{2,1,0:T(8,128)(2,1)S(1)}, u32[]{:S(2)}, u32[]{:S(2)}) %collective-permute-start.10) | collective-permute-done | bytes 393248 | tf_op jit(solution)/shard_map/ppermute | solution.py:63
  78.3 5.8 %collective-permute-done.11 = bf16[4,64,768]{2,1,0:T(8,128)(2,1)S(1)} collective-permute-done((bf16[4,64,768]{2,1,0:T(8,128)(2,1)S(1)}, bf16[4,64,768]{2,1,0:T(8,128)(2,1)S(1)}, u32[]{:S(2)}, u32[]{:S(2)}) %collective-permute-start.11) | collective-permute-done | bytes 393248 | tf_op jit(solution)/shard_map/ppermute | solution.py:63
  84.2 4.2 %collective-permute-start.17 = (bf16[1,64,1024]{2,1,0:T(8,128)(2,1)S(1)}, bf16[1,64,1024]{2,1,0:T(8,128)(2,1)S(1)}, u32[]{:S(2)}, u32[]{:S(2)}) collective-permute-start(bf16[1,64,1024]{2,1,0:T(8,128)(2,1)S(1)} %bitcast.232), channel_id=1, source_target_pairs={{0,2},{2,0},{4,6},{6,4},{1,3},{3,1},{5,7},{7,5},{8,10},{10,8},{12,... | collective-permute-start | bytes 393224 | tf_op jit(solution)/shard_map/ppermute | solution.py:102
  94.0 3.4 collective-permute-start.18
  97.4 8.9 %shard_map.326 = (bf16[256,512]{1,0:T(8,128)(2,1)S(1)}, f32[4,8,512]{2,1,0:T(8,128)S(1)}) custom-call(bf16[256,512]{1,0:T(8,128)(2,1)S(1)} %get-tuple-element.152.q_ref, s32[8,512]{1,0:T(8,128)S(1)} %broadcast_in_dim.58.low_ref, bf16[128,512]{1,0:T(8,128)(2,1)S(1)} %get-tuple-element.153.refs_0_, bf16[128,512]{1,0:T(8,128)(2,1)S(1)} %collective-permute-done.12.refs_1_, ...), custom_call_target="tpu_custom_call" | custom-call | flops 8999999488 | bytes 1000 | tf_op jit(solution)/shard_map/pallas_call | solution.py:202
  106.3 16.4 %collective-permute-done.18 = bf16[2,64,1024]{2,1,0:T(8,128)(2,1)S(1)} collective-permute-done((bf16[2,64,1024]{2,1,0:T(8,128)(2,1)S(1)}, bf16[2,64,1024]{2,1,0:T(8,128)(2,1)S(1)}, u32[]{:S(2)}, u32[]{:S(2)}) %collective-permute-start.18) | collective-permute-done | bytes 262176 | tf_op jit(solution)/shard_map/ppermute | solution.py:102
  123.6 2.7 fusion.50
  128.7 6.7 %shard_map.327 = (f32[768,512]{1,0:T(8,128)S(1)}, f32[512,128]{1,0:T(8,128)S(1)}, f32[512,128]{1,0:T(8,128)S(1)}, f32[128,512]{1,0:T(8,128)S(1)}, f32[128,512]{1...) custom-call(f32[768,640]{1,0:T(8,128)S(1)} %slice.215.u_ref, ...), custom_call_target="tpu_custom_call" | custom-call | flops 7000000000 | bytes 1000 | tf_op jit(solution)/shard_map/pallas_call | solution.py:202
  136.2 3.9 collective-permute-start.21
  140.0 5.4 %collective-permute-start.22 = (bf16[800,128]{1,0:T(8,128)(2,1)S(1)}, bf16[800,128]{1,0:T(8,128)(2,1)S(1)}, u32[]{:S(2)}, u32[]{:S(2)}) collective-permute-start(bf16[800,128]{1,0:T(8,128)(2,1)S(1)} %get-tuple-element.172), channel_id=1, source_target_pairs={{0,4},{2,6},{1,5},{3,7},{8,12},{10,14},{9,13},{11,15},{16,20},{18,... | collective-permute-start | bytes 614408 | tf_op jit(solution)/shard_map/ppermute | solution.py:69
  148.4 4.4 %collective-permute-done.22.refs_1_ = bf16[800,128]{1,0:T(8,128)(2,1)S(1)} collective-permute-done((bf16[800,128]{1,0:T(8,128)(2,1)S(1)}, bf16[800,128]{1,0:T(8,128)(2,1)S(1)}, u32[]{:S(2)}, u32[]{:S(2)}) %collective-permute-start.22) | collective-permute-done | bytes 204832 | tf_op jit(solution)/shard_map/ppermute | solution.py:69
  152.9 3.8 collective-permute-done.23.refs_2_
  156.8 2.2 shard_map.328
  162.1 11.8 %collective-permute-done.26 = bf16[2,4,64,512]{3,2,1,0:T(8,128)(2,1)S(1)} collective-permute-done((bf16[2,4,64,512]{3,2,1,0:T(8,128)(2,1)S(1)}, bf16[2,4,64,512]{3,2,1,0:T(8,128)(2,1)S(1)}, u32[]{:S(2)}, u32[]{:S(2)}) %collective-permute-start.26) | collective-permute-done | bytes 524320 | tf_op jit(solution)/shard_map/ppermute | solution.py:63
  182.9 4.8 %fusion.2 = f32[512,2048]{1,0:T(8,128)S(1)} fusion(bf16[512,1024]{1,0:T(8,128)(2,1)} %multiply_convert_fusion.3.n2_ref, bf16[1024,3072]{1,0:T(8,128)(2,1)} %all-gather.2.cloned.1.call-done), kind=kOutput, calls=%fused_computation.2 | convolution fusion | flops 2147483648 | bytes 9437184 | tf_op jit(solution)/shard_map/dot_general | solution.py:27
  189.8 4.9 %fusion.47 = (bf16[512,1024]{1,0:T(8,128)(2,1)}, f32[512,1024]{1,0:T(8,128)}) fusion(bf16[512,1024]{1,0:T(8,128)(2,1)S(1)} %multiply_convert_fusion.2.m_ref, bf16[1024,3072]{1,0:T(8,128)(2,1)} %all-gather.2.cloned.1.call-done), kind=kOutput, calls=%fused_computation.179 | convolution fusion | flops 1074266112 | bytes 6291456 | tf_op jit(solution)/shard_map/dot_general | solution.py:27
  197.8 4.4 %multiply_reduce_fusion = (f32[]{:T(128)}, f32[512,1024]{1,0:T(8,128)S(1)}) fusion(bf16[1,512,1024]{2,1,0:T(8,128)(2,1)} %param.20, f32[512]{0:T(512)S(1)} %bitcast.246, f32[512,1024]{1,0:T(8,128)} %copy-done.2, f32[512,1024]{1,0:T(8,128)} %get-tuple-element.339, bf16[512,1024]{1,0:T(8,128)(2,1)} %collective-permute-done.28), kind=kLoop, calls=%fused_computation.9 | loop fusion | flops 4194303 | bytes 8390660 | tf_op jit(solution)/shard_map/reduce_sum | solution.py:1135
  202.2 2.1 fusion.41
  205.5 4.0 multiply_convert_fusion.1
  209.8 4.0 fusion.48
  213.8 4.4 %shard_map.335 = bf16[1024,3072]{1,0:T(8,128)(2,1)S(1)} custom-call(bf16[512,1024]{1,0:T(8,128)(2,1)S(1)} %copy-done.17, bf16[512,1024]{1,0:T(8,128)(2,1)S(1)} %get-tuple-element.296.e_ref, bf16[512,2048]{1,0:T(8,128)(2,1)S(1)} %pad_maximum_fusion.2.ggu_ref, bf16[512,1024]{1,0:T(8,128)(2,1)S(1)} %copy-done.16), custom_call_target="tpu_custom_call" | custom-call | flops 1000 | bytes 1000 | tf_op jit(solution)/shard_map/pallas_call | solution.py:975
  218.2 2.7 copy-done.1
  221.7 2.3 collective-permute-done.29.low_ref
  228.8 2.9 shard_map.329
  234.5 2.1 fusion.10
  238.2 3.2 shard_map.330
  247.4 13.7 %shard_map.331 = (bf16[256,512]{1,0:T(8,128)(2,1)S(1)}, bf16[128,512]{1,0:T(8,128)(2,1)S(1)}, bf16[128,512]{1,0:T(8,128)(2,1)S(1)}, bf16[128,512]{1,0:T(8,128)(2,1)S(1)}, bf16[128,512]{1,0:T(8,128)(2,1)S(1)}) custom-call(bf16[256,512]{1,0:T(8,128)(2,1)S(1)} %copy-done.74, s32[8,512]{1,0:T(8,128)S(1)} %copy-done.46, bf16[256,512]{1,0:T(8,128)(2,1)S(1)} %copy-done.76, ...), custom_call_target="tpu_custom_call" | custom-call | flops 14000000000 | bytes 1000 | tf_op jit(solution)/shard_map/pallas_call | solution.py:202
  261.1 10.6 %collective-permute-done.34 = bf16[2,4,64,512]{3,2,1,0:T(8,128)(2,1)S(1)} collective-permute-done((bf16[2,4,64,512]{3,2,1,0:T(8,128)(2,1)S(1)}, bf16[2,4,64,512]{3,2,1,0:T(8,128)(2,1)S(1)}, u32[]{:S(2)}, u32[]{:S(2)}) %collective-permute-start.34) | collective-permute-done | bytes 524320 | tf_op jit(solution)/shard_map/ppermute | solution.py:63
  278.4 13.4 %shard_map.332 = (f32[768,512]{1,0:T(8,128)S(1)}, f32[256,512]{1,0:T(8,128)S(1)}, f32[16,512]{1,0:T(8,128)S(1)}, f32[8,128]{1,0:T(8,128)S(1)}) custom-call(f32[768,512]{1,0:T(8,128)S(1)} %get-tuple-element.194.gy_ref, f32[768,512]{1,0:T(8,128)S(1)} %copy-done.78, f32[512,128]{1,0:T(8,128)S(1)} %copy-done.84, f32[512,128]{1,0:T(8,128)S(1)} %copy-done.82, ...), custom_call_target="tpu_custom_call" | custom-call | flops 12999999488 | bytes 1000 | tf_op jit(solution)/shard_map/pallas_call | solution.py:202
  291.9 4.0 shard_map.333
  300.4 8.1 %shard_map.334 = (f32[1024,512]{1,0:T(8,128)S(1)}, f32[8,1024]{1,0:T(8,128)S(1)}, f32[768,128]{1,0:T(8,128)S(1)}, f32[256,128]{1,0:T(8,128)S(1)}) custom-call(f32[768,640]{1,0:T(8,128)S(1)} %copy-done.24, f32[768,640]{1,0:T(8,128)S(1)} %copy-done.68, f32[768,512]{1,0:T(8,128)S(1)} %get-tuple-element.209.gxs_ref, f32[256,512]{1,0:T(8,128)S(1)} %get-tuple-element.210.gbc_ref, ...), custom_call_target="tpu_custom_call" | custom-call | flops 8000000000 | bytes 1000 | tf_op jit(solution)/shard_map/pallas_call | solution.py:202
  311.6 2.5 collective-permute-done.40
  317.0 2.3 fusion.13
  329.4 6.3 %shard_map.337 = (bf16[1024,1152]{1,0:T(8,128)(2,1)S(1)}, f32[1024,512]{1,0:T(8,128)S(1)}, bf16[1024,512]{1,0:T(8,128)(2,1)S(1)}, f32[1024,128]{1,0:T(8,128)}) custom-call(bf16[1024,640]{1,0:T(8,128)(2,1)S(1)} %copy-done.11, bf16[1024,640]{1,0:T(8,128)(2,1)S(1)} %copy-done.28, f32[8,640]{1,0:T(8,128)S(1)} %copy-done.42, ...), custom_call_target="tpu_custom_call" | custom-call | flops 1000 | bytes 1000 | tf_op jit(solution)/shard_map/pallas_call | solution.py:832
  339.6 9.6 %collective-permute-done.46 = bf16[2,4,64,512]{3,2,1,0:T(8,128)(2,1)S(1)} collective-permute-done((bf16[2,4,64,512]{3,2,1,0:T(8,128)(2,1)S(1)}, bf16[2,4,64,512]{3,2,1,0:T(8,128)(2,1)S(1)}, u32[]{:S(2)}, u32[]{:S(2)}) %collective-permute-start.46) | collective-permute-done | bytes 524320 | tf_op jit(solution)/shard_map/ppermute | solution.py:63
  351.0 5.2 %collective-permute-done.48 = bf16[2,4,64,640]{3,2,1,0:T(8,128)(2,1)S(1)} collective-permute-done((bf16[2,4,64,640]{3,2,1,0:T(8,128)(2,1)S(1)}, bf16[2,4,64,640]{3,2,1,0:T(8,128)(2,1)S(1)}, u32[]{:S(2)}, u32[]{:S(2)}) %collective-permute-start.48) | collective-permute-done | bytes 655392 | tf_op jit(solution)/shard_map/ppermute | solution.py:63
  358.1 3.3 collective-permute-start.50
  364.3 2.5 shard_map.338
  370.8 11.1 %collective-permute-done.50 = bf16[2,64,2176]{2,1,0:T(8,128)(2,1)} collective-permute-done((bf16[2,64,2176]{2,1,0:T(8,128)(2,1)}, bf16[2,64,2176]{2,1,0:T(8,128)(2,1)}, u32[]{:S(2)}, u32[]{:S(2)}) %collective-permute-start.50) | collective-permute-done | bytes 557088 | tf_op jit(solution)/shard_map/ppermute | solution.py:169
  385.9 2.9 collective-permute-start.56
  388.8 6.8 %collective-permute-done.53 = bf16[64,1152]{1,0:T(8,128)(2,1)S(1)} collective-permute-done((bf16[64,1152]{1,0:T(8,128)(2,1)S(1)}, bf16[64,1152]{1,0:T(8,128)(2,1)S(1)}, u32[]{:S(2)}, u32[]{:S(2)}) %collective-permute-start.53) | collective-permute-done | bytes 147488 | tf_op jit(solution)/shard_map/ppermute | solution.py:63
  (487 shorter events, 127.2 us)
Async XLA Ops:
  7.2 175.7 %all-gather.2.cloned.1.call-start = ((), (), s32[]{:S(2)}) async-start(), calls=%async_computation.2 | async-start | bytes 6684672 | tf_op jit(solution)/shard_map/all_gather | solution.py:1079
  14.0 12.3 %collective-permute-start = (bf16[64,768]{1,0:T(8,128)(2,1)S(1)}, bf16[64,768]{1,0:T(8,128)(2,1)S(1)}, u32[]{:S(2)}, u32[]{:S(2)}) collective-permute-start(bf16[64,768]{1,0:T(8,128)(2,1)S(1)} %shard_map.322), channel_id=1, source_target_pairs={{0,6},{2,0},{4,2},{6,4},{1,7},{3,1},{5,3},{7,5},{8,14},{10,8},{12,... | collective-permute-start | bytes 294920 | tf_op jit(solution)/shard_map/ppermute | solution.py:63
  19.1 8.7 %collective-permute-start.1 = (bf16[64,768]{1,0:T(8,128)(2,1)S(1)}, bf16[64,768]{1,0:T(8,128)(2,1)S(1)}, u32[]{:S(2)}, u32[]{:S(2)}) collective-permute-start(bf16[64,768]{1,0:T(8,128)(2,1)S(1)} %shard_map.322), channel_id=1, source_target_pairs={{0,4},{2,6},{4,0},{6,2},{1,5},{3,7},{5,1},{7,3},{8,12},{10,14},{12... | collective-permute-start | bytes 294920 | tf_op jit(solution)/shard_map/ppermute | solution.py:63
  19.1 8.8 %collective-permute-start.2 = (bf16[64,768]{1,0:T(8,128)(2,1)S(1)}, bf16[64,768]{1,0:T(8,128)(2,1)S(1)}, u32[]{:S(2)}, u32[]{:S(2)}) collective-permute-start(bf16[64,768]{1,0:T(8,128)(2,1)S(1)} %shard_map.322), channel_id=1, source_target_pairs={{0,2},{2,4},{4,6},{6,0},{1,3},{3,5},{5,7},{7,1},{8,10},{10,12},{12... | collective-permute-start | bytes 294920 | tf_op jit(solution)/shard_map/ppermute | solution.py:63
  20.8 11.0 %collective-permute-start.5 = (bf16[16,1024]{1,0:T(8,128)(2,1)S(1)}, bf16[16,1024]{1,0:T(8,128)(2,1)S(1)}, u32[]{:S(2)}, u32[]{:S(2)}) collective-permute-start(bf16[16,1024]{1,0:T(8,128)(2,1)S(1)} %slice_bitcast_fusion.4), channel_id=1, source_target_pairs={{0,2},{2,4},{4,6},{1,3},{3,5},{5,7},{8,10},{10,12},{12,14},{9,11},... | collective-permute-start | bytes 98312 | tf_op jit(solution)/shard_map/ppermute | solution.py:69
  26.1 288.2 %reduce-scatter.3.cloned.1.call-start = ((), (), s32[]{:S(2)}) async-start(), calls=%async_computation.3 | async-start | bytes 7864320 | tf_op jit(solution)/shard_map/reduce_scatter | solution.py:1150
  30.2 9.0 %collective-permute-start.6 = (bf16[4,64,384]{2,1,0:T(8,128)(2,1)S(1)}, bf16[4,64,384]{2,1,0:T(8,128)(2,1)S(1)}, u32[]{:S(2)}, u32[]{:S(2)}) collective-permute-start(bf16[4,64,384]{2,1,0:T(8,128)(2,1)S(1)} %get-tuple-element.331), channel_id=1, source_target_pairs={{0,16},{8,24},{16,0},{24,8},{1,17},{9,25},{17,1},{25,9},{2,18},{10... | collective-permute-start | bytes 589832 | tf_op jit(solution)/shard_map/ppermute | solution.py:63
  32.4 12.0 %collective-permute-start.3 = (bf16[1,64,1536]{2,1,0:T(8,128)(2,1)S(1)}, bf16[1,64,1536]{2,1,0:T(8,128)(2,1)S(1)}, u32[]{:S(2)}, u32[]{:S(2)}) collective-permute-start(bf16[1,64,1536]{2,1,0:T(8,128)(2,1)S(1)} %bitcast.223), channel_id=1, source_target_pairs={{0,2},{2,0},{4,6},{6,4},{1,3},{3,1},{5,7},{7,5},{8,10},{10,8},{12,... | collective-permute-start | bytes 589832 | tf_op jit(solution)/shard_map/ppermute | solution.py:102
  34.6 13.0 %collective-permute-start.9 = (bf16[2,4,64,384]{3,2,1,0:T(8,128)(2,1)S(1)}, bf16[2,4,64,384]{3,2,1,0:T(8,128)(2,1)S(1)}, u32[]{:S(2)}, u32[]{:S(2)}) collective-permute-start(bf16[2,4,64,384]{3,2,1,0:T(8,128)(2,1)S(1)} %maximum_select_fusion.15), channel_id=1, source_target_pairs={{0,16},{8,24},{16,0},{24,8},{1,17},{9,25},{17,1},{25,9},{2,18},{10... | collective-permute-start | bytes 1179656 | tf_op jit(solution)/shard_map/ppermute | solution.py:63
  44.5 18.5 %collective-permute-start.4 = (bf16[2,64,1536]{2,1,0:T(8,128)(2,1)S(1)}, bf16[2,64,1536]{2,1,0:T(8,128)(2,1)S(1)}, u32[]{:S(2)}, u32[]{:S(2)}) collective-permute-start(bf16[2,64,1536]{2,1,0:T(8,128)(2,1)S(1)} %maximum_select_fusion.12), channel_id=1, source_target_pairs={{0,4},{2,6},{4,0},{6,2},{1,5},{3,7},{5,1},{7,3},{8,12},{10,14},{12... | collective-permute-start | bytes 1179656 | tf_op jit(solution)/shard_map/ppermute | solution.py:102
  63.2 14.9 %collective-permute-start.10 = (bf16[4,64,768]{2,1,0:T(8,128)(2,1)S(1)}, bf16[4,64,768]{2,1,0:T(8,128)(2,1)S(1)}, u32[]{:S(2)}, u32[]{:S(2)}) collective-permute-start(bf16[4,64,768]{2,1,0:T(8,128)(2,1)S(1)} %get-tuple-element.310), channel_id=1, source_target_pairs={{0,16},{8,24},{16,0},{24,8},{1,17},{9,25},{17,1},{25,9},{2,18},{10... | collective-permute-start | bytes 1179656 | tf_op jit(solution)/shard_map/ppermute | solution.py:63
  64.5 19.5 %collective-permute-start.11 = (bf16[4,64,768]{2,1,0:T(8,128)(2,1)S(1)}, bf16[4,64,768]{2,1,0:T(8,128)(2,1)S(1)}, u32[]{:S(2)}, u32[]{:S(2)}) collective-permute-start(bf16[4,64,768]{2,1,0:T(8,128)(2,1)S(1)} %get-tuple-element.309), channel_id=1, source_target_pairs={{0,8},{8,0},{16,24},{24,16},{1,9},{9,1},{17,25},{25,17},{2,10},{10... | collective-permute-start | bytes 1179656 | tf_op jit(solution)/shard_map/ppermute | solution.py:63
  66.0 18.2 %collective-permute-start.12 = (bf16[128,512]{1,0:T(8,128)(2,1)S(1)}, bf16[128,512]{1,0:T(8,128)(2,1)S(1)}, u32[]{:S(2)}, u32[]{:S(2)}) collective-permute-start(bf16[128,512]{1,0:T(8,128)(2,1)S(1)} %get-tuple-element.153.refs_0_), channel_id=1, source_target_pairs={{0,2},{2,4},{4,6},{1,3},{3,5},{5,7},{8,10},{10,12},{12,14},{9,11},... | collective-permute-start | bytes 393224 | tf_op jit(solution)/shard_map/ppermute | solution.py:69
  67.3 16.9 %collective-permute-start.13 = (bf16[128,512]{1,0:T(8,128)(2,1)S(1)}, bf16[128,512]{1,0:T(8,128)(2,1)S(1)}, u32[]{:S(2)}, u32[]{:S(2)}) collective-permute-start(bf16[128,512]{1,0:T(8,128)(2,1)S(1)} %get-tuple-element.153.refs_0_), channel_id=1, source_target_pairs={{0,4},{2,6},{1,5},{3,7},{8,12},{10,14},{9,13},{11,15},{16,20},{18,... | collective-permute-start | bytes 393224 | tf_op jit(solution)/shard_map/ppermute | solution.py:69
  71.7 12.5 %collective-permute-start.14 = (bf16[128,512]{1,0:T(8,128)(2,1)S(1)}, bf16[128,512]{1,0:T(8,128)(2,1)S(1)}, u32[]{:S(2)}, u32[]{:S(2)}) collective-permute-start(bf16[128,512]{1,0:T(8,128)(2,1)S(1)} %get-tuple-element.153.refs_0_), channel_id=1, source_target_pairs={{0,6},{1,7},{8,14},{9,15},{16,22},{17,23},{24,30},{25,31}} | collective-permute-start | bytes 393224 | tf_op jit(solution)/shard_map/ppermute | solution.py:69
  84.2 9.7 %collective-permute-start.17 = (bf16[1,64,1024]{2,1,0:T(8,128)(2,1)S(1)}, bf16[1,64,1024]{2,1,0:T(8,128)(2,1)S(1)}, u32[]{:S(2)}, u32[]{:S(2)}) collective-permute-start(bf16[1,64,1024]{2,1,0:T(8,128)(2,1)S(1)} %bitcast.232), channel_id=1, source_target_pairs={{0,2},{2,0},{4,6},{6,4},{1,3},{3,1},{5,7},{7,5},{8,10},{10,8},{12,... | collective-permute-start | bytes 393224 | tf_op jit(solution)/shard_map/ppermute | solution.py:102
  88.4 34.4 %collective-permute-start.16 = (bf16[2,4,64,768]{3,2,1,0:T(8,128)(2,1)S(1)}, bf16[2,4,64,768]{3,2,1,0:T(8,128)(2,1)S(1)}, u32[]{:S(2)}, u32[]{:S(2)}) collective-permute-start(bf16[2,4,64,768]{3,2,1,0:T(8,128)(2,1)S(1)} %maximum_select_fusion.8), channel_id=1, source_target_pairs={{0,16},{8,24},{16,0},{24,8},{1,17},{9,25},{17,1},{25,9},{2,18},{10... | collective-permute-start | bytes 2359304 | tf_op jit(solution)/shard_map/ppermute | solution.py:63
  90.3 32.8 %collective-permute-start.15 = (bf16[2,4,64,768]{3,2,1,0:T(8,128)(2,1)S(1)}, bf16[2,4,64,768]{3,2,1,0:T(8,128)(2,1)S(1)}, u32[]{:S(2)}, u32[]{:S(2)}) collective-permute-start(bf16[2,4,64,768]{3,2,1,0:T(8,128)(2,1)S(1)} %maximum_select_fusion.7), channel_id=1, source_target_pairs={{0,8},{8,0},{16,24},{24,16},{1,9},{9,1},{17,25},{25,17},{2,10},{10... | collective-permute-start | bytes 2359304 | tf_op jit(solution)/shard_map/ppermute | solution.py:63
  94.0 28.8 %collective-permute-start.18 = (bf16[2,64,1024]{2,1,0:T(8,128)(2,1)S(1)}, bf16[2,64,1024]{2,1,0:T(8,128)(2,1)S(1)}, u32[]{:S(2)}, u32[]{:S(2)}) collective-permute-start(bf16[2,64,1024]{2,1,0:T(8,128)(2,1)S(1)} %maximum_select_fusion.16), channel_id=1, source_target_pairs={{0,4},{2,6},{4,0},{6,2},{1,5},{3,7},{5,1},{7,3},{8,12},{10,14},{12... | collective-permute-start | bytes 786440 | tf_op jit(solution)/shard_map/ppermute | solution.py:102
  126.5 20.4 %collective-permute-start.19 = (bf16[4,64,512]{2,1,0:T(8,128)(2,1)S(1)}, bf16[4,64,512]{2,1,0:T(8,128)(2,1)S(1)}, u32[]{:S(2)}, u32[]{:S(2)}) collective-permute-start(bf16[4,64,512]{2,1,0:T(8,128)(2,1)S(1)} %get-tuple-element.325), channel_id=1, source_target_pairs={{0,16},{8,24},{16,0},{24,8},{1,17},{9,25},{17,1},{25,9},{2,18},{10... | collective-permute-start | bytes 786440 | tf_op jit(solution)/shard_map/ppermute | solution.py:63
  127.0 20.0 %collective-permute-start.20 = (bf16[4,64,512]{2,1,0:T(8,128)(2,1)S(1)}, bf16[4,64,512]{2,1,0:T(8,128)(2,1)S(1)}, u32[]{:S(2)}, u32[]{:S(2)}) collective-permute-start(bf16[4,64,512]{2,1,0:T(8,128)(2,1)S(1)} %get-tuple-element.324), channel_id=1, source_target_pairs={{0,8},{8,0},{16,24},{24,16},{1,9},{9,1},{17,25},{25,17},{2,10},{10... | collective-permute-start | bytes 786440 | tf_op jit(solution)/shard_map/ppermute | solution.py:63
  136.2 12.3 %collective-permute-start.21 = (bf16[800,128]{1,0:T(8,128)(2,1)S(1)}, bf16[800,128]{1,0:T(8,128)(2,1)S(1)}, u32[]{:S(2)}, u32[]{:S(2)}) collective-permute-start(bf16[800,128]{1,0:T(8,128)(2,1)S(1)} %get-tuple-element.172), channel_id=1, source_target_pairs={{0,2},{2,4},{4,6},{1,3},{3,5},{5,7},{8,10},{10,12},{12,14},{9,11},... | collective-permute-start | bytes 614408 | tf_op jit(solution)/shard_map/ppermute | solution.py:69
  140.0 12.8 %collective-permute-start.22 = (bf16[800,128]{1,0:T(8,128)(2,1)S(1)}, bf16[800,128]{1,0:T(8,128)(2,1)S(1)}, u32[]{:S(2)}, u32[]{:S(2)}) collective-permute-start(bf16[800,128]{1,0:T(8,128)(2,1)S(1)} %get-tuple-element.172), channel_id=1, source_target_pairs={{0,4},{2,6},{1,5},{3,7},{8,12},{10,14},{9,13},{11,15},{16,20},{18,... | collective-permute-start | bytes 614408 | tf_op jit(solution)/shard_map/ppermute | solution.py:69
  145.4 11.3 %collective-permute-start.23 = (bf16[800,128]{1,0:T(8,128)(2,1)S(1)}, bf16[800,128]{1,0:T(8,128)(2,1)S(1)}, u32[]{:S(2)}, u32[]{:S(2)}) collective-permute-start(bf16[800,128]{1,0:T(8,128)(2,1)S(1)} %get-tuple-element.172), channel_id=1, source_target_pairs={{0,6},{1,7},{8,14},{9,15},{16,22},{17,23},{24,30},{25,31}} | collective-permute-start | bytes 614408 | tf_op jit(solution)/shard_map/ppermute | solution.py:69
  159.4 14.5 %collective-permute-start.26 = (bf16[2,4,64,512]{3,2,1,0:T(8,128)(2,1)S(1)}, bf16[2,4,64,512]{3,2,1,0:T(8,128)(2,1)S(1)}, u32[]{:S(2)}, u32[]{:S(2)}) collective-permute-start(bf16[2,4,64,512]{3,2,1,0:T(8,128)(2,1)S(1)} %maximum_select_fusion.11), channel_id=1, source_target_pairs={{0,16},{8,24},{16,0},{24,8},{1,17},{9,25},{17,1},{25,9},{2,18},{10... | collective-permute-start | bytes 1572872 | tf_op jit(solution)/shard_map/ppermute | solution.py:63
  161.3 14.0 %collective-permute-start.25 = (bf16[2,4,64,512]{3,2,1,0:T(8,128)(2,1)S(1)}, bf16[2,4,64,512]{3,2,1,0:T(8,128)(2,1)S(1)}, u32[]{:S(2)}, u32[]{:S(2)}) collective-permute-start(bf16[2,4,64,512]{3,2,1,0:T(8,128)(2,1)S(1)} %maximum_select_fusion.10), channel_id=1, source_target_pairs={{0,8},{8,0},{16,24},{24,16},{1,9},{9,1},{17,25},{25,17},{2,10},{10... | collective-permute-start | bytes 1572872 | tf_op jit(solution)/shard_map/ppermute | solution.py:63
  220.9 145.9 %reduce-scatter.5.cloned.1.call-start = ((), (), s32[]{:S(2)}) async-start(), calls=%async_computation.4 | async-start | bytes 1966080 | tf_op jit(solution)/shard_map/reduce_scatter | solution.py:1180
  241.4 30.7 %collective-permute-start.31 = (bf16[800,128]{1,0:T(8,128)(2,1)S(1)}, bf16[800,128]{1,0:T(8,128)(2,1)S(1)}, u32[]{:S(2)}, u32[]{:S(2)}) collective-permute-start(bf16[800,128]{1,0:T(8,128)(2,1)S(1)} %get-tuple-element.182), channel_id=1, source_target_pairs={{2,0},{4,2},{6,4},{3,1},{5,3},{7,5},{10,8},{12,10},{14,12},{11,9},... | collective-permute-start | bytes 614408 | tf_op jit(solution)/shard_map/ppermute | solution.py:69
  242.7 29.4 %collective-permute-start.32 = (bf16[800,128]{1,0:T(8,128)(2,1)S(1)}, bf16[800,128]{1,0:T(8,128)(2,1)S(1)}, u32[]{:S(2)}, u32[]{:S(2)}) collective-permute-start(bf16[800,128]{1,0:T(8,128)(2,1)S(1)} %get-tuple-element.182), channel_id=1, source_target_pairs={{4,0},{6,2},{5,1},{7,3},{12,8},{14,10},{13,9},{15,11},{20,16},{22,... | collective-permute-start | bytes 614408 | tf_op jit(solution)/shard_map/ppermute | solution.py:69
  244.0 28.1 %collective-permute-start.33 = (bf16[800,128]{1,0:T(8,128)(2,1)S(1)}, bf16[800,128]{1,0:T(8,128)(2,1)S(1)}, u32[]{:S(2)}, u32[]{:S(2)}) collective-permute-start(bf16[800,128]{1,0:T(8,128)(2,1)S(1)} %get-tuple-element.182), channel_id=1, source_target_pairs={{6,0},{7,1},{14,8},{15,9},{22,16},{23,17},{30,24},{31,25}} | collective-permute-start | bytes 614408 | tf_op jit(solution)/shard_map/ppermute | solution.py:69
  245.9 25.9 %collective-permute-start.34 = (bf16[2,4,64,512]{3,2,1,0:T(8,128)(2,1)S(1)}, bf16[2,4,64,512]{3,2,1,0:T(8,128)(2,1)S(1)}, u32[]{:S(2)}, u32[]{:S(2)}) collective-permute-start(bf16[2,4,64,512]{3,2,1,0:T(8,128)(2,1)S(1)} %dynamic-slice_bitcast_fusion.5), channel_id=1, source_target_pairs={{0,8},{8,0},{16,24},{24,16},{1,9},{9,1},{17,25},{25,17},{2,10},{10... | collective-permute-start | bytes 1572872 | tf_op jit(solution)/shard_map/ppermute | solution.py:63
  246.0 25.9 %collective-permute-start.35 = (bf16[2,4,64,512]{3,2,1,0:T(8,128)(2,1)S(1)}, bf16[2,4,64,512]{3,2,1,0:T(8,128)(2,1)S(1)}, u32[]{:S(2)}, u32[]{:S(2)}) collective-permute-start(bf16[2,4,64,512]{3,2,1,0:T(8,128)(2,1)S(1)} %dynamic-slice_bitcast_fusion.4), channel_id=1, source_target_pairs={{0,16},{8,24},{16,0},{24,8},{1,17},{9,25},{17,1},{25,9},{2,18},{10... | collective-permute-start | bytes 1572872 | tf_op jit(solution)/shard_map/ppermute | solution.py:63
  272.1 19.7 %collective-permute-start.36 = (bf16[128,512]{1,0:T(8,128)(2,1)S(1)}, bf16[128,512]{1,0:T(8,128)(2,1)S(1)}, u32[]{:S(2)}, u32[]{:S(2)}) collective-permute-start(bf16[128,512]{1,0:T(8,128)(2,1)S(1)} %get-tuple-element.191), channel_id=1, source_target_pairs={{2,0},{4,2},{6,4},{3,1},{5,3},{7,5},{10,8},{12,10},{14,12},{11,9},... | collective-permute-start | bytes 393224 | tf_op jit(solution)/shard_map/ppermute | solution.py:69
  273.4 18.4 %collective-permute-start.37 = (bf16[128,512]{1,0:T(8,128)(2,1)S(1)}, bf16[128,512]{1,0:T(8,128)(2,1)S(1)}, u32[]{:S(2)}, u32[]{:S(2)}) collective-permute-start(bf16[128,512]{1,0:T(8,128)(2,1)S(1)} %get-tuple-element.192), channel_id=1, source_target_pairs={{4,0},{6,2},{5,1},{7,3},{12,8},{14,10},{13,9},{15,11},{20,16},{22,... | collective-permute-start | bytes 393224 | tf_op jit(solution)/shard_map/ppermute | solution.py:69
  274.7 17.1 %collective-permute-start.38 = (bf16[128,512]{1,0:T(8,128)(2,1)S(1)}, bf16[128,512]{1,0:T(8,128)(2,1)S(1)}, u32[]{:S(2)}, u32[]{:S(2)}) collective-permute-start(bf16[128,512]{1,0:T(8,128)(2,1)S(1)} %get-tuple-element.193), channel_id=1, source_target_pairs={{6,0},{7,1},{14,8},{15,9},{22,16},{23,17},{30,24},{31,25}} | collective-permute-start | bytes 393224 | tf_op jit(solution)/shard_map/ppermute | solution.py:69
  276.0 33.9 %collective-permute-start.42 = (bf16[4,64,512]{2,1,0:T(8,128)(2,1)S(1)}, bf16[4,64,512]{2,1,0:T(8,128)(2,1)S(1)}, u32[]{:S(2)}, u32[]{:S(2)}) collective-permute-start(bf16[4,64,512]{2,1,0:T(8,128)(2,1)S(1)} %dynamic-slice_bitcast_fusion.10), channel_id=1, source_target_pairs={{0,16},{8,24},{16,0},{24,8},{1,17},{9,25},{17,1},{25,9},{2,18},{10... | collective-permute-start | bytes 786440 | tf_op jit(solution)/shard_map/ppermute | solution.py:63
  276.6 34.3 %collective-permute-start.43 = (bf16[4,64,512]{2,1,0:T(8,128)(2,1)S(1)}, bf16[4,64,512]{2,1,0:T(8,128)(2,1)S(1)}, u32[]{:S(2)}, u32[]{:S(2)}) collective-permute-start(bf16[4,64,512]{2,1,0:T(8,128)(2,1)S(1)} %dynamic-slice_bitcast_fusion.9), channel_id=1, source_target_pairs={{0,8},{8,0},{16,24},{24,16},{1,9},{9,1},{17,25},{25,17},{2,10},{10... | collective-permute-start | bytes 786440 | tf_op jit(solution)/shard_map/ppermute | solution.py:63
  297.4 16.7 %collective-permute-start.40 = (bf16[2,4,64,512]{3,2,1,0:T(8,128)(2,1)S(1)}, bf16[2,4,64,512]{3,2,1,0:T(8,128)(2,1)S(1)}, u32[]{:S(2)}, u32[]{:S(2)}) collective-permute-start(bf16[2,4,64,512]{3,2,1,0:T(8,128)(2,1)S(1)} %dynamic-slice_bitcast_fusion.3), channel_id=1, source_target_pairs={{0,8},{8,0},{16,24},{24,16},{1,9},{9,1},{17,25},{25,17},{2,10},{10... | collective-permute-start | bytes 1572872 | tf_op jit(solution)/shard_map/ppermute | solution.py:63
  298.7 18.3 %collective-permute-start.41 = (bf16[2,4,64,640]{3,2,1,0:T(8,128)(2,1)}, bf16[2,4,64,640]{3,2,1,0:T(8,128)(2,1)}, u32[]{:S(2)}, u32[]{:S(2)}) collective-permute-start(bf16[2,4,64,640]{3,2,1,0:T(8,128)(2,1)} %dynamic-slice_bitcast_fusion.1), channel_id=1, source_target_pairs={{0,16},{8,24},{16,0},{24,8},{1,17},{9,25},{17,1},{25,9},{2,18},{10... | collective-permute-start | bytes 1966088 | tf_op jit(solution)/shard_map/ppermute | solution.py:63
  320.9 14.8 %collective-permute-start.44 = (bf16[4,64,512]{2,1,0:T(8,128)(2,1)}, bf16[4,64,512]{2,1,0:T(8,128)(2,1)}, u32[]{:S(2)}, u32[]{:S(2)}) collective-permute-start(bf16[4,64,512]{2,1,0:T(8,128)(2,1)} %dynamic-slice_bitcast_fusion.8), channel_id=1, source_target_pairs={{0,16},{8,24},{16,0},{24,8},{1,17},{9,25},{17,1},{25,9},{2,18},{10... | collective-permute-start | bytes 786440 | tf_op jit(solution)/shard_map/ppermute | solution.py:63
  324.4 12.4 %collective-permute-start.45 = (bf16[4,64,640]{2,1,0:T(8,128)(2,1)S(1)}, bf16[4,64,640]{2,1,0:T(8,128)(2,1)S(1)}, u32[]{:S(2)}, u32[]{:S(2)}) collective-permute-start(bf16[4,64,640]{2,1,0:T(8,128)(2,1)S(1)} %dynamic-slice_bitcast_fusion.6), channel_id=1, source_target_pairs={{0,8},{8,0},{16,24},{24,16},{1,9},{9,1},{17,25},{25,17},{2,10},{10... | collective-permute-start | bytes 983048 | tf_op jit(solution)/shard_map/ppermute | solution.py:63
  337.2 11.9 %collective-permute-start.46 = (bf16[2,4,64,512]{3,2,1,0:T(8,128)(2,1)S(1)}, bf16[2,4,64,512]{3,2,1,0:T(8,128)(2,1)S(1)}, u32[]{:S(2)}, u32[]{:S(2)}) collective-permute-start(bf16[2,4,64,512]{3,2,1,0:T(8,128)(2,1)S(1)} %dynamic-slice_bitcast_fusion.2), channel_id=1, source_target_pairs={{0,8},{8,0},{16,24},{24,16},{1,9},{9,1},{17,25},{25,17},{2,10},{10... | collective-permute-start | bytes 1572872 | tf_op jit(solution)/shard_map/ppermute | solution.py:63
  339.0 17.2 %collective-permute-start.48 = (bf16[2,4,64,640]{3,2,1,0:T(8,128)(2,1)S(1)}, bf16[2,4,64,640]{3,2,1,0:T(8,128)(2,1)S(1)}, u32[]{:S(2)}, u32[]{:S(2)}) collective-permute-start(bf16[2,4,64,640]{3,2,1,0:T(8,128)(2,1)S(1)} %dynamic-slice_bitcast_fusion), channel_id=1, source_target_pairs={{0,16},{8,24},{16,0},{24,8},{1,17},{9,25},{17,1},{25,9},{2,18},{10... | collective-permute-start | bytes 1966088 | tf_op jit(solution)/shard_map/ppermute | solution.py:63
  349.4 12.1 %collective-permute-start.47 = (bf16[4,64,512]{2,1,0:T(8,128)(2,1)S(1)}, bf16[4,64,512]{2,1,0:T(8,128)(2,1)S(1)}, u32[]{:S(2)}, u32[]{:S(2)}) collective-permute-start(bf16[4,64,512]{2,1,0:T(8,128)(2,1)S(1)} %dynamic-slice_bitcast_fusion.7), channel_id=1, source_target_pairs={{0,16},{8,24},{16,0},{24,8},{1,17},{9,25},{17,1},{25,9},{2,18},{10... | collective-permute-start | bytes 786440 | tf_op jit(solution)/shard_map/ppermute | solution.py:63
  358.1 23.8 %collective-permute-start.50 = (bf16[2,64,2176]{2,1,0:T(8,128)(2,1)}, bf16[2,64,2176]{2,1,0:T(8,128)(2,1)}, u32[]{:S(2)}, u32[]{:S(2)}) collective-permute-start(bf16[2,64,2176]{2,1,0:T(8,128)(2,1)} %broadcast_select_fusion), channel_id=1, source_target_pairs={{0,4},{2,6},{4,0},{6,2},{1,5},{3,7},{5,1},{7,3},{8,12},{10,14},{12... | collective-permute-start | bytes 1671176 | tf_op jit(solution)/shard_map/ppermute | solution.py:169
  383.9 11.7 %collective-permute-start.53 = (bf16[64,1152]{1,0:T(8,128)(2,1)S(1)}, bf16[64,1152]{1,0:T(8,128)(2,1)S(1)}, u32[]{:S(2)}, u32[]{:S(2)}) collective-permute-start(bf16[64,1152]{1,0:T(8,128)(2,1)S(1)} %get-tuple-element.315), channel_id=1, source_target_pairs={{0,4},{2,6},{4,0},{6,2},{1,5},{3,7},{5,1},{7,3},{8,12},{10,14},{12... | collective-permute-start | bytes 442376 | tf_op jit(solution)/shard_map/ppermute | solution.py:63
  383.9 11.7 %collective-permute-start.52 = (bf16[64,1152]{1,0:T(8,128)(2,1)S(1)}, bf16[64,1152]{1,0:T(8,128)(2,1)S(1)}, u32[]{:S(2)}, u32[]{:S(2)}) collective-permute-start(bf16[64,1152]{1,0:T(8,128)(2,1)S(1)} %get-tuple-element.313), channel_id=1, source_target_pairs={{0,2},{2,4},{4,6},{6,0},{1,3},{3,5},{5,7},{7,1},{8,10},{10,12},{12... | collective-permute-start | bytes 442376 | tf_op jit(solution)/shard_map/ppermute | solution.py:63
  385.9 13.6 %collective-permute-start.56 = (bf16[1,64,2176]{2,1,0:T(8,128)(2,1)S(1)}, bf16[1,64,2176]{2,1,0:T(8,128)(2,1)S(1)}, u32[]{:S(2)}, u32[]{:S(2)}) collective-permute-start(bf16[1,64,2176]{2,1,0:T(8,128)(2,1)S(1)} %broadcast_select_fusion.1), channel_id=1, source_target_pairs={{0,2},{2,0},{4,6},{6,4},{1,3},{3,1},{5,7},{7,5},{8,10},{10,8},{12,... | collective-permute-start | bytes 835592 | tf_op jit(solution)/shard_map/ppermute | solution.py:169
  (138 other events, 1885.8 us)
Sparse Core Ops, SparseCore 0:
  26.2 122.2 all-gather.1
  221.0 86.9 reduce-scatter.2
  323.3 35.9 reduce-scatter.4

commit v2 on v1

--- a/solution.py
+++ b/solution.py
@@ -206,7 +206,7 @@
         out_specs=[pl.BlockSpec(memory_space=pltpu.VMEM)] * len(outs),
         scratch_shapes=[pltpu.VMEM(s, d) for s, d in scratch],
         compiler_params=pltpu.CompilerParams(vmem_limit_bytes=VMEM_LIMIT),
-        cost_estimate=pl.CostEstimate(flops=COSTS.get(name, 1) * 10**9, bytes_accessed=1000, transcendentals=0),
+        cost_estimate=pl.CostEstimate(flops=COSTS.get(name, 1) * 5 * 10**8, bytes_accessed=1000, transcendentals=0),
     )(*args)
 
 
@@ -247,15 +247,17 @@
             low = low_ref[0:1, lanes]
             top = jnp.full((1, width), masked_score, f32)
             for j in range(blocks):
-                scores = block_scores(key_ref[j], query, low, at, j * length, width)
-                score_ref[j] = scores
+                seen = length if j else at + width
+                scores = block_scores(key_ref[j, :seen, :], query, low, at, j * length, width)
+                score_ref[j, :seen, :] = scores
                 top = jnp.maximum(top, jnp.max(scores, axis=0, keepdims=True))
             total = jnp.zeros((1, width), f32)
             mixed = jnp.zeros((HEAD_SIZE, width), f32)
             for j in range(blocks):
-                weight = jnp.exp(score_ref[j] - top)
+                seen = length if j else at + width
+                weight = jnp.exp(score_ref[j, :seen, :] - top)
                 total = total + jnp.sum(weight, axis=0, keepdims=True)
-                mixed = mixed + dot(kv[j][HEAD_SIZE:, :], weight.astype(bf16), 1, 0)
+                mixed = mixed + dot(kv[j][HEAD_SIZE:, :seen], weight.astype(bf16), 1, 0)
             out_ref[rows, lanes] = (mixed / total).astype(bf16)
             log_ref[h, :, lanes] = jnp.broadcast_to(top + jnp.log(total), (8, width))
 
@@ -295,13 +297,14 @@
             inner = jnp.sum(grad.astype(f32) * out_ref[rows, lanes].astype(f32), axis=0, keepdims=True)
             gq = jnp.zeros((HEAD_SIZE, width), f32)
             for j in range(blocks):
-                scores = block_scores(key_ref[j], query, low, at, j * length, width)
+                seen = length if j else at + width
+                scores = block_scores(key_ref[j, :seen, :], query, low, at, j * length, width)
                 probs = jnp.exp(scores - log_total)
-                grad_probs = dot(value_ref[j], grad, 1, 0)
+                grad_probs = dot(value_ref[j, :seen, :], grad, 1, 0)
                 grad_scores = (probs * (grad_probs - inner)).astype(bf16)
-                gq = gq + dot(kv[j][:HEAD_SIZE, :], grad_scores, 1, 0)
-                sum_ref[j, :HEAD_SIZE, :] += dot(query, grad_scores, 1, 1)
-                sum_ref[j, HEAD_SIZE:, :] += dot(grad, probs.astype(bf16), 1, 1)
+                gq = gq + dot(kv[j][:HEAD_SIZE, :seen], grad_scores, 1, 0)
+                sum_ref[j, :HEAD_SIZE, :seen] += dot(query, grad_scores, 1, 1)
+                sum_ref[j, HEAD_SIZE:, :seen] += dot(grad, probs.astype(bf16), 1, 1)
             gq = rotated(gq * HEAD_SIZE**-0.5, cos_ref[:, lanes], -sin_ref[:, lanes])
             gq_ref[rows, lanes] = gq.astype(bf16)
 
@@ -816,7 +819,7 @@
         term = dot(weights, grad, 1, 0)
         total = term if total is None else total + term
         at += rows
-    gn_ref[...] = total
+    gn_ref[...] = total.astype(bf16)
 
 
 def rows_call(body, outs, cuts, *args):
@@ -836,7 +839,7 @@
         in_specs=[spec(a.shape, cut) for a, cut in zip(args, cuts, strict=True)],
         out_specs=[spec(s) for s, _ in outs],
         compiler_params=pltpu.CompilerParams(vmem_limit_bytes=VMEM_LIMIT),
-        cost_estimate=pl.CostEstimate(flops=1000, bytes_accessed=1000, transcendentals=0),
+        cost_estimate=pl.CostEstimate(flops=4 * 5 * 10**8, bytes_accessed=1000, transcendentals=0),
     )(*args)
 
 
@@ -845,7 +848,7 @@
     columns = gq.shape[0] + gkv[0].shape[0] + gz.shape[0]
     return rows_call(
         functools.partial(early_body, len(gkv)),
-        [((features, columns), bf16), ((features, length), f32)],
+        [((features, columns), bf16), ((features, length), bf16)],
         (0, None, None, None, None, 0, gz.shape[0]) + (None,) * len(gkv),
         n1, gq, gz, cosine, sine, first_w, last_w, *gkv,
     )
@@ -867,14 +870,13 @@
     return call(functools.partial(join_body, rows, heads), [((rows + 128, length), bf16)], [], grads, behind, step)[0]
 
 
-def late_body(shape, width, rest_at, n1_ref, xt_ref, scale_ref, g_ref, first_ref, u_ref, gn_ref, two_ref, inner_a_ref, inner_b_ref, basis_ref, head_ref, loss_ref, gw_ref, total_ref, low_ref, tail_ref):
+def late_body(shape, width, rest_at, n1_ref, xt_ref, scale_ref, g_ref, first_ref, u_ref, gn_ref, two_ref, inner_a_ref, inner_b_ref, basis_ref, head_ref, loss_ref, gw_ref, low_ref, tail_ref):
     rows, inner_rows, bc_rows, heads = shape
     grad = g_ref[...]
     columns = grad.shape[0]
     made = dot(n1_ref[:, HALO:], grad, 1, 1)
     gw_ref[:, : columns - 128] = made[:, : columns - 128].astype(bf16)
-    total = gn_ref[...] + dot(u_ref[:, width:], grad[:width], 1, 0) + dot(first_ref[:, rest_at:], grad[width:], 1, 0)
-    total_ref[...] = total
+    total = gn_ref[...].astype(f32) + dot(u_ref[:, width:], grad[:width], 1, 0) + dot(first_ref[:, rest_at:], grad[width:], 1, 0)
     low_ref[...] = total.astype(bf16)
     scaled = xt_ref[:, HALO:].astype(f32) * scale_ref[0:1, HALO:]
     column = lax.broadcasted_iota(jnp.int32, tail_ref.shape, 1)
@@ -897,10 +899,10 @@
     features, length = gn.shape
     return rows_call(
         functools.partial(late_body, shape, width, rest_at),
-        [((features, grads.shape[0]), bf16), ((features, length), f32), ((features, length), bf16), ((features, 128), f32)],
+        [((features, grads.shape[0]), bf16), ((features, length), bf16), ((features, 128), f32)],
         (0, 0, None, None, 0, 0, 0, 1, 0, 0, 0, None, None),
         n1, xt, scale, grads, first_w, u_w, gn, two, inner_a, inner_b, basis, head, loss,
-    )[:3]
+    )[:2]
 
 
 def finish_body(shape, total_ref, other_ref, count_ref, bc_ref, norm_ref, step_ref, ssm_ref, two_ref, inner_ref, basis_ref, head_ref, loss_ref):
@@ -950,7 +952,7 @@
     length = x_ref.shape[0]
     for at in range(0, length, HALO):
         rows = slice(at, at + HALO)
-        grad = jnp.transpose(own_ref[:, rows] + low_ref[:, rows].astype(f32)) * gain_ref[0:1, :]
+        grad = jnp.transpose(own_ref[:, rows].astype(f32) + low_ref[:, rows].astype(f32)) * gain_ref[0:1, :]
         x = x_ref[rows, :].astype(f32)
         scale = lax.rsqrt(jnp.mean(x * x, axis=1, keepdims=True) + eps)
         inner = jnp.mean(grad * x, axis=1, keepdims=True)
@@ -979,7 +981,7 @@
         in_specs=[cut, cut, pl.BlockSpec(ggu.shape, lambda i: (0, 0)), pl.BlockSpec(m.shape, lambda i: (0, 0))],
         out_specs=pl.BlockSpec((features // blocks, columns), lambda i: (i, 0)),
         compiler_params=pltpu.CompilerParams(vmem_limit_bytes=VMEM_LIMIT),
-        cost_estimate=pl.CostEstimate(flops=1000, bytes_accessed=1000, transcendentals=0),
+        cost_estimate=pl.CostEstimate(flops=4 * 5 * 10**8, bytes_accessed=1000, transcendentals=0),
     )(n2, e, ggu, m)
 
 
@@ -1127,8 +1129,9 @@
     scale_two = rms_scale(residual)
     normed_two = (residual * scale_two * gain_two).astype(bf16)
     gateup = dot(normed_two, gateup_w, 1, 0)
-    gate_part, up_part = gateup[:, :ff_local], gateup[:, ff_local:]
-    hidden_mlp = (jax.nn.silu(gate_part) * up_part).astype(bf16)
+    hidden_mlp = (jax.nn.silu(gateup[:, :ff_local]) * gateup[:, ff_local:]).astype(bf16)
+    gateup, hidden_mlp = tied(gateup.astype(bf16), hidden_mlp)
+    gate_part, up_part = gateup[:, :ff_local].astype(f32), gateup[:, ff_local:].astype(f32)
     part = dot(hidden_mlp, down_w, 1, 1)
     final_rows = residual + (part + swapped(part.astype(bf16)).astype(f32))
     difference = (final_rows - teacher.reshape(length, MODEL_WIDTH).astype(f32)) * live_rows
@@ -1182,7 +1185,7 @@
     behind, early_parts, out_parts = tied(behind, early_parts, out_parts)
     early_parts = scatter_second(early_parts)
     grad_late = joined(heads, grad_conv, behind, grad_step)
-    late_w, grad_normed, low_normed = late_products(
+    late_w, low_normed = late_products(
         shape[1:-1], width, qkv_width, n1, xt, scale_one, grad_late, first_w, mixer_w, grad_first,
         grad_gain_two, grad_gain_ssm, grad_inner, grad_bc_taps, grad_head, loss_row,
     )
@@ -1190,7 +1193,7 @@
     late_w, low_normed, early_parts, out_parts = tied(late_w, low_normed, early_parts, out_parts)
     late_parts = scatter_first(late_w, heads)
     inner_kept, inner_other = halved([*early_parts, *out_parts])
-    grad_input = input_grad(grad_normed, swapped(low_normed), flat_in, grad_residual, gain_one)
+    grad_input = input_grad(low_normed, swapped(low_normed), flat_in, grad_residual, gain_one)
     gateup_out = mlp_out[:, : 2 * ff_local].astype(f32).reshape(rows, 2, ff_local)
     down_out = mlp_out[:, 2 * ff_local :].astype(f32).T
     late_parts = scatter_second(late_parts, heads)

time: 416 us -> 409 us (0.983)
    unnamed x269 -> x263, local copies, waits for them, and re-layouts: 29.1 us -> 25.5 us
  transfers between devices with their start and end apart: 60 -> 60, of which waited for: 29 -> 31; matrix products, arithmetic and copies ran while one was open for 9% -> 9% of each run, Pallas kernels for 18% -> 18%
where the time goes in v2:
time: 409 us; the launch traced here: 402 us
  waiting for transfers between devices  130 us (32%)
  starting transfers between devices  87.1 us (21%)
  Pallas kernels  76.4 us (19%)
  local copies, waits for them, and re-layouts  36.7 us (9%)
  other arithmetic  27.2 us (7%)
  matrix products  27 us (7%)
  between operations  17.7 us (4%)
    ppermute x30, waiting for transfers between devices, shifted(): return lax.ppermute(value, axis, pairs)  69.4 us
    pallas_call x15, Pallas kernels, call(): pl.pallas_call(body, out_shape=[jax.ShapeDtypeStruct(s, d) for s, d in ou...  63 us
    ppermute x30, starting transfers between devices, shifted(): return lax.ppermute(value, axis, pairs)  38.9 us
    ppermute x4, waiting for transfers between devices, gathered_line(): other = lax.ppermute(value, zdim[0], [(i, i ^ step) for i in range(size)])  37.2 us
    ppermute x14, starting transfers between devices, passed_along(): return lax.ppermute(value, axis, pairs)  31.5 us
    dot_general x9, matrix products, dot(): lax.dot_general(left, right, (((left_dim,), (right_dim,)), ((), ())), pre...  27 us
    unnamed x263, local copies, waits for them, and re-layouts  25.5 us
    ppermute x4, starting transfers between devices, gathered_line(): other = lax.ppermute(value, zdim[0], [(i, i ^ step) for i in range(size)])  10.5 us
  transfers between devices with their start and end apart: 60, of which 31 were waited for; matrix products, arithmetic and copies ran while one was open for 9% of the time, Pallas kernels for 18%

profile of v2, /device:TPU:0, one launch (start us, length us, event | category | flops | bytes accessed | tf_op | source)
XLA Modules:
  0.0 402.4 jit_solution(10780140682417836994)
XLA Ops:
  14.0 5.1 %collective-permute-start = (bf16[64,768]{1,0:T(8,128)(2,1)S(1)}, bf16[64,768]{1,0:T(8,128)(2,1)S(1)}, u32[]{:S(2)}, u32[]{:S(2)}) collective-permute-start(bf16[64,768]{1,0:T(8,128)(2,1)S(1)} %shard_map.322), channel_id=1, source_target_pairs={{0,6},{2,0},{4,2},{6,4},{1,7},{3,1},{5,3},{7,5},{8,14},{10,8},{12,... | collective-permute-start | bytes 294920 | tf_op jit(solution)/shard_map/ppermute | solution.py:63
  20.8 4.4 %collective-permute-start.5 = (bf16[16,1024]{1,0:T(8,128)(2,1)S(1)}, bf16[16,1024]{1,0:T(8,128)(2,1)S(1)}, u32[]{:S(2)}, u32[]{:S(2)}) collective-permute-start(bf16[16,1024]{1,0:T(8,128)(2,1)S(1)} %slice_bitcast_fusion.4), channel_id=1, source_target_pairs={{0,2},{2,4},{4,6},{1,3},{3,5},{5,7},{8,10},{10,12},{12,14},{9,11},... | collective-permute-start | bytes 98312 | tf_op jit(solution)/shard_map/ppermute | solution.py:69
  37.8 6.1 %collective-permute-done.3 = bf16[1,64,1536]{2,1,0:T(8,128)(2,1)S(1)} collective-permute-done((bf16[1,64,1536]{2,1,0:T(8,128)(2,1)S(1)}, bf16[1,64,1536]{2,1,0:T(8,128)(2,1)S(1)}, u32[]{:S(2)}, u32[]{:S(2)}) %collective-permute-start.3) | collective-permute-done | bytes 196640 | tf_op jit(solution)/shard_map/ppermute | solution.py:102
  44.0 2.4 collective-permute-start.4
  50.5 12.4 %collective-permute-done.4 = bf16[2,64,1536]{2,1,0:T(8,128)(2,1)S(1)} collective-permute-done((bf16[2,64,1536]{2,1,0:T(8,128)(2,1)S(1)}, bf16[2,64,1536]{2,1,0:T(8,128)(2,1)S(1)}, u32[]{:S(2)}, u32[]{:S(2)}) %collective-permute-start.4) | collective-permute-done | bytes 393248 | tf_op jit(solution)/shard_map/ppermute | solution.py:102
  67.3 4.4 %collective-permute-start.13 = (bf16[128,512]{1,0:T(8,128)(2,1)S(1)}, bf16[128,512]{1,0:T(8,128)(2,1)S(1)}, u32[]{:S(2)}, u32[]{:S(2)}) collective-permute-start(bf16[128,512]{1,0:T(8,128)(2,1)S(1)} %get-tuple-element.154.refs_0_), channel_id=1, source_target_pairs={{0,4},{2,6},{1,5},{3,7},{8,12},{10,14},{9,13},{11,15},{16,20},{18,... | collective-permute-start | bytes 393224 | tf_op jit(solution)/shard_map/ppermute | solution.py:69
  73.2 4.9 %collective-permute-done.10 = bf16[4,64,768]{2,1,0:T(8,128)(2,1)S(1)} collective-permute-done((bf16[4,64,768]{2,1,0:T(8,128)(2,1)S(1)}, bf16[4,64,768]{2,1,0:T(8,128)(2,1)S(1)}, u32[]{:S(2)}, u32[]{:S(2)}) %collective-permute-start.10) | collective-permute-done | bytes 393248 | tf_op jit(solution)/shard_map/ppermute | solution.py:63
  78.2 5.9 %collective-permute-done.11 = bf16[4,64,768]{2,1,0:T(8,128)(2,1)S(1)} collective-permute-done((bf16[4,64,768]{2,1,0:T(8,128)(2,1)S(1)}, bf16[4,64,768]{2,1,0:T(8,128)(2,1)S(1)}, u32[]{:S(2)}, u32[]{:S(2)}) %collective-permute-start.11) | collective-permute-done | bytes 393248 | tf_op jit(solution)/shard_map/ppermute | solution.py:63
  84.2 4.0 collective-permute-start.17
  88.2 2.1 collective-permute-start.16
  94.1 3.4 collective-permute-start.18
  97.5 8.6 %shard_map.326 = (bf16[256,512]{1,0:T(8,128)(2,1)S(1)}, f32[4,8,512]{2,1,0:T(8,128)S(1)}) custom-call(bf16[256,512]{1,0:T(8,128)(2,1)S(1)} %get-tuple-element.153.q_ref, s32[8,512]{1,0:T(8,128)S(1)} %broadcast_in_dim.58.low_ref, bf16[128,512]{1,0:T(8,128)(2,1)S(1)} %get-tuple-element.154.refs_0_, bf16[128,512]{1,0:T(8,128)(2,1)S(1)} %collective-permute-done.12.refs_1_, ...), custom_call_target="tpu_custom_call" | custom-call | flops 4499999744 | bytes 1000 | tf_op jit(solution)/shard_map/pallas_call | solution.py:202
  106.1 16.8 %collective-permute-done.18 = bf16[2,64,1024]{2,1,0:T(8,128)(2,1)S(1)} collective-permute-done((bf16[2,64,1024]{2,1,0:T(8,128)(2,1)S(1)}, bf16[2,64,1024]{2,1,0:T(8,128)(2,1)S(1)}, u32[]{:S(2)}, u32[]{:S(2)}) %collective-permute-start.18) | collective-permute-done | bytes 262176 | tf_op jit(solution)/shard_map/ppermute | solution.py:102
  123.8 2.7 fusion.60
  128.9 6.7 %shard_map.327 = (f32[768,512]{1,0:T(8,128)S(1)}, f32[512,128]{1,0:T(8,128)S(1)}, f32[512,128]{1,0:T(8,128)S(1)}, f32[128,512]{1,0:T(8,128)S(1)}, f32[128,512]{1...) custom-call(f32[768,640]{1,0:T(8,128)S(1)} %slice.223.u_ref, ...), custom_call_target="tpu_custom_call" | custom-call | flops 3500000000 | bytes 1000 | tf_op jit(solution)/shard_map/pallas_call | solution.py:202
  137.9 3.9 collective-permute-start.21
  141.8 5.3 %collective-permute-start.22 = (bf16[800,128]{1,0:T(8,128)(2,1)S(1)}, bf16[800,128]{1,0:T(8,128)(2,1)S(1)}, u32[]{:S(2)}, u32[]{:S(2)}) collective-permute-start(bf16[800,128]{1,0:T(8,128)(2,1)S(1)} %get-tuple-element.173), channel_id=1, source_target_pairs={{0,4},{2,6},{1,5},{3,7},{8,12},{10,14},{9,13},{11,15},{16,20},{18,... | collective-permute-start | bytes 614408 | tf_op jit(solution)/shard_map/ppermute | solution.py:69
  148.9 3.8 collective-permute-done.22.refs_1_
  152.7 3.6 collective-permute-done.23.refs_2_
  156.4 2.3 shard_map.328
  159.1 2.2 collective-permute-start.26
  163.0 10.9 %collective-permute-done.26 = bf16[2,4,64,512]{3,2,1,0:T(8,128)(2,1)S(1)} collective-permute-done((bf16[2,4,64,512]{3,2,1,0:T(8,128)(2,1)S(1)}, bf16[2,4,64,512]{3,2,1,0:T(8,128)(2,1)S(1)}, u32[]{:S(2)}, u32[]{:S(2)}) %collective-permute-start.26) | collective-permute-done | bytes 524320 | tf_op jit(solution)/shard_map/ppermute | solution.py:63
  180.7 6.2 %fusion.56 = (bf16[512,2048]{1,0:T(8,128)(2,1)}, f32[512,2048]{1,0:T(8,128)S(1)}) fusion(bf16[512,1024]{1,0:T(8,128)(2,1)S(1)} %multiply_convert_fusion.n2_ref, bf16[1024,3072]{1,0:T(8,128)(2,1)} %all-gather.2.cloned.1.call-done), kind=kOutput, calls=%fused_computation.188 | convolution fusion | flops 2148532224 | bytes 11534336 | tf_op jit(solution)/shard_map/dot_general | solution.py:27
  187.5 4.5 %fusion.57 = (bf16[512,1024]{1,0:T(8,128)(2,1)}, f32[512,1024]{1,0:T(8,128)}) fusion(bf16[512,1024]{1,0:T(8,128)(2,1)S(1)} %fusion.12.m_ref, bf16[1024,3072]{1,0:T(8,128)(2,1)} %all-gather.2.cloned.1.call-done), kind=kOutput, calls=%fused_computation.189 | convolution fusion | flops 1074266112 | bytes 6291456 | tf_op jit(solution)/shard_map/dot_general | solution.py:27
  195.1 3.8 multiply_reduce_fusion
  198.9 2.1 fusion.50
  201.0 4.2 %fusion.9 = (bf16[512,1024]{1,0:T(8,128)(2,1)S(1)}, bf16[512,1024]{1,0:T(8,128)(2,1)S(1)}) fusion(bf16[512,2048]{1,0:T(8,128)(2,1)S(1)} %copy-done.120, bf16[512,1024]{1,0:T(8,128)(2,1)S(1)} %get-tuple-element.298.e_ref, bf16[1024,3072]{1,0:T(8,128)(2,1)} %all-gather.2.cloned.1.call-done), kind=kOutput, calls=%fused_computation.13 | convolution fusion | flops 1081606144 | bytes 7340032 | tf_op jit(solution)/shard_map/dot_general | solution.py:27
  205.4 4.0 fusion.58
  209.4 4.4 %shard_map.335 = bf16[1024,3072]{1,0:T(8,128)(2,1)S(1)} custom-call(bf16[512,1024]{1,0:T(8,128)(2,1)S(1)} %copy-done.19, bf16[512,1024]{1,0:T(8,128)(2,1)S(1)} %get-tuple-element.298.e_ref, bf16[512,2048]{1,0:T(8,128)(2,1)S(1)} %pad_maximum_fusion.2.ggu_ref, bf16[512,1024]{1,0:T(8,128)(2,1)S(1)} %fusion.12.m_ref), custom_call_target="tpu_custom_call" | custom-call | flops 2000000000 | bytes 1000 | tf_op jit(solution)/shard_map/pallas_call | solution.py:977
  213.8 2.7 copy-done.2
  230.9 3.2 shard_map.330
  240.5 13.2 %shard_map.331 = (bf16[256,512]{1,0:T(8,128)(2,1)S(1)}, bf16[128,512]{1,0:T(8,128)(2,1)S(1)}, bf16[128,512]{1,0:T(8,128)(2,1)S(1)}, bf16[128,512]{1,0:T(8,128)(2,1)S(1)}, bf16[128,512]{1,0:T(8,128)(2,1)S(1)}) custom-call(bf16[256,512]{1,0:T(8,128)(2,1)S(1)} %copy-done.60, s32[8,512]{1,0:T(8,128)S(1)} %copy-done.54, bf16[256,512]{1,0:T(8,128)(2,1)S(1)} %copy-done.87, ...), custom_call_target="tpu_custom_call" | custom-call | flops 7000000000 | bytes 1000 | tf_op jit(solution)/shard_map/pallas_call | solution.py:202
  253.8 10.6 %collective-permute-done.34 = bf16[2,4,64,512]{3,2,1,0:T(8,128)(2,1)S(1)} collective-permute-done((bf16[2,4,64,512]{3,2,1,0:T(8,128)(2,1)S(1)}, bf16[2,4,64,512]{3,2,1,0:T(8,128)(2,1)S(1)}, u32[]{:S(2)}, u32[]{:S(2)}) %collective-permute-start.34) | collective-permute-done | bytes 524320 | tf_op jit(solution)/shard_map/ppermute | solution.py:63
  271.4 13.4 %shard_map.332 = (f32[768,512]{1,0:T(8,128)S(1)}, f32[256,512]{1,0:T(8,128)S(1)}, f32[16,512]{1,0:T(8,128)S(1)}, f32[8,128]{1,0:T(8,128)S(1)}) custom-call(f32[768,512]{1,0:T(8,128)S(1)} %get-tuple-element.197.gy_ref, f32[768,512]{1,0:T(8,128)S(1)} %copy-done.77, f32[512,128]{1,0:T(8,128)S(1)} %copy-done.81, f32[512,128]{1,0:T(8,128)S(1)} %copy-done.40, ...), custom_call_target="tpu_custom_call" | custom-call | flops 6499999744 | bytes 1000 | tf_op jit(solution)/shard_map/pallas_call | solution.py:202
  284.8 4.0 shard_map.333
  293.2 8.8 %shard_map.334 = (f32[1024,512]{1,0:T(8,128)S(1)}, f32[8,1024]{1,0:T(8,128)}, f32[768,128]{1,0:T(8,128)S(1)}, f32[256,128]{1,0:T(8,128)S(1)}) custom-call(f32[768,640]{1,0:T(8,128)S(1)} %copy-done.28, f32[768,640]{1,0:T(8,128)S(1)} %copy-done.26, f32[768,512]{1,0:T(8,128)S(1)} %get-tuple-element.212.gxs_ref, f32[256,512]{1,0:T(8,128)S(1)} %get-tuple-element.213.gbc_ref, ...), custom_call_target="tpu_custom_call" | custom-call | flops 4000000000 | bytes 1000 | tf_op jit(solution)/shard_map/pallas_call | solution.py:202
  306.3 3.9 collective-permute-done.40
  313.1 2.3 fusion.22
  327.5 5.0 %shard_map.337 = (bf16[1024,1152]{1,0:T(8,128)(2,1)S(1)}, bf16[1024,512]{1,0:T(8,128)(2,1)S(1)}, f32[1024,128]{1,0:T(8,128)}) custom-call(bf16[1024,640]{1,0:T(8,128)(2,1)S(1)} %copy-done.15, bf16[1024,640]{1,0:T(8,128)(2,1)S(1)} %copy-done.12, f32[8,640]{1,0:T(8,128)S(1)} %copy-done.44, bf16[1152,512]{1,0:T(8,128)(2,1)S(1)} %shard_map.336.g_ref, ...), custom_call_target="tpu_custom_call" | custom-call | flops 2000000000 | bytes 1000 | tf_op jit(solution)/shard_map/pallas_call | solution.py:835
  335.4 9.1 %collective-permute-done.46 = bf16[2,4,64,512]{3,2,1,0:T(8,128)(2,1)S(1)} collective-permute-done((bf16[2,4,64,512]{3,2,1,0:T(8,128)(2,1)S(1)}, bf16[2,4,64,512]{3,2,1,0:T(8,128)(2,1)S(1)}, u32[]{:S(2)}, u32[]{:S(2)}) %collective-permute-start.46) | collective-permute-done | bytes 524320 | tf_op jit(solution)/shard_map/ppermute | solution.py:63
  345.7 5.8 %collective-permute-done.48 = bf16[2,4,64,640]{3,2,1,0:T(8,128)(2,1)S(1)} collective-permute-done((bf16[2,4,64,640]{3,2,1,0:T(8,128)(2,1)S(1)}, bf16[2,4,64,640]{3,2,1,0:T(8,128)(2,1)S(1)}, u32[]{:S(2)}, u32[]{:S(2)}) %collective-permute-start.48) | collective-permute-done | bytes 655392 | tf_op jit(solution)/shard_map/ppermute | solution.py:63
  352.7 2.5 collective-permute-start.50
  355.3 3.9 collective-permute-done.49
  359.6 2.5 shard_map.338
  366.0 8.8 %collective-permute-done.50 = bf16[2,64,2176]{2,1,0:T(8,128)(2,1)S(1)} collective-permute-done((bf16[2,64,2176]{2,1,0:T(8,128)(2,1)S(1)}, bf16[2,64,2176]{2,1,0:T(8,128)(2,1)S(1)}, u32[]{:S(2)}, u32[]{:S(2)}) %collective-permute-start.50) | collective-permute-done | bytes 557088 | tf_op jit(solution)/shard_map/ppermute | solution.py:169
  374.9 2.3 collective-permute-start.54
  378.1 2.9 collective-permute-start.56
  381.7 6.7 %collective-permute-done.53 = bf16[64,1152]{1,0:T(8,128)(2,1)S(1)} collective-permute-done((bf16[64,1152]{1,0:T(8,128)(2,1)S(1)}, bf16[64,1152]{1,0:T(8,128)(2,1)S(1)}, u32[]{:S(2)}, u32[]{:S(2)}) %collective-permute-start.53) | collective-permute-done | bytes 147488 | tf_op jit(solution)/shard_map/ppermute | solution.py:63
  (481 shorter events, 122.2 us)
Async XLA Ops:
  7.2 173.5 %all-gather.2.cloned.1.call-start = ((), (), s32[]{:S(2)}) async-start(), calls=%async_computation.2 | async-start | bytes 6684672 | tf_op jit(solution)/shard_map/all_gather | solution.py:1081
  14.0 12.3 %collective-permute-start = (bf16[64,768]{1,0:T(8,128)(2,1)S(1)}, bf16[64,768]{1,0:T(8,128)(2,1)S(1)}, u32[]{:S(2)}, u32[]{:S(2)}) collective-permute-start(bf16[64,768]{1,0:T(8,128)(2,1)S(1)} %shard_map.322), channel_id=1, source_target_pairs={{0,6},{2,0},{4,2},{6,4},{1,7},{3,1},{5,3},{7,5},{8,14},{10,8},{12,... | collective-permute-start | bytes 294920 | tf_op jit(solution)/shard_map/ppermute | solution.py:63
  19.1 8.7 %collective-permute-start.1 = (bf16[64,768]{1,0:T(8,128)(2,1)S(1)}, bf16[64,768]{1,0:T(8,128)(2,1)S(1)}, u32[]{:S(2)}, u32[]{:S(2)}) collective-permute-start(bf16[64,768]{1,0:T(8,128)(2,1)S(1)} %shard_map.322), channel_id=1, source_target_pairs={{0,4},{2,6},{4,0},{6,2},{1,5},{3,7},{5,1},{7,3},{8,12},{10,14},{12... | collective-permute-start | bytes 294920 | tf_op jit(solution)/shard_map/ppermute | solution.py:63
  19.1 8.8 %collective-permute-start.2 = (bf16[64,768]{1,0:T(8,128)(2,1)S(1)}, bf16[64,768]{1,0:T(8,128)(2,1)S(1)}, u32[]{:S(2)}, u32[]{:S(2)}) collective-permute-start(bf16[64,768]{1,0:T(8,128)(2,1)S(1)} %shard_map.322), channel_id=1, source_target_pairs={{0,2},{2,4},{4,6},{6,0},{1,3},{3,5},{5,7},{7,1},{8,10},{10,12},{12... | collective-permute-start | bytes 294920 | tf_op jit(solution)/shard_map/ppermute | solution.py:63
  20.8 10.9 %collective-permute-start.5 = (bf16[16,1024]{1,0:T(8,128)(2,1)S(1)}, bf16[16,1024]{1,0:T(8,128)(2,1)S(1)}, u32[]{:S(2)}, u32[]{:S(2)}) collective-permute-start(bf16[16,1024]{1,0:T(8,128)(2,1)S(1)} %slice_bitcast_fusion.4), channel_id=1, source_target_pairs={{0,2},{2,4},{4,6},{1,3},{3,5},{5,7},{8,10},{10,12},{12,14},{9,11},... | collective-permute-start | bytes 98312 | tf_op jit(solution)/shard_map/ppermute | solution.py:69
  26.1 285.1 %reduce-scatter.3.cloned.1.call-start = ((), (), s32[]{:S(2)}) async-start(), calls=%async_computation.3 | async-start | bytes 7864320 | tf_op jit(solution)/shard_map/reduce_scatter | solution.py:1153
  32.4 11.6 %collective-permute-start.3 = (bf16[1,64,1536]{2,1,0:T(8,128)(2,1)S(1)}, bf16[1,64,1536]{2,1,0:T(8,128)(2,1)S(1)}, u32[]{:S(2)}, u32[]{:S(2)}) collective-permute-start(bf16[1,64,1536]{2,1,0:T(8,128)(2,1)S(1)} %bitcast.223), channel_id=1, source_target_pairs={{0,2},{2,0},{4,6},{6,4},{1,3},{3,1},{5,7},{7,5},{8,10},{10,8},{12,... | collective-permute-start | bytes 589832 | tf_op jit(solution)/shard_map/ppermute | solution.py:102
  34.6 12.5 %collective-permute-start.9 = (bf16[2,4,64,384]{3,2,1,0:T(8,128)(2,1)S(1)}, bf16[2,4,64,384]{3,2,1,0:T(8,128)(2,1)S(1)}, u32[]{:S(2)}, u32[]{:S(2)}) collective-permute-start(bf16[2,4,64,384]{3,2,1,0:T(8,128)(2,1)S(1)} %maximum_select_fusion.15), channel_id=1, source_target_pairs={{0,16},{8,24},{16,0},{24,8},{1,17},{9,25},{17,1},{25,9},{2,18},{10... | collective-permute-start | bytes 1179656 | tf_op jit(solution)/shard_map/ppermute | solution.py:63
  36.9 10.5 %collective-permute-start.7 = (bf16[2,4,64,384]{3,2,1,0:T(8,128)(2,1)S(1)}, bf16[2,4,64,384]{3,2,1,0:T(8,128)(2,1)S(1)}, u32[]{:S(2)}, u32[]{:S(2)}) collective-permute-start(bf16[2,4,64,384]{3,2,1,0:T(8,128)(2,1)S(1)} %maximum_select_fusion.13), channel_id=1, source_target_pairs={{0,8},{8,0},{16,24},{24,16},{1,9},{9,1},{17,25},{25,17},{2,10},{10... | collective-permute-start | bytes 1179656 | tf_op jit(solution)/shard_map/ppermute | solution.py:63
  44.0 18.9 %collective-permute-start.4 = (bf16[2,64,1536]{2,1,0:T(8,128)(2,1)S(1)}, bf16[2,64,1536]{2,1,0:T(8,128)(2,1)S(1)}, u32[]{:S(2)}, u32[]{:S(2)}) collective-permute-start(bf16[2,64,1536]{2,1,0:T(8,128)(2,1)S(1)} %maximum_select_fusion.12), channel_id=1, source_target_pairs={{0,4},{2,6},{4,0},{6,2},{1,5},{3,7},{5,1},{7,3},{8,12},{10,14},{12... | collective-permute-start | bytes 1179656 | tf_op jit(solution)/shard_map/ppermute | solution.py:102
  63.2 14.9 %collective-permute-start.10 = (bf16[4,64,768]{2,1,0:T(8,128)(2,1)S(1)}, bf16[4,64,768]{2,1,0:T(8,128)(2,1)S(1)}, u32[]{:S(2)}, u32[]{:S(2)}) collective-permute-start(bf16[4,64,768]{2,1,0:T(8,128)(2,1)S(1)} %get-tuple-element.312), channel_id=1, source_target_pairs={{0,16},{8,24},{16,0},{24,8},{1,17},{9,25},{17,1},{25,9},{2,18},{10... | collective-permute-start | bytes 1179656 | tf_op jit(solution)/shard_map/ppermute | solution.py:63
  64.5 19.6 %collective-permute-start.11 = (bf16[4,64,768]{2,1,0:T(8,128)(2,1)S(1)}, bf16[4,64,768]{2,1,0:T(8,128)(2,1)S(1)}, u32[]{:S(2)}, u32[]{:S(2)}) collective-permute-start(bf16[4,64,768]{2,1,0:T(8,128)(2,1)S(1)} %get-tuple-element.311), channel_id=1, source_target_pairs={{0,8},{8,0},{16,24},{24,16},{1,9},{9,1},{17,25},{25,17},{2,10},{10... | collective-permute-start | bytes 1179656 | tf_op jit(solution)/shard_map/ppermute | solution.py:63
  66.0 18.2 %collective-permute-start.12 = (bf16[128,512]{1,0:T(8,128)(2,1)S(1)}, bf16[128,512]{1,0:T(8,128)(2,1)S(1)}, u32[]{:S(2)}, u32[]{:S(2)}) collective-permute-start(bf16[128,512]{1,0:T(8,128)(2,1)S(1)} %get-tuple-element.154.refs_0_), channel_id=1, source_target_pairs={{0,2},{2,4},{4,6},{1,3},{3,5},{5,7},{8,10},{10,12},{12,14},{9,11},... | collective-permute-start | bytes 393224 | tf_op jit(solution)/shard_map/ppermute | solution.py:69
  67.3 16.9 %collective-permute-start.13 = (bf16[128,512]{1,0:T(8,128)(2,1)S(1)}, bf16[128,512]{1,0:T(8,128)(2,1)S(1)}, u32[]{:S(2)}, u32[]{:S(2)}) collective-permute-start(bf16[128,512]{1,0:T(8,128)(2,1)S(1)} %get-tuple-element.154.refs_0_), channel_id=1, source_target_pairs={{0,4},{2,6},{1,5},{3,7},{8,12},{10,14},{9,13},{11,15},{16,20},{18,... | collective-permute-start | bytes 393224 | tf_op jit(solution)/shard_map/ppermute | solution.py:69
  71.7 12.6 %collective-permute-start.14 = (bf16[128,512]{1,0:T(8,128)(2,1)S(1)}, bf16[128,512]{1,0:T(8,128)(2,1)S(1)}, u32[]{:S(2)}, u32[]{:S(2)}) collective-permute-start(bf16[128,512]{1,0:T(8,128)(2,1)S(1)} %get-tuple-element.154.refs_0_), channel_id=1, source_target_pairs={{0,6},{1,7},{8,14},{9,15},{16,22},{17,23},{24,30},{25,31}} | collective-permute-start | bytes 393224 | tf_op jit(solution)/shard_map/ppermute | solution.py:69
  84.2 9.8 %collective-permute-start.17 = (bf16[1,64,1024]{2,1,0:T(8,128)(2,1)S(1)}, bf16[1,64,1024]{2,1,0:T(8,128)(2,1)S(1)}, u32[]{:S(2)}, u32[]{:S(2)}) collective-permute-start(bf16[1,64,1024]{2,1,0:T(8,128)(2,1)S(1)} %bitcast.232), channel_id=1, source_target_pairs={{0,2},{2,0},{4,6},{6,4},{1,3},{3,1},{5,7},{7,5},{8,10},{10,8},{12,... | collective-permute-start | bytes 393224 | tf_op jit(solution)/shard_map/ppermute | solution.py:102
  88.2 34.8 %collective-permute-start.16 = (bf16[2,4,64,768]{3,2,1,0:T(8,128)(2,1)S(1)}, bf16[2,4,64,768]{3,2,1,0:T(8,128)(2,1)S(1)}, u32[]{:S(2)}, u32[]{:S(2)}) collective-permute-start(bf16[2,4,64,768]{3,2,1,0:T(8,128)(2,1)S(1)} %maximum_select_fusion.8), channel_id=1, source_target_pairs={{0,16},{8,24},{16,0},{24,8},{1,17},{9,25},{17,1},{25,9},{2,18},{10... | collective-permute-start | bytes 2359304 | tf_op jit(solution)/shard_map/ppermute | solution.py:63
  90.3 33.0 %collective-permute-start.15 = (bf16[2,4,64,768]{3,2,1,0:T(8,128)(2,1)S(1)}, bf16[2,4,64,768]{3,2,1,0:T(8,128)(2,1)S(1)}, u32[]{:S(2)}, u32[]{:S(2)}) collective-permute-start(bf16[2,4,64,768]{3,2,1,0:T(8,128)(2,1)S(1)} %maximum_select_fusion.7), channel_id=1, source_target_pairs={{0,8},{8,0},{16,24},{24,16},{1,9},{9,1},{17,25},{25,17},{2,10},{10... | collective-permute-start | bytes 2359304 | tf_op jit(solution)/shard_map/ppermute | solution.py:63
  94.1 28.8 %collective-permute-start.18 = (bf16[2,64,1024]{2,1,0:T(8,128)(2,1)S(1)}, bf16[2,64,1024]{2,1,0:T(8,128)(2,1)S(1)}, u32[]{:S(2)}, u32[]{:S(2)}) collective-permute-start(bf16[2,64,1024]{2,1,0:T(8,128)(2,1)S(1)} %maximum_select_fusion.16), channel_id=1, source_target_pairs={{0,4},{2,6},{4,0},{6,2},{1,5},{3,7},{5,1},{7,3},{8,12},{10,14},{12... | collective-permute-start | bytes 786440 | tf_op jit(solution)/shard_map/ppermute | solution.py:102
  126.7 22.0 %collective-permute-start.19 = (bf16[4,64,512]{2,1,0:T(8,128)(2,1)S(1)}, bf16[4,64,512]{2,1,0:T(8,128)(2,1)S(1)}, u32[]{:S(2)}, u32[]{:S(2)}) collective-permute-start(bf16[4,64,512]{2,1,0:T(8,128)(2,1)S(1)} %get-tuple-element.327), channel_id=1, source_target_pairs={{0,16},{8,24},{16,0},{24,8},{1,17},{9,25},{17,1},{25,9},{2,18},{10... | collective-permute-start | bytes 786440 | tf_op jit(solution)/shard_map/ppermute | solution.py:63
  127.2 21.6 %collective-permute-start.20 = (bf16[4,64,512]{2,1,0:T(8,128)(2,1)S(1)}, bf16[4,64,512]{2,1,0:T(8,128)(2,1)S(1)}, u32[]{:S(2)}, u32[]{:S(2)}) collective-permute-start(bf16[4,64,512]{2,1,0:T(8,128)(2,1)S(1)} %get-tuple-element.326), channel_id=1, source_target_pairs={{0,8},{8,0},{16,24},{24,16},{1,9},{9,1},{17,25},{25,17},{2,10},{10... | collective-permute-start | bytes 786440 | tf_op jit(solution)/shard_map/ppermute | solution.py:63
  137.9 11.0 %collective-permute-start.21 = (bf16[800,128]{1,0:T(8,128)(2,1)S(1)}, bf16[800,128]{1,0:T(8,128)(2,1)S(1)}, u32[]{:S(2)}, u32[]{:S(2)}) collective-permute-start(bf16[800,128]{1,0:T(8,128)(2,1)S(1)} %get-tuple-element.173), channel_id=1, source_target_pairs={{0,2},{2,4},{4,6},{1,3},{3,5},{5,7},{8,10},{10,12},{12,14},{9,11},... | collective-permute-start | bytes 614408 | tf_op jit(solution)/shard_map/ppermute | solution.py:69
  141.8 10.9 %collective-permute-start.22 = (bf16[800,128]{1,0:T(8,128)(2,1)S(1)}, bf16[800,128]{1,0:T(8,128)(2,1)S(1)}, u32[]{:S(2)}, u32[]{:S(2)}) collective-permute-start(bf16[800,128]{1,0:T(8,128)(2,1)S(1)} %get-tuple-element.173), channel_id=1, source_target_pairs={{0,4},{2,6},{1,5},{3,7},{8,12},{10,14},{9,13},{11,15},{16,20},{18,... | collective-permute-start | bytes 614408 | tf_op jit(solution)/shard_map/ppermute | solution.py:69
  147.1 9.2 %collective-permute-start.23 = (bf16[800,128]{1,0:T(8,128)(2,1)S(1)}, bf16[800,128]{1,0:T(8,128)(2,1)S(1)}, u32[]{:S(2)}, u32[]{:S(2)}) collective-permute-start(bf16[800,128]{1,0:T(8,128)(2,1)S(1)} %get-tuple-element.173), channel_id=1, source_target_pairs={{0,6},{1,7},{8,14},{9,15},{16,22},{17,23},{24,30},{25,31}} | collective-permute-start | bytes 614408 | tf_op jit(solution)/shard_map/ppermute | solution.py:69
  159.1 14.8 %collective-permute-start.26 = (bf16[2,4,64,512]{3,2,1,0:T(8,128)(2,1)S(1)}, bf16[2,4,64,512]{3,2,1,0:T(8,128)(2,1)S(1)}, u32[]{:S(2)}, u32[]{:S(2)}) collective-permute-start(bf16[2,4,64,512]{3,2,1,0:T(8,128)(2,1)S(1)} %maximum_select_fusion.11), channel_id=1, source_target_pairs={{0,16},{8,24},{16,0},{24,8},{1,17},{9,25},{17,1},{25,9},{2,18},{10... | collective-permute-start | bytes 1572872 | tf_op jit(solution)/shard_map/ppermute | solution.py:63
  161.3 14.0 %collective-permute-start.25 = (bf16[2,4,64,512]{3,2,1,0:T(8,128)(2,1)S(1)}, bf16[2,4,64,512]{3,2,1,0:T(8,128)(2,1)S(1)}, u32[]{:S(2)}, u32[]{:S(2)}) collective-permute-start(bf16[2,4,64,512]{3,2,1,0:T(8,128)(2,1)S(1)} %maximum_select_fusion.10), channel_id=1, source_target_pairs={{0,8},{8,0},{16,24},{24,16},{1,9},{9,1},{17,25},{25,17},{2,10},{10... | collective-permute-start | bytes 1572872 | tf_op jit(solution)/shard_map/ppermute | solution.py:63
  216.5 145.6 %reduce-scatter.5.cloned.1.call-start = ((), (), s32[]{:S(2)}) async-start(), calls=%async_computation.4 | async-start | bytes 1966080 | tf_op jit(solution)/shard_map/reduce_scatter | solution.py:1183
  234.1 31.5 %collective-permute-start.31 = (bf16[800,128]{1,0:T(8,128)(2,1)S(1)}, bf16[800,128]{1,0:T(8,128)(2,1)S(1)}, u32[]{:S(2)}, u32[]{:S(2)}) collective-permute-start(bf16[800,128]{1,0:T(8,128)(2,1)S(1)} %get-tuple-element.185), channel_id=1, source_target_pairs={{2,0},{4,2},{6,4},{3,1},{5,3},{7,5},{10,8},{12,10},{14,12},{11,9},... | collective-permute-start | bytes 614408 | tf_op jit(solution)/shard_map/ppermute | solution.py:69
  235.4 30.2 %collective-permute-start.32 = (bf16[800,128]{1,0:T(8,128)(2,1)S(1)}, bf16[800,128]{1,0:T(8,128)(2,1)S(1)}, u32[]{:S(2)}, u32[]{:S(2)}) collective-permute-start(bf16[800,128]{1,0:T(8,128)(2,1)S(1)} %get-tuple-element.185), channel_id=1, source_target_pairs={{4,0},{6,2},{5,1},{7,3},{12,8},{14,10},{13,9},{15,11},{20,16},{22,... | collective-permute-start | bytes 614408 | tf_op jit(solution)/shard_map/ppermute | solution.py:69
  236.7 28.9 %collective-permute-start.33 = (bf16[800,128]{1,0:T(8,128)(2,1)S(1)}, bf16[800,128]{1,0:T(8,128)(2,1)S(1)}, u32[]{:S(2)}, u32[]{:S(2)}) collective-permute-start(bf16[800,128]{1,0:T(8,128)(2,1)S(1)} %get-tuple-element.185), channel_id=1, source_target_pairs={{6,0},{7,1},{14,8},{15,9},{22,16},{23,17},{30,24},{31,25}} | collective-permute-start | bytes 614408 | tf_op jit(solution)/shard_map/ppermute | solution.py:69
  238.5 25.9 %collective-permute-start.34 = (bf16[2,4,64,512]{3,2,1,0:T(8,128)(2,1)S(1)}, bf16[2,4,64,512]{3,2,1,0:T(8,128)(2,1)S(1)}, u32[]{:S(2)}, u32[]{:S(2)}) collective-permute-start(bf16[2,4,64,512]{3,2,1,0:T(8,128)(2,1)S(1)} %dynamic-slice_bitcast_fusion.5), channel_id=1, source_target_pairs={{0,8},{8,0},{16,24},{24,16},{1,9},{9,1},{17,25},{25,17},{2,10},{10... | collective-permute-start | bytes 1572872 | tf_op jit(solution)/shard_map/ppermute | solution.py:63
  239.6 25.8 %collective-permute-start.35 = (bf16[2,4,64,512]{3,2,1,0:T(8,128)(2,1)S(1)}, bf16[2,4,64,512]{3,2,1,0:T(8,128)(2,1)S(1)}, u32[]{:S(2)}, u32[]{:S(2)}) collective-permute-start(bf16[2,4,64,512]{3,2,1,0:T(8,128)(2,1)S(1)} %dynamic-slice_bitcast_fusion.4), channel_id=1, source_target_pairs={{0,16},{8,24},{16,0},{24,8},{1,17},{9,25},{17,1},{25,9},{2,18},{10... | collective-permute-start | bytes 1572872 | tf_op jit(solution)/shard_map/ppermute | solution.py:63
  265.6 19.2 %collective-permute-start.36 = (bf16[128,512]{1,0:T(8,128)(2,1)S(1)}, bf16[128,512]{1,0:T(8,128)(2,1)S(1)}, u32[]{:S(2)}, u32[]{:S(2)}) collective-permute-start(bf16[128,512]{1,0:T(8,128)(2,1)S(1)} %get-tuple-element.194), channel_id=1, source_target_pairs={{2,0},{4,2},{6,4},{3,1},{5,3},{7,5},{10,8},{12,10},{14,12},{11,9},... | collective-permute-start | bytes 393224 | tf_op jit(solution)/shard_map/ppermute | solution.py:69
  266.9 17.9 %collective-permute-start.37 = (bf16[128,512]{1,0:T(8,128)(2,1)S(1)}, bf16[128,512]{1,0:T(8,128)(2,1)S(1)}, u32[]{:S(2)}, u32[]{:S(2)}) collective-permute-start(bf16[128,512]{1,0:T(8,128)(2,1)S(1)} %get-tuple-element.195), channel_id=1, source_target_pairs={{4,0},{6,2},{5,1},{7,3},{12,8},{14,10},{13,9},{15,11},{20,16},{22,... | collective-permute-start | bytes 393224 | tf_op jit(solution)/shard_map/ppermute | solution.py:69
  268.2 16.6 %collective-permute-start.38 = (bf16[128,512]{1,0:T(8,128)(2,1)S(1)}, bf16[128,512]{1,0:T(8,128)(2,1)S(1)}, u32[]{:S(2)}, u32[]{:S(2)}) collective-permute-start(bf16[128,512]{1,0:T(8,128)(2,1)S(1)} %get-tuple-element.196), channel_id=1, source_target_pairs={{6,0},{7,1},{14,8},{15,9},{22,16},{23,17},{30,24},{31,25}} | collective-permute-start | bytes 393224 | tf_op jit(solution)/shard_map/ppermute | solution.py:69
  269.5 35.2 %collective-permute-start.42 = (bf16[4,64,512]{2,1,0:T(8,128)(2,1)S(1)}, bf16[4,64,512]{2,1,0:T(8,128)(2,1)S(1)}, u32[]{:S(2)}, u32[]{:S(2)}) collective-permute-start(bf16[4,64,512]{2,1,0:T(8,128)(2,1)S(1)} %dynamic-slice_bitcast_fusion.10), channel_id=1, source_target_pairs={{0,16},{8,24},{16,0},{24,8},{1,17},{9,25},{17,1},{25,9},{2,18},{10... | collective-permute-start | bytes 786440 | tf_op jit(solution)/shard_map/ppermute | solution.py:63
  270.3 35.2 %collective-permute-start.43 = (bf16[4,64,512]{2,1,0:T(8,128)(2,1)S(1)}, bf16[4,64,512]{2,1,0:T(8,128)(2,1)S(1)}, u32[]{:S(2)}, u32[]{:S(2)}) collective-permute-start(bf16[4,64,512]{2,1,0:T(8,128)(2,1)S(1)} %dynamic-slice_bitcast_fusion.9), channel_id=1, source_target_pairs={{0,8},{8,0},{16,24},{24,16},{1,9},{9,1},{17,25},{25,17},{2,10},{10... | collective-permute-start | bytes 786440 | tf_op jit(solution)/shard_map/ppermute | solution.py:63
  289.8 20.4 %collective-permute-start.40 = (bf16[2,4,64,512]{3,2,1,0:T(8,128)(2,1)S(1)}, bf16[2,4,64,512]{3,2,1,0:T(8,128)(2,1)S(1)}, u32[]{:S(2)}, u32[]{:S(2)}) collective-permute-start(bf16[2,4,64,512]{3,2,1,0:T(8,128)(2,1)S(1)} %dynamic-slice_bitcast_fusion.3), channel_id=1, source_target_pairs={{0,8},{8,0},{16,24},{24,16},{1,9},{9,1},{17,25},{25,17},{2,10},{10... | collective-permute-start | bytes 1572872 | tf_op jit(solution)/shard_map/ppermute | solution.py:63
  291.9 21.2 %collective-permute-start.41 = (bf16[2,4,64,640]{3,2,1,0:T(8,128)(2,1)}, bf16[2,4,64,640]{3,2,1,0:T(8,128)(2,1)}, u32[]{:S(2)}, u32[]{:S(2)}) collective-permute-start(bf16[2,4,64,640]{3,2,1,0:T(8,128)(2,1)} %dynamic-slice_bitcast_fusion.1), channel_id=1, source_target_pairs={{0,16},{8,24},{16,0},{24,8},{1,17},{9,25},{17,1},{25,9},{2,18},{10... | collective-permute-start | bytes 1966088 | tf_op jit(solution)/shard_map/ppermute | solution.py:63
  318.4 14.2 %collective-permute-start.44 = (bf16[4,64,512]{2,1,0:T(8,128)(2,1)S(1)}, bf16[4,64,512]{2,1,0:T(8,128)(2,1)S(1)}, u32[]{:S(2)}, u32[]{:S(2)}) collective-permute-start(bf16[4,64,512]{2,1,0:T(8,128)(2,1)S(1)} %dynamic-slice_bitcast_fusion.8), channel_id=1, source_target_pairs={{0,16},{8,24},{16,0},{24,8},{1,17},{9,25},{17,1},{25,9},{2,18},{10... | collective-permute-start | bytes 786440 | tf_op jit(solution)/shard_map/ppermute | solution.py:63
  320.9 11.7 %collective-permute-start.45 = (bf16[4,64,640]{2,1,0:T(8,128)(2,1)S(1)}, bf16[4,64,640]{2,1,0:T(8,128)(2,1)S(1)}, u32[]{:S(2)}, u32[]{:S(2)}) collective-permute-start(bf16[4,64,640]{2,1,0:T(8,128)(2,1)S(1)} %dynamic-slice_bitcast_fusion.6), channel_id=1, source_target_pairs={{0,8},{8,0},{16,24},{24,16},{1,9},{9,1},{17,25},{25,17},{2,10},{10... | collective-permute-start | bytes 983048 | tf_op jit(solution)/shard_map/ppermute | solution.py:63
  333.1 11.4 %collective-permute-start.46 = (bf16[2,4,64,512]{3,2,1,0:T(8,128)(2,1)S(1)}, bf16[2,4,64,512]{3,2,1,0:T(8,128)(2,1)S(1)}, u32[]{:S(2)}, u32[]{:S(2)}) collective-permute-start(bf16[2,4,64,512]{3,2,1,0:T(8,128)(2,1)S(1)} %dynamic-slice_bitcast_fusion.2), channel_id=1, source_target_pairs={{0,8},{8,0},{16,24},{24,16},{1,9},{9,1},{17,25},{25,17},{2,10},{10... | collective-permute-start | bytes 1572872 | tf_op jit(solution)/shard_map/ppermute | solution.py:63
  334.5 17.0 %collective-permute-start.48 = (bf16[2,4,64,640]{3,2,1,0:T(8,128)(2,1)S(1)}, bf16[2,4,64,640]{3,2,1,0:T(8,128)(2,1)S(1)}, u32[]{:S(2)}, u32[]{:S(2)}) collective-permute-start(bf16[2,4,64,640]{3,2,1,0:T(8,128)(2,1)S(1)} %dynamic-slice_bitcast_fusion), channel_id=1, source_target_pairs={{0,16},{8,24},{16,0},{24,8},{1,17},{9,25},{17,1},{25,9},{2,18},{10... | collective-permute-start | bytes 1966088 | tf_op jit(solution)/shard_map/ppermute | solution.py:63
  344.7 10.5 %collective-permute-start.47 = (bf16[4,64,512]{2,1,0:T(8,128)(2,1)S(1)}, bf16[4,64,512]{2,1,0:T(8,128)(2,1)S(1)}, u32[]{:S(2)}, u32[]{:S(2)}) collective-permute-start(bf16[4,64,512]{2,1,0:T(8,128)(2,1)S(1)} %dynamic-slice_bitcast_fusion.7), channel_id=1, source_target_pairs={{0,16},{8,24},{16,0},{24,8},{1,17},{9,25},{17,1},{25,9},{2,18},{10... | collective-permute-start | bytes 786440 | tf_op jit(solution)/shard_map/ppermute | solution.py:63
  352.7 22.1 %collective-permute-start.50 = (bf16[2,64,2176]{2,1,0:T(8,128)(2,1)S(1)}, bf16[2,64,2176]{2,1,0:T(8,128)(2,1)S(1)}, u32[]{:S(2)}, u32[]{:S(2)}) collective-permute-start(bf16[2,64,2176]{2,1,0:T(8,128)(2,1)S(1)} %broadcast_select_fusion), channel_id=1, source_target_pairs={{0,4},{2,6},{4,0},{6,2},{1,5},{3,7},{5,1},{7,3},{8,12},{10,14},{12... | collective-permute-start | bytes 1671176 | tf_op jit(solution)/shard_map/ppermute | solution.py:169
  377.2 11.3 %collective-permute-start.53 = (bf16[64,1152]{1,0:T(8,128)(2,1)S(1)}, bf16[64,1152]{1,0:T(8,128)(2,1)S(1)}, u32[]{:S(2)}, u32[]{:S(2)}) collective-permute-start(bf16[64,1152]{1,0:T(8,128)(2,1)S(1)} %get-tuple-element.317), channel_id=1, source_target_pairs={{0,4},{2,6},{4,0},{6,2},{1,5},{3,7},{5,1},{7,3},{8,12},{10,14},{12... | collective-permute-start | bytes 442376 | tf_op jit(solution)/shard_map/ppermute | solution.py:63
  377.2 11.3 %collective-permute-start.52 = (bf16[64,1152]{1,0:T(8,128)(2,1)S(1)}, bf16[64,1152]{1,0:T(8,128)(2,1)S(1)}, u32[]{:S(2)}, u32[]{:S(2)}) collective-permute-start(bf16[64,1152]{1,0:T(8,128)(2,1)S(1)} %get-tuple-element.315), channel_id=1, source_target_pairs={{0,2},{2,4},{4,6},{6,0},{1,3},{3,5},{5,7},{7,1},{8,10},{10,12},{12... | collective-permute-start | bytes 442376 | tf_op jit(solution)/shard_map/ppermute | solution.py:63
  378.1 14.3 %collective-permute-start.56 = (bf16[1,64,2176]{2,1,0:T(8,128)(2,1)S(1)}, bf16[1,64,2176]{2,1,0:T(8,128)(2,1)S(1)}, u32[]{:S(2)}, u32[]{:S(2)}) collective-permute-start(bf16[1,64,2176]{2,1,0:T(8,128)(2,1)S(1)} %broadcast_select_fusion.1), channel_id=1, source_target_pairs={{0,2},{2,0},{4,6},{6,4},{1,3},{3,1},{5,7},{7,5},{8,10},{10,8},{12,... | collective-permute-start | bytes 835592 | tf_op jit(solution)/shard_map/ppermute | solution.py:169
  (135 other events, 1532.2 us)
Sparse Core Ops, SparseCore 0:
  26.2 122.9 all-gather.1
  216.6 91.2 reduce-scatter.2
  315.5 36.3 reduce-scatter.4

commit v3 on v2

--- a/solution.py
+++ b/solution.py
@@ -995,7 +995,7 @@
         total = total + jnp.sum(grad * (res * scale), axis=0, keepdims=True)
         grad = grad * gain_ref[0:1, :]
         inner = jnp.mean(grad * res, axis=1, keepdims=True)
-        grad = gf_ref[rows, :] + scale * grad - scale * scale * scale * res * inner
+        grad = gf_ref[rows, :].astype(f32) + scale * grad - scale * scale * scale * res * inner
         out_ref[rows, :] = grad
         ea_ref[rows, :] = grad.astype(bf16)
     ggain_ref[...] = jnp.broadcast_to(total, ggain_ref.shape)
@@ -1151,7 +1151,7 @@
     loss_row = jnp.where(lax.broadcasted_iota(jnp.int32, (8, 128), 1) == loss_lane, local_sq, 0.0)
     mlp_grads = mlp_weight_grads(normed_two, grad_low, grad_gateup, hidden_mlp)
     mlp_out = lax.psum_scatter(mlp_grads, "fsdp", scatter_dimension=0, tiled=True)
-    grad_residual, grad_out, grad_gain_two = residual_back(part, swapped(low_part), residual, grad_final, gain_two_rows)
+    grad_residual, grad_out, grad_gain_two = residual_back(part, swapped(low_part), residual, grad_low, gain_two_rows)
 
     grad_branches = dot(out_w, grad_out, 0, 1)
     grad_attn = grad_branches[:attn_width].astype(bf16)

time: 409 us -> 409 us (level)
    unnamed x263 -> x265, local copies, waits for them, and re-layouts: 25.5 us -> 23.7 us
where the time goes in v3:
time: 409 us; the launch traced here: 403 us
  waiting for transfers between devices  131 us (32%)
  starting transfers between devices  87.3 us (21%)
  Pallas kernels  77.8 us (19%)
  local copies, waits for them, and re-layouts  34.9 us (9%)
  matrix products  27.2 us (7%)
  other arithmetic  26.8 us (7%)
  between operations  17.7 us (4%)
    ppermute x30, waiting for transfers between devices, shifted(): return lax.ppermute(value, axis, pairs)  69.4 us
    pallas_call x15, Pallas kernels, call(): pl.pallas_call(body, out_shape=[jax.ShapeDtypeStruct(s, d) for s, d in ou...  64.5 us
    ppermute x30, starting transfers between devices, shifted(): return lax.ppermute(value, axis, pairs)  39 us
    ppermute x4, waiting for transfers between devices, gathered_line(): other = lax.ppermute(value, zdim[0], [(i, i ^ step) for i in range(size)])  37.1 us
    ppermute x14, starting transfers between devices, passed_along(): return lax.ppermute(value, axis, pairs)  31.5 us
    dot_general x9, matrix products, dot(): lax.dot_general(left, right, (((left_dim,), (right_dim,)), ((), ())), pre...  27.2 us
    unnamed x265, local copies, waits for them, and re-layouts  23.7 us
    ppermute x4, starting transfers between devices, gathered_line(): other = lax.ppermute(value, zdim[0], [(i, i ^ step) for i in range(size)])  10.6 us
  transfers between devices with their start and end apart: 60, of which 31 were waited for; matrix products, arithmetic and copies ran while one was open for 9% of the time, Pallas kernels for 18%

profile of v3, /device:TPU:0, one launch (start us, length us, event | category | flops | bytes accessed | tf_op | source)
XLA Modules:
  0.0 402.9 jit_solution(17936235478067807862)
XLA Ops:
  14.0 5.1 %collective-permute-start = (bf16[64,768]{1,0:T(8,128)(2,1)S(1)}, bf16[64,768]{1,0:T(8,128)(2,1)S(1)}, u32[]{:S(2)}, u32[]{:S(2)}) collective-permute-start(bf16[64,768]{1,0:T(8,128)(2,1)S(1)} %shard_map.322), channel_id=1, source_target_pairs={{0,6},{2,0},{4,2},{6,4},{1,7},{3,1},{5,3},{7,5},{8,14},{10,8},{12,... | collective-permute-start | bytes 294920 | tf_op jit(solution)/shard_map/ppermute | solution.py:63
  20.8 4.4 %collective-permute-start.5 = (bf16[16,1024]{1,0:T(8,128)(2,1)S(1)}, bf16[16,1024]{1,0:T(8,128)(2,1)S(1)}, u32[]{:S(2)}, u32[]{:S(2)}) collective-permute-start(bf16[16,1024]{1,0:T(8,128)(2,1)S(1)} %slice_bitcast_fusion.4), channel_id=1, source_target_pairs={{0,2},{2,4},{4,6},{1,3},{3,5},{5,7},{8,10},{10,12},{12,14},{9,11},... | collective-permute-start | bytes 98312 | tf_op jit(solution)/shard_map/ppermute | solution.py:69
  37.8 6.1 %collective-permute-done.3 = bf16[1,64,1536]{2,1,0:T(8,128)(2,1)S(1)} collective-permute-done((bf16[1,64,1536]{2,1,0:T(8,128)(2,1)S(1)}, bf16[1,64,1536]{2,1,0:T(8,128)(2,1)S(1)}, u32[]{:S(2)}, u32[]{:S(2)}) %collective-permute-start.3) | collective-permute-done | bytes 196640 | tf_op jit(solution)/shard_map/ppermute | solution.py:102
  44.0 2.5 collective-permute-start.4
  50.5 12.4 %collective-permute-done.4 = bf16[2,64,1536]{2,1,0:T(8,128)(2,1)S(1)} collective-permute-done((bf16[2,64,1536]{2,1,0:T(8,128)(2,1)S(1)}, bf16[2,64,1536]{2,1,0:T(8,128)(2,1)S(1)}, u32[]{:S(2)}, u32[]{:S(2)}) %collective-permute-start.4) | collective-permute-done | bytes 393248 | tf_op jit(solution)/shard_map/ppermute | solution.py:102
  67.3 4.4 %collective-permute-start.13 = (bf16[128,512]{1,0:T(8,128)(2,1)S(1)}, bf16[128,512]{1,0:T(8,128)(2,1)S(1)}, u32[]{:S(2)}, u32[]{:S(2)}) collective-permute-start(bf16[128,512]{1,0:T(8,128)(2,1)S(1)} %get-tuple-element.154.refs_0_), channel_id=1, source_target_pairs={{0,4},{2,6},{1,5},{3,7},{8,12},{10,14},{9,13},{11,15},{16,20},{18,... | collective-permute-start | bytes 393224 | tf_op jit(solution)/shard_map/ppermute | solution.py:69
  73.2 4.9 %collective-permute-done.10 = bf16[4,64,768]{2,1,0:T(8,128)(2,1)S(1)} collective-permute-done((bf16[4,64,768]{2,1,0:T(8,128)(2,1)S(1)}, bf16[4,64,768]{2,1,0:T(8,128)(2,1)S(1)}, u32[]{:S(2)}, u32[]{:S(2)}) %collective-permute-start.10) | collective-permute-done | bytes 393248 | tf_op jit(solution)/shard_map/ppermute | solution.py:63
  78.2 5.8 %collective-permute-done.11 = bf16[4,64,768]{2,1,0:T(8,128)(2,1)S(1)} collective-permute-done((bf16[4,64,768]{2,1,0:T(8,128)(2,1)S(1)}, bf16[4,64,768]{2,1,0:T(8,128)(2,1)S(1)}, u32[]{:S(2)}, u32[]{:S(2)}) %collective-permute-start.11) | collective-permute-done | bytes 393248 | tf_op jit(solution)/shard_map/ppermute | solution.py:63
  84.2 4.0 collective-permute-start.17
  94.1 3.4 collective-permute-start.18
  97.5 8.6 %shard_map.326 = (bf16[256,512]{1,0:T(8,128)(2,1)S(1)}, f32[4,8,512]{2,1,0:T(8,128)S(1)}) custom-call(bf16[256,512]{1,0:T(8,128)(2,1)S(1)} %get-tuple-element.153.q_ref, s32[8,512]{1,0:T(8,128)S(1)} %broadcast_in_dim.58.low_ref, bf16[128,512]{1,0:T(8,128)(2,1)S(1)} %get-tuple-element.154.refs_0_, bf16[128,512]{1,0:T(8,128)(2,1)S(1)} %collective-permute-done.12.refs_1_, ...), custom_call_target="tpu_custom_call" | custom-call | flops 4499999744 | bytes 1000 | tf_op jit(solution)/shard_map/pallas_call | solution.py:202
  106.2 16.8 %collective-permute-done.18 = bf16[2,64,1024]{2,1,0:T(8,128)(2,1)S(1)} collective-permute-done((bf16[2,64,1024]{2,1,0:T(8,128)(2,1)S(1)}, bf16[2,64,1024]{2,1,0:T(8,128)(2,1)S(1)}, u32[]{:S(2)}, u32[]{:S(2)}) %collective-permute-start.18) | collective-permute-done | bytes 262176 | tf_op jit(solution)/shard_map/ppermute | solution.py:102
  123.8 2.7 fusion.57
  128.9 6.7 %shard_map.327 = (f32[768,512]{1,0:T(8,128)S(1)}, f32[512,128]{1,0:T(8,128)S(1)}, f32[512,128]{1,0:T(8,128)S(1)}, f32[128,512]{1,0:T(8,128)S(1)}, f32[128,512]{1...) custom-call(f32[768,640]{1,0:T(8,128)S(1)} %slice.223.u_ref, ...), custom_call_target="tpu_custom_call" | custom-call | flops 3500000000 | bytes 1000 | tf_op jit(solution)/shard_map/pallas_call | solution.py:202
  137.9 3.9 collective-permute-start.21
  141.8 5.3 %collective-permute-start.22 = (bf16[800,128]{1,0:T(8,128)(2,1)S(1)}, bf16[800,128]{1,0:T(8,128)(2,1)S(1)}, u32[]{:S(2)}, u32[]{:S(2)}) collective-permute-start(bf16[800,128]{1,0:T(8,128)(2,1)S(1)} %get-tuple-element.173), channel_id=1, source_target_pairs={{0,4},{2,6},{1,5},{3,7},{8,12},{10,14},{9,13},{11,15},{16,20},{18,... | collective-permute-start | bytes 614408 | tf_op jit(solution)/shard_map/ppermute | solution.py:69
  148.8 3.8 collective-permute-done.22.refs_1_
  152.7 3.6 collective-permute-done.23.refs_2_
  156.4 2.3 shard_map.328
  159.1 2.2 collective-permute-start.26
  163.0 10.9 %collective-permute-done.26 = bf16[2,4,64,512]{3,2,1,0:T(8,128)(2,1)S(1)} collective-permute-done((bf16[2,4,64,512]{3,2,1,0:T(8,128)(2,1)S(1)}, bf16[2,4,64,512]{3,2,1,0:T(8,128)(2,1)S(1)}, u32[]{:S(2)}, u32[]{:S(2)}) %collective-permute-start.26) | collective-permute-done | bytes 524320 | tf_op jit(solution)/shard_map/ppermute | solution.py:63
  180.7 6.2 %fusion.53 = (bf16[512,2048]{1,0:T(8,128)(2,1)}, f32[512,2048]{1,0:T(8,128)S(1)}) fusion(bf16[512,1024]{1,0:T(8,128)(2,1)S(1)} %multiply_convert_fusion.1.n2_ref, bf16[1024,3072]{1,0:T(8,128)(2,1)} %all-gather.2.cloned.1.call-done), kind=kOutput, calls=%fused_computation.187 | convolution fusion | flops 2148532224 | bytes 11534336 | tf_op jit(solution)/shard_map/dot_general | solution.py:27
  187.5 4.9 %fusion.54 = (bf16[512,1024]{1,0:T(8,128)(2,1)}, f32[512,1024]{1,0:T(8,128)}) fusion(bf16[512,1024]{1,0:T(8,128)(2,1)S(1)} %fusion.12.m_ref, bf16[1024,3072]{1,0:T(8,128)(2,1)} %all-gather.2.cloned.1.call-done), kind=kOutput, calls=%fused_computation.188 | convolution fusion | flops 1074266112 | bytes 6291456 | tf_op jit(solution)/shard_map/dot_general | solution.py:27
  195.4 3.9 multiply_reduce_fusion
  199.3 2.3 multiply_convert_fusion
  201.6 4.0 %fusion.9 = (bf16[512,1024]{1,0:T(8,128)(2,1)S(1)}, bf16[512,1024]{1,0:T(8,128)(2,1)S(1)}) fusion(bf16[512,2048]{1,0:T(8,128)(2,1)S(1)} %copy-done.121, bf16[512,1024]{1,0:T(8,128)(2,1)S(1)} %get-tuple-element.304.gf_ref.e_ref, bf16[1024,3072]{1,0:T(8,128)(2,1)} %all-gather.2.cloned.1.call-done), kind=kOutput, calls=%fused_computation.13 | convolution fusion | flops 1081606144 | bytes 7340032 | tf_op jit(solution)/shard_map/dot_general | solution.py:27
  205.9 4.0 %fusion.55 = (bf16[512,1024]{1,0:T(8,128)(2,1)}, f32[512,1024]{1,0:T(8,128)}) fusion(bf16[1024,3072]{1,0:T(8,128)(2,1)S(1)} %bitcast.253, bf16[512,1024]{1,0:T(8,128)(2,1)S(1)} %get-tuple-element.301, bf16[512,1024]{1,0:T(8,128)(2,1)S(1)} %get-tuple-element.300), kind=kOutput, calls=%fused_computation.189 | convolution fusion | flops 2152202240 | bytes 9437184 | tf_op jit(solution)/shard_map/dot_general | solution.py:27
  209.9 4.4 %shard_map.335 = bf16[1024,3072]{1,0:T(8,128)(2,1)S(1)} custom-call(bf16[512,1024]{1,0:T(8,128)(2,1)S(1)} %copy-done.20, bf16[512,1024]{1,0:T(8,128)(2,1)S(1)} %get-tuple-element.304.gf_ref.e_ref, bf16[512,2048]{1,0:T(8,128)(2,1)S(1)} %pad_maximum_fusion.2.ggu_ref, bf16[512,1024]{1,0:T(8,128)(2,1)S(1)} %copy-done.18), custom_call_target="tpu_custom_call" | custom-call | flops 2000000000 | bytes 1000 | tf_op jit(solution)/shard_map/pallas_call | solution.py:977
  214.3 2.7 copy-done.2
  222.4 2.6 shard_map.329
  231.2 3.2 shard_map.330
  241.0 13.2 %shard_map.331 = (bf16[256,512]{1,0:T(8,128)(2,1)S(1)}, bf16[128,512]{1,0:T(8,128)(2,1)S(1)}, bf16[128,512]{1,0:T(8,128)(2,1)S(1)}, bf16[128,512]{1,0:T(8,128)(2,1)S(1)}, bf16[128,512]{1,0:T(8,128)(2,1)S(1)}) custom-call(bf16[256,512]{1,0:T(8,128)(2,1)S(1)} %copy-done.61, s32[8,512]{1,0:T(8,128)S(1)} %copy-done.55, bf16[256,512]{1,0:T(8,128)(2,1)S(1)} %copy-done.88, ...), custom_call_target="tpu_custom_call" | custom-call | flops 7000000000 | bytes 1000 | tf_op jit(solution)/shard_map/pallas_call | solution.py:202
  254.3 10.5 %collective-permute-done.34 = bf16[2,4,64,512]{3,2,1,0:T(8,128)(2,1)S(1)} collective-permute-done((bf16[2,4,64,512]{3,2,1,0:T(8,128)(2,1)S(1)}, bf16[2,4,64,512]{3,2,1,0:T(8,128)(2,1)S(1)}, u32[]{:S(2)}, u32[]{:S(2)}) %collective-permute-start.34) | collective-permute-done | bytes 524320 | tf_op jit(solution)/shard_map/ppermute | solution.py:63
  271.9 13.4 %shard_map.332 = (f32[768,512]{1,0:T(8,128)S(1)}, f32[256,512]{1,0:T(8,128)S(1)}, f32[16,512]{1,0:T(8,128)S(1)}, f32[8,128]{1,0:T(8,128)S(1)}) custom-call(f32[768,512]{1,0:T(8,128)S(1)} %get-tuple-element.197.gy_ref, f32[768,512]{1,0:T(8,128)S(1)} %copy-done.78, f32[512,128]{1,0:T(8,128)S(1)} %copy-done.82, f32[512,128]{1,0:T(8,128)S(1)} %copy-done.41, ...), custom_call_target="tpu_custom_call" | custom-call | flops 6499999744 | bytes 1000 | tf_op jit(solution)/shard_map/pallas_call | solution.py:202
  285.3 3.9 shard_map.333
  293.7 8.8 %shard_map.334 = (f32[1024,512]{1,0:T(8,128)S(1)}, f32[8,1024]{1,0:T(8,128)}, f32[768,128]{1,0:T(8,128)S(1)}, f32[256,128]{1,0:T(8,128)S(1)}) custom-call(f32[768,640]{1,0:T(8,128)S(1)} %copy-done.29, f32[768,640]{1,0:T(8,128)S(1)} %copy-done.27, f32[768,512]{1,0:T(8,128)S(1)} %get-tuple-element.212.gxs_ref, f32[256,512]{1,0:T(8,128)S(1)} %get-tuple-element.213.gbc_ref, ...), custom_call_target="tpu_custom_call" | custom-call | flops 4000000000 | bytes 1000 | tf_op jit(solution)/shard_map/pallas_call | solution.py:202
  306.7 4.0 collective-permute-done.40
  313.6 2.3 fusion.21
  328.0 5.0 %shard_map.337 = (bf16[1024,1152]{1,0:T(8,128)(2,1)S(1)}, bf16[1024,512]{1,0:T(8,128)(2,1)S(1)}, f32[1024,128]{1,0:T(8,128)}) custom-call(bf16[1024,640]{1,0:T(8,128)(2,1)S(1)} %copy-done.14, bf16[1024,640]{1,0:T(8,128)(2,1)S(1)} %copy-done.11, f32[8,640]{1,0:T(8,128)S(1)} %copy-done.45, bf16[1152,512]{1,0:T(8,128)(2,1)S(1)} %shard_map.336.g_ref, ...), custom_call_target="tpu_custom_call" | custom-call | flops 2000000000 | bytes 1000 | tf_op jit(solution)/shard_map/pallas_call | solution.py:835
  335.9 9.1 %collective-permute-done.46 = bf16[2,4,64,512]{3,2,1,0:T(8,128)(2,1)S(1)} collective-permute-done((bf16[2,4,64,512]{3,2,1,0:T(8,128)(2,1)S(1)}, bf16[2,4,64,512]{3,2,1,0:T(8,128)(2,1)S(1)}, u32[]{:S(2)}, u32[]{:S(2)}) %collective-permute-start.46) | collective-permute-done | bytes 524320 | tf_op jit(solution)/shard_map/ppermute | solution.py:63
  346.2 5.8 %collective-permute-done.48 = bf16[2,4,64,640]{3,2,1,0:T(8,128)(2,1)S(1)} collective-permute-done((bf16[2,4,64,640]{3,2,1,0:T(8,128)(2,1)S(1)}, bf16[2,4,64,640]{3,2,1,0:T(8,128)(2,1)S(1)}, u32[]{:S(2)}, u32[]{:S(2)}) %collective-permute-start.48) | collective-permute-done | bytes 655392 | tf_op jit(solution)/shard_map/ppermute | solution.py:63
  353.2 2.5 collective-permute-start.50
  355.8 3.9 collective-permute-done.49
  360.1 2.5 shard_map.338
  366.5 8.7 %collective-permute-done.50 = bf16[2,64,2176]{2,1,0:T(8,128)(2,1)S(1)} collective-permute-done((bf16[2,64,2176]{2,1,0:T(8,128)(2,1)S(1)}, bf16[2,64,2176]{2,1,0:T(8,128)(2,1)S(1)}, u32[]{:S(2)}, u32[]{:S(2)}) %collective-permute-start.50) | collective-permute-done | bytes 557088 | tf_op jit(solution)/shard_map/ppermute | solution.py:169
  375.3 2.3 collective-permute-start.54
  378.5 2.9 collective-permute-start.56
  382.3 6.6 %collective-permute-done.53 = bf16[64,1152]{1,0:T(8,128)(2,1)S(1)} collective-permute-done((bf16[64,1152]{1,0:T(8,128)(2,1)S(1)}, bf16[64,1152]{1,0:T(8,128)(2,1)S(1)}, u32[]{:S(2)}, u32[]{:S(2)}) %collective-permute-start.53) | collective-permute-done | bytes 147488 | tf_op jit(solution)/shard_map/ppermute | solution.py:63
  (483 shorter events, 121.8 us)
Async XLA Ops:
  7.2 173.5 %all-gather.2.cloned.1.call-start = ((), (), s32[]{:S(2)}) async-start(), calls=%async_computation.2 | async-start | bytes 6684672 | tf_op jit(solution)/shard_map/all_gather | solution.py:1081
  14.0 12.3 %collective-permute-start = (bf16[64,768]{1,0:T(8,128)(2,1)S(1)}, bf16[64,768]{1,0:T(8,128)(2,1)S(1)}, u32[]{:S(2)}, u32[]{:S(2)}) collective-permute-start(bf16[64,768]{1,0:T(8,128)(2,1)S(1)} %shard_map.322), channel_id=1, source_target_pairs={{0,6},{2,0},{4,2},{6,4},{1,7},{3,1},{5,3},{7,5},{8,14},{10,8},{12,... | collective-permute-start | bytes 294920 | tf_op jit(solution)/shard_map/ppermute | solution.py:63
  19.1 8.7 %collective-permute-start.1 = (bf16[64,768]{1,0:T(8,128)(2,1)S(1)}, bf16[64,768]{1,0:T(8,128)(2,1)S(1)}, u32[]{:S(2)}, u32[]{:S(2)}) collective-permute-start(bf16[64,768]{1,0:T(8,128)(2,1)S(1)} %shard_map.322), channel_id=1, source_target_pairs={{0,4},{2,6},{4,0},{6,2},{1,5},{3,7},{5,1},{7,3},{8,12},{10,14},{12... | collective-permute-start | bytes 294920 | tf_op jit(solution)/shard_map/ppermute | solution.py:63
  19.1 8.8 %collective-permute-start.2 = (bf16[64,768]{1,0:T(8,128)(2,1)S(1)}, bf16[64,768]{1,0:T(8,128)(2,1)S(1)}, u32[]{:S(2)}, u32[]{:S(2)}) collective-permute-start(bf16[64,768]{1,0:T(8,128)(2,1)S(1)} %shard_map.322), channel_id=1, source_target_pairs={{0,2},{2,4},{4,6},{6,0},{1,3},{3,5},{5,7},{7,1},{8,10},{10,12},{12... | collective-permute-start | bytes 294920 | tf_op jit(solution)/shard_map/ppermute | solution.py:63
  20.8 10.9 %collective-permute-start.5 = (bf16[16,1024]{1,0:T(8,128)(2,1)S(1)}, bf16[16,1024]{1,0:T(8,128)(2,1)S(1)}, u32[]{:S(2)}, u32[]{:S(2)}) collective-permute-start(bf16[16,1024]{1,0:T(8,128)(2,1)S(1)} %slice_bitcast_fusion.4), channel_id=1, source_target_pairs={{0,2},{2,4},{4,6},{1,3},{3,5},{5,7},{8,10},{10,12},{12,14},{9,11},... | collective-permute-start | bytes 98312 | tf_op jit(solution)/shard_map/ppermute | solution.py:69
  26.1 285.5 %reduce-scatter.3.cloned.1.call-start = ((), (), s32[]{:S(2)}) async-start(), calls=%async_computation.3 | async-start | bytes 7864320 | tf_op jit(solution)/shard_map/reduce_scatter | solution.py:1153
  32.4 11.5 %collective-permute-start.3 = (bf16[1,64,1536]{2,1,0:T(8,128)(2,1)S(1)}, bf16[1,64,1536]{2,1,0:T(8,128)(2,1)S(1)}, u32[]{:S(2)}, u32[]{:S(2)}) collective-permute-start(bf16[1,64,1536]{2,1,0:T(8,128)(2,1)S(1)} %bitcast.222), channel_id=1, source_target_pairs={{0,2},{2,0},{4,6},{6,4},{1,3},{3,1},{5,7},{7,5},{8,10},{10,8},{12,... | collective-permute-start | bytes 589832 | tf_op jit(solution)/shard_map/ppermute | solution.py:102
  34.6 12.5 %collective-permute-start.9 = (bf16[2,4,64,384]{3,2,1,0:T(8,128)(2,1)S(1)}, bf16[2,4,64,384]{3,2,1,0:T(8,128)(2,1)S(1)}, u32[]{:S(2)}, u32[]{:S(2)}) collective-permute-start(bf16[2,4,64,384]{3,2,1,0:T(8,128)(2,1)S(1)} %maximum_select_fusion.15), channel_id=1, source_target_pairs={{0,16},{8,24},{16,0},{24,8},{1,17},{9,25},{17,1},{25,9},{2,18},{10... | collective-permute-start | bytes 1179656 | tf_op jit(solution)/shard_map/ppermute | solution.py:63
  36.9 10.5 %collective-permute-start.7 = (bf16[2,4,64,384]{3,2,1,0:T(8,128)(2,1)S(1)}, bf16[2,4,64,384]{3,2,1,0:T(8,128)(2,1)S(1)}, u32[]{:S(2)}, u32[]{:S(2)}) collective-permute-start(bf16[2,4,64,384]{3,2,1,0:T(8,128)(2,1)S(1)} %maximum_select_fusion.13), channel_id=1, source_target_pairs={{0,8},{8,0},{16,24},{24,16},{1,9},{9,1},{17,25},{25,17},{2,10},{10... | collective-permute-start | bytes 1179656 | tf_op jit(solution)/shard_map/ppermute | solution.py:63
  44.0 18.9 %collective-permute-start.4 = (bf16[2,64,1536]{2,1,0:T(8,128)(2,1)S(1)}, bf16[2,64,1536]{2,1,0:T(8,128)(2,1)S(1)}, u32[]{:S(2)}, u32[]{:S(2)}) collective-permute-start(bf16[2,64,1536]{2,1,0:T(8,128)(2,1)S(1)} %maximum_select_fusion.12), channel_id=1, source_target_pairs={{0,4},{2,6},{4,0},{6,2},{1,5},{3,7},{5,1},{7,3},{8,12},{10,14},{12... | collective-permute-start | bytes 1179656 | tf_op jit(solution)/shard_map/ppermute | solution.py:102
  63.2 14.9 %collective-permute-start.10 = (bf16[4,64,768]{2,1,0:T(8,128)(2,1)S(1)}, bf16[4,64,768]{2,1,0:T(8,128)(2,1)S(1)}, u32[]{:S(2)}, u32[]{:S(2)}) collective-permute-start(bf16[4,64,768]{2,1,0:T(8,128)(2,1)S(1)} %get-tuple-element.311), channel_id=1, source_target_pairs={{0,16},{8,24},{16,0},{24,8},{1,17},{9,25},{17,1},{25,9},{2,18},{10... | collective-permute-start | bytes 1179656 | tf_op jit(solution)/shard_map/ppermute | solution.py:63
  64.5 19.6 %collective-permute-start.11 = (bf16[4,64,768]{2,1,0:T(8,128)(2,1)S(1)}, bf16[4,64,768]{2,1,0:T(8,128)(2,1)S(1)}, u32[]{:S(2)}, u32[]{:S(2)}) collective-permute-start(bf16[4,64,768]{2,1,0:T(8,128)(2,1)S(1)} %get-tuple-element.310), channel_id=1, source_target_pairs={{0,8},{8,0},{16,24},{24,16},{1,9},{9,1},{17,25},{25,17},{2,10},{10... | collective-permute-start | bytes 1179656 | tf_op jit(solution)/shard_map/ppermute | solution.py:63
  66.0 18.2 %collective-permute-start.12 = (bf16[128,512]{1,0:T(8,128)(2,1)S(1)}, bf16[128,512]{1,0:T(8,128)(2,1)S(1)}, u32[]{:S(2)}, u32[]{:S(2)}) collective-permute-start(bf16[128,512]{1,0:T(8,128)(2,1)S(1)} %get-tuple-element.154.refs_0_), channel_id=1, source_target_pairs={{0,2},{2,4},{4,6},{1,3},{3,5},{5,7},{8,10},{10,12},{12,14},{9,11},... | collective-permute-start | bytes 393224 | tf_op jit(solution)/shard_map/ppermute | solution.py:69
  67.3 16.9 %collective-permute-start.13 = (bf16[128,512]{1,0:T(8,128)(2,1)S(1)}, bf16[128,512]{1,0:T(8,128)(2,1)S(1)}, u32[]{:S(2)}, u32[]{:S(2)}) collective-permute-start(bf16[128,512]{1,0:T(8,128)(2,1)S(1)} %get-tuple-element.154.refs_0_), channel_id=1, source_target_pairs={{0,4},{2,6},{1,5},{3,7},{8,12},{10,14},{9,13},{11,15},{16,20},{18,... | collective-permute-start | bytes 393224 | tf_op jit(solution)/shard_map/ppermute | solution.py:69
  71.7 12.6 %collective-permute-start.14 = (bf16[128,512]{1,0:T(8,128)(2,1)S(1)}, bf16[128,512]{1,0:T(8,128)(2,1)S(1)}, u32[]{:S(2)}, u32[]{:S(2)}) collective-permute-start(bf16[128,512]{1,0:T(8,128)(2,1)S(1)} %get-tuple-element.154.refs_0_), channel_id=1, source_target_pairs={{0,6},{1,7},{8,14},{9,15},{16,22},{17,23},{24,30},{25,31}} | collective-permute-start | bytes 393224 | tf_op jit(solution)/shard_map/ppermute | solution.py:69
  84.2 9.8 %collective-permute-start.17 = (bf16[1,64,1024]{2,1,0:T(8,128)(2,1)S(1)}, bf16[1,64,1024]{2,1,0:T(8,128)(2,1)S(1)}, u32[]{:S(2)}, u32[]{:S(2)}) collective-permute-start(bf16[1,64,1024]{2,1,0:T(8,128)(2,1)S(1)} %bitcast.231), channel_id=1, source_target_pairs={{0,2},{2,0},{4,6},{6,4},{1,3},{3,1},{5,7},{7,5},{8,10},{10,8},{12,... | collective-permute-start | bytes 393224 | tf_op jit(solution)/shard_map/ppermute | solution.py:102
  88.2 34.8 %collective-permute-start.16 = (bf16[2,4,64,768]{3,2,1,0:T(8,128)(2,1)S(1)}, bf16[2,4,64,768]{3,2,1,0:T(8,128)(2,1)S(1)}, u32[]{:S(2)}, u32[]{:S(2)}) collective-permute-start(bf16[2,4,64,768]{3,2,1,0:T(8,128)(2,1)S(1)} %maximum_select_fusion.8), channel_id=1, source_target_pairs={{0,16},{8,24},{16,0},{24,8},{1,17},{9,25},{17,1},{25,9},{2,18},{10... | collective-permute-start | bytes 2359304 | tf_op jit(solution)/shard_map/ppermute | solution.py:63
  90.3 33.0 %collective-permute-start.15 = (bf16[2,4,64,768]{3,2,1,0:T(8,128)(2,1)S(1)}, bf16[2,4,64,768]{3,2,1,0:T(8,128)(2,1)S(1)}, u32[]{:S(2)}, u32[]{:S(2)}) collective-permute-start(bf16[2,4,64,768]{3,2,1,0:T(8,128)(2,1)S(1)} %maximum_select_fusion.7), channel_id=1, source_target_pairs={{0,8},{8,0},{16,24},{24,16},{1,9},{9,1},{17,25},{25,17},{2,10},{10... | collective-permute-start | bytes 2359304 | tf_op jit(solution)/shard_map/ppermute | solution.py:63
  94.1 28.8 %collective-permute-start.18 = (bf16[2,64,1024]{2,1,0:T(8,128)(2,1)S(1)}, bf16[2,64,1024]{2,1,0:T(8,128)(2,1)S(1)}, u32[]{:S(2)}, u32[]{:S(2)}) collective-permute-start(bf16[2,64,1024]{2,1,0:T(8,128)(2,1)S(1)} %maximum_select_fusion.16), channel_id=1, source_target_pairs={{0,4},{2,6},{4,0},{6,2},{1,5},{3,7},{5,1},{7,3},{8,12},{10,14},{12... | collective-permute-start | bytes 786440 | tf_op jit(solution)/shard_map/ppermute | solution.py:102
  126.7 22.0 %collective-permute-start.19 = (bf16[4,64,512]{2,1,0:T(8,128)(2,1)S(1)}, bf16[4,64,512]{2,1,0:T(8,128)(2,1)S(1)}, u32[]{:S(2)}, u32[]{:S(2)}) collective-permute-start(bf16[4,64,512]{2,1,0:T(8,128)(2,1)S(1)} %get-tuple-element.326), channel_id=1, source_target_pairs={{0,16},{8,24},{16,0},{24,8},{1,17},{9,25},{17,1},{25,9},{2,18},{10... | collective-permute-start | bytes 786440 | tf_op jit(solution)/shard_map/ppermute | solution.py:63
  127.2 21.5 %collective-permute-start.20 = (bf16[4,64,512]{2,1,0:T(8,128)(2,1)S(1)}, bf16[4,64,512]{2,1,0:T(8,128)(2,1)S(1)}, u32[]{:S(2)}, u32[]{:S(2)}) collective-permute-start(bf16[4,64,512]{2,1,0:T(8,128)(2,1)S(1)} %get-tuple-element.325), channel_id=1, source_target_pairs={{0,8},{8,0},{16,24},{24,16},{1,9},{9,1},{17,25},{25,17},{2,10},{10... | collective-permute-start | bytes 786440 | tf_op jit(solution)/shard_map/ppermute | solution.py:63
  137.9 11.0 %collective-permute-start.21 = (bf16[800,128]{1,0:T(8,128)(2,1)S(1)}, bf16[800,128]{1,0:T(8,128)(2,1)S(1)}, u32[]{:S(2)}, u32[]{:S(2)}) collective-permute-start(bf16[800,128]{1,0:T(8,128)(2,1)S(1)} %get-tuple-element.173), channel_id=1, source_target_pairs={{0,2},{2,4},{4,6},{1,3},{3,5},{5,7},{8,10},{10,12},{12,14},{9,11},... | collective-permute-start | bytes 614408 | tf_op jit(solution)/shard_map/ppermute | solution.py:69
  141.8 10.9 %collective-permute-start.22 = (bf16[800,128]{1,0:T(8,128)(2,1)S(1)}, bf16[800,128]{1,0:T(8,128)(2,1)S(1)}, u32[]{:S(2)}, u32[]{:S(2)}) collective-permute-start(bf16[800,128]{1,0:T(8,128)(2,1)S(1)} %get-tuple-element.173), channel_id=1, source_target_pairs={{0,4},{2,6},{1,5},{3,7},{8,12},{10,14},{9,13},{11,15},{16,20},{18,... | collective-permute-start | bytes 614408 | tf_op jit(solution)/shard_map/ppermute | solution.py:69
  147.1 9.2 %collective-permute-start.23 = (bf16[800,128]{1,0:T(8,128)(2,1)S(1)}, bf16[800,128]{1,0:T(8,128)(2,1)S(1)}, u32[]{:S(2)}, u32[]{:S(2)}) collective-permute-start(bf16[800,128]{1,0:T(8,128)(2,1)S(1)} %get-tuple-element.173), channel_id=1, source_target_pairs={{0,6},{1,7},{8,14},{9,15},{16,22},{17,23},{24,30},{25,31}} | collective-permute-start | bytes 614408 | tf_op jit(solution)/shard_map/ppermute | solution.py:69
  159.1 14.8 %collective-permute-start.26 = (bf16[2,4,64,512]{3,2,1,0:T(8,128)(2,1)S(1)}, bf16[2,4,64,512]{3,2,1,0:T(8,128)(2,1)S(1)}, u32[]{:S(2)}, u32[]{:S(2)}) collective-permute-start(bf16[2,4,64,512]{3,2,1,0:T(8,128)(2,1)S(1)} %maximum_select_fusion.11), channel_id=1, source_target_pairs={{0,16},{8,24},{16,0},{24,8},{1,17},{9,25},{17,1},{25,9},{2,18},{10... | collective-permute-start | bytes 1572872 | tf_op jit(solution)/shard_map/ppermute | solution.py:63
  161.3 14.0 %collective-permute-start.25 = (bf16[2,4,64,512]{3,2,1,0:T(8,128)(2,1)S(1)}, bf16[2,4,64,512]{3,2,1,0:T(8,128)(2,1)S(1)}, u32[]{:S(2)}, u32[]{:S(2)}) collective-permute-start(bf16[2,4,64,512]{3,2,1,0:T(8,128)(2,1)S(1)} %maximum_select_fusion.10), channel_id=1, source_target_pairs={{0,8},{8,0},{16,24},{24,16},{1,9},{9,1},{17,25},{25,17},{2,10},{10... | collective-permute-start | bytes 1572872 | tf_op jit(solution)/shard_map/ppermute | solution.py:63
  217.0 145.6 %reduce-scatter.5.cloned.1.call-start = ((), (), s32[]{:S(2)}) async-start(), calls=%async_computation.4 | async-start | bytes 1966080 | tf_op jit(solution)/shard_map/reduce_scatter | solution.py:1183
  234.4 31.6 %collective-permute-start.31 = (bf16[800,128]{1,0:T(8,128)(2,1)S(1)}, bf16[800,128]{1,0:T(8,128)(2,1)S(1)}, u32[]{:S(2)}, u32[]{:S(2)}) collective-permute-start(bf16[800,128]{1,0:T(8,128)(2,1)S(1)} %get-tuple-element.185), channel_id=1, source_target_pairs={{2,0},{4,2},{6,4},{3,1},{5,3},{7,5},{10,8},{12,10},{14,12},{11,9},... | collective-permute-start | bytes 614408 | tf_op jit(solution)/shard_map/ppermute | solution.py:69
  235.7 30.3 %collective-permute-start.32 = (bf16[800,128]{1,0:T(8,128)(2,1)S(1)}, bf16[800,128]{1,0:T(8,128)(2,1)S(1)}, u32[]{:S(2)}, u32[]{:S(2)}) collective-permute-start(bf16[800,128]{1,0:T(8,128)(2,1)S(1)} %get-tuple-element.185), channel_id=1, source_target_pairs={{4,0},{6,2},{5,1},{7,3},{12,8},{14,10},{13,9},{15,11},{20,16},{22,... | collective-permute-start | bytes 614408 | tf_op jit(solution)/shard_map/ppermute | solution.py:69
  237.0 29.0 %collective-permute-start.33 = (bf16[800,128]{1,0:T(8,128)(2,1)S(1)}, bf16[800,128]{1,0:T(8,128)(2,1)S(1)}, u32[]{:S(2)}, u32[]{:S(2)}) collective-permute-start(bf16[800,128]{1,0:T(8,128)(2,1)S(1)} %get-tuple-element.185), channel_id=1, source_target_pairs={{6,0},{7,1},{14,8},{15,9},{22,16},{23,17},{30,24},{31,25}} | collective-permute-start | bytes 614408 | tf_op jit(solution)/shard_map/ppermute | solution.py:69
  238.9 25.9 %collective-permute-start.34 = (bf16[2,4,64,512]{3,2,1,0:T(8,128)(2,1)S(1)}, bf16[2,4,64,512]{3,2,1,0:T(8,128)(2,1)S(1)}, u32[]{:S(2)}, u32[]{:S(2)}) collective-permute-start(bf16[2,4,64,512]{3,2,1,0:T(8,128)(2,1)S(1)} %dynamic-slice_bitcast_fusion.5), channel_id=1, source_target_pairs={{0,8},{8,0},{16,24},{24,16},{1,9},{9,1},{17,25},{25,17},{2,10},{10... | collective-permute-start | bytes 1572872 | tf_op jit(solution)/shard_map/ppermute | solution.py:63
  240.1 25.8 %collective-permute-start.35 = (bf16[2,4,64,512]{3,2,1,0:T(8,128)(2,1)S(1)}, bf16[2,4,64,512]{3,2,1,0:T(8,128)(2,1)S(1)}, u32[]{:S(2)}, u32[]{:S(2)}) collective-permute-start(bf16[2,4,64,512]{3,2,1,0:T(8,128)(2,1)S(1)} %dynamic-slice_bitcast_fusion.4), channel_id=1, source_target_pairs={{0,16},{8,24},{16,0},{24,8},{1,17},{9,25},{17,1},{25,9},{2,18},{10... | collective-permute-start | bytes 1572872 | tf_op jit(solution)/shard_map/ppermute | solution.py:63
  266.0 19.2 %collective-permute-start.36 = (bf16[128,512]{1,0:T(8,128)(2,1)S(1)}, bf16[128,512]{1,0:T(8,128)(2,1)S(1)}, u32[]{:S(2)}, u32[]{:S(2)}) collective-permute-start(bf16[128,512]{1,0:T(8,128)(2,1)S(1)} %get-tuple-element.194), channel_id=1, source_target_pairs={{2,0},{4,2},{6,4},{3,1},{5,3},{7,5},{10,8},{12,10},{14,12},{11,9},... | collective-permute-start | bytes 393224 | tf_op jit(solution)/shard_map/ppermute | solution.py:69
  267.3 17.9 %collective-permute-start.37 = (bf16[128,512]{1,0:T(8,128)(2,1)S(1)}, bf16[128,512]{1,0:T(8,128)(2,1)S(1)}, u32[]{:S(2)}, u32[]{:S(2)}) collective-permute-start(bf16[128,512]{1,0:T(8,128)(2,1)S(1)} %get-tuple-element.195), channel_id=1, source_target_pairs={{4,0},{6,2},{5,1},{7,3},{12,8},{14,10},{13,9},{15,11},{20,16},{22,... | collective-permute-start | bytes 393224 | tf_op jit(solution)/shard_map/ppermute | solution.py:69
  268.6 16.7 %collective-permute-start.38 = (bf16[128,512]{1,0:T(8,128)(2,1)S(1)}, bf16[128,512]{1,0:T(8,128)(2,1)S(1)}, u32[]{:S(2)}, u32[]{:S(2)}) collective-permute-start(bf16[128,512]{1,0:T(8,128)(2,1)S(1)} %get-tuple-element.196), channel_id=1, source_target_pairs={{6,0},{7,1},{14,8},{15,9},{22,16},{23,17},{30,24},{31,25}} | collective-permute-start | bytes 393224 | tf_op jit(solution)/shard_map/ppermute | solution.py:69
  270.0 35.2 %collective-permute-start.42 = (bf16[4,64,512]{2,1,0:T(8,128)(2,1)S(1)}, bf16[4,64,512]{2,1,0:T(8,128)(2,1)S(1)}, u32[]{:S(2)}, u32[]{:S(2)}) collective-permute-start(bf16[4,64,512]{2,1,0:T(8,128)(2,1)S(1)} %dynamic-slice_bitcast_fusion.10), channel_id=1, source_target_pairs={{0,16},{8,24},{16,0},{24,8},{1,17},{9,25},{17,1},{25,9},{2,18},{10... | collective-permute-start | bytes 786440 | tf_op jit(solution)/shard_map/ppermute | solution.py:63
  270.8 35.2 %collective-permute-start.43 = (bf16[4,64,512]{2,1,0:T(8,128)(2,1)S(1)}, bf16[4,64,512]{2,1,0:T(8,128)(2,1)S(1)}, u32[]{:S(2)}, u32[]{:S(2)}) collective-permute-start(bf16[4,64,512]{2,1,0:T(8,128)(2,1)S(1)} %dynamic-slice_bitcast_fusion.9), channel_id=1, source_target_pairs={{0,8},{8,0},{16,24},{24,16},{1,9},{9,1},{17,25},{25,17},{2,10},{10... | collective-permute-start | bytes 786440 | tf_op jit(solution)/shard_map/ppermute | solution.py:63
  290.3 20.4 %collective-permute-start.40 = (bf16[2,4,64,512]{3,2,1,0:T(8,128)(2,1)S(1)}, bf16[2,4,64,512]{3,2,1,0:T(8,128)(2,1)S(1)}, u32[]{:S(2)}, u32[]{:S(2)}) collective-permute-start(bf16[2,4,64,512]{3,2,1,0:T(8,128)(2,1)S(1)} %dynamic-slice_bitcast_fusion.3), channel_id=1, source_target_pairs={{0,8},{8,0},{16,24},{24,16},{1,9},{9,1},{17,25},{25,17},{2,10},{10... | collective-permute-start | bytes 1572872 | tf_op jit(solution)/shard_map/ppermute | solution.py:63
  292.4 21.2 %collective-permute-start.41 = (bf16[2,4,64,640]{3,2,1,0:T(8,128)(2,1)}, bf16[2,4,64,640]{3,2,1,0:T(8,128)(2,1)}, u32[]{:S(2)}, u32[]{:S(2)}) collective-permute-start(bf16[2,4,64,640]{3,2,1,0:T(8,128)(2,1)} %dynamic-slice_bitcast_fusion.1), channel_id=1, source_target_pairs={{0,16},{8,24},{16,0},{24,8},{1,17},{9,25},{17,1},{25,9},{2,18},{10... | collective-permute-start | bytes 1966088 | tf_op jit(solution)/shard_map/ppermute | solution.py:63
  318.9 14.2 %collective-permute-start.44 = (bf16[4,64,512]{2,1,0:T(8,128)(2,1)S(1)}, bf16[4,64,512]{2,1,0:T(8,128)(2,1)S(1)}, u32[]{:S(2)}, u32[]{:S(2)}) collective-permute-start(bf16[4,64,512]{2,1,0:T(8,128)(2,1)S(1)} %dynamic-slice_bitcast_fusion.8), channel_id=1, source_target_pairs={{0,16},{8,24},{16,0},{24,8},{1,17},{9,25},{17,1},{25,9},{2,18},{10... | collective-permute-start | bytes 786440 | tf_op jit(solution)/shard_map/ppermute | solution.py:63
  321.4 11.7 %collective-permute-start.45 = (bf16[4,64,640]{2,1,0:T(8,128)(2,1)S(1)}, bf16[4,64,640]{2,1,0:T(8,128)(2,1)S(1)}, u32[]{:S(2)}, u32[]{:S(2)}) collective-permute-start(bf16[4,64,640]{2,1,0:T(8,128)(2,1)S(1)} %dynamic-slice_bitcast_fusion.6), channel_id=1, source_target_pairs={{0,8},{8,0},{16,24},{24,16},{1,9},{9,1},{17,25},{25,17},{2,10},{10... | collective-permute-start | bytes 983048 | tf_op jit(solution)/shard_map/ppermute | solution.py:63
  333.6 11.4 %collective-permute-start.46 = (bf16[2,4,64,512]{3,2,1,0:T(8,128)(2,1)S(1)}, bf16[2,4,64,512]{3,2,1,0:T(8,128)(2,1)S(1)}, u32[]{:S(2)}, u32[]{:S(2)}) collective-permute-start(bf16[2,4,64,512]{3,2,1,0:T(8,128)(2,1)S(1)} %dynamic-slice_bitcast_fusion.2), channel_id=1, source_target_pairs={{0,8},{8,0},{16,24},{24,16},{1,9},{9,1},{17,25},{25,17},{2,10},{10... | collective-permute-start | bytes 1572872 | tf_op jit(solution)/shard_map/ppermute | solution.py:63
  335.0 17.0 %collective-permute-start.48 = (bf16[2,4,64,640]{3,2,1,0:T(8,128)(2,1)S(1)}, bf16[2,4,64,640]{3,2,1,0:T(8,128)(2,1)S(1)}, u32[]{:S(2)}, u32[]{:S(2)}) collective-permute-start(bf16[2,4,64,640]{3,2,1,0:T(8,128)(2,1)S(1)} %dynamic-slice_bitcast_fusion), channel_id=1, source_target_pairs={{0,16},{8,24},{16,0},{24,8},{1,17},{9,25},{17,1},{25,9},{2,18},{10... | collective-permute-start | bytes 1966088 | tf_op jit(solution)/shard_map/ppermute | solution.py:63
  345.2 10.4 %collective-permute-start.47 = (bf16[4,64,512]{2,1,0:T(8,128)(2,1)S(1)}, bf16[4,64,512]{2,1,0:T(8,128)(2,1)S(1)}, u32[]{:S(2)}, u32[]{:S(2)}) collective-permute-start(bf16[4,64,512]{2,1,0:T(8,128)(2,1)S(1)} %dynamic-slice_bitcast_fusion.7), channel_id=1, source_target_pairs={{0,16},{8,24},{16,0},{24,8},{1,17},{9,25},{17,1},{25,9},{2,18},{10... | collective-permute-start | bytes 786440 | tf_op jit(solution)/shard_map/ppermute | solution.py:63
  353.2 22.0 %collective-permute-start.50 = (bf16[2,64,2176]{2,1,0:T(8,128)(2,1)S(1)}, bf16[2,64,2176]{2,1,0:T(8,128)(2,1)S(1)}, u32[]{:S(2)}, u32[]{:S(2)}) collective-permute-start(bf16[2,64,2176]{2,1,0:T(8,128)(2,1)S(1)} %broadcast_select_fusion), channel_id=1, source_target_pairs={{0,4},{2,6},{4,0},{6,2},{1,5},{3,7},{5,1},{7,3},{8,12},{10,14},{12... | collective-permute-start | bytes 1671176 | tf_op jit(solution)/shard_map/ppermute | solution.py:169
  377.6 11.3 %collective-permute-start.53 = (bf16[64,1152]{1,0:T(8,128)(2,1)S(1)}, bf16[64,1152]{1,0:T(8,128)(2,1)S(1)}, u32[]{:S(2)}, u32[]{:S(2)}) collective-permute-start(bf16[64,1152]{1,0:T(8,128)(2,1)S(1)} %get-tuple-element.316), channel_id=1, source_target_pairs={{0,4},{2,6},{4,0},{6,2},{1,5},{3,7},{5,1},{7,3},{8,12},{10,14},{12... | collective-permute-start | bytes 442376 | tf_op jit(solution)/shard_map/ppermute | solution.py:63
  377.6 11.3 %collective-permute-start.52 = (bf16[64,1152]{1,0:T(8,128)(2,1)S(1)}, bf16[64,1152]{1,0:T(8,128)(2,1)S(1)}, u32[]{:S(2)}, u32[]{:S(2)}) collective-permute-start(bf16[64,1152]{1,0:T(8,128)(2,1)S(1)} %get-tuple-element.314), channel_id=1, source_target_pairs={{0,2},{2,4},{4,6},{6,0},{1,3},{3,5},{5,7},{7,1},{8,10},{10,12},{12... | collective-permute-start | bytes 442376 | tf_op jit(solution)/shard_map/ppermute | solution.py:63
  378.5 14.3 %collective-permute-start.56 = (bf16[1,64,2176]{2,1,0:T(8,128)(2,1)S(1)}, bf16[1,64,2176]{2,1,0:T(8,128)(2,1)S(1)}, u32[]{:S(2)}, u32[]{:S(2)}) collective-permute-start(bf16[1,64,2176]{2,1,0:T(8,128)(2,1)S(1)} %broadcast_select_fusion.1), channel_id=1, source_target_pairs={{0,2},{2,0},{4,6},{6,4},{1,3},{3,1},{5,7},{7,5},{8,10},{10,8},{12,... | collective-permute-start | bytes 835592 | tf_op jit(solution)/shard_map/ppermute | solution.py:169
  (136 other events, 1549.5 us)
Sparse Core Ops, SparseCore 0:
  26.2 122.9 all-gather.1
  217.1 91.2 reduce-scatter.2
  316.0 36.3 reduce-scatter.4
